TPU v7x, 256 devices: a whole 4x4x8 slice. The times are simulated.
256 devices in a mesh: dp: 64 (over y, x, z_hi), tensor: 4 (over z_lo, core).
Axes of the slice: x: 4, y: 4, z: 8 (z_hi: 4, z_lo: 2; z = z_hi * 2 + z_lo), core: 2. Of those that a mesh axis runs over, the one named last changes fastest.
Arguments:
- inputs: bfloat16 [7168, 128], P('dp'), may hold values from -6 to 6
- ln_gain: float32 [7168], P('dp'), may hold values from 0.5 to 1.5
- segment_ids: int32 [128], replicated, may hold values from 0 to 7, never falling along the last dimension, each value on 1 to 32 neighbouring positions
- w_in: bfloat16 [7168, 14336], P('dp', 'tensor'), may hold values from -0.0625 to 0.0625
- w_out: bfloat16 [7168, 14336], P('dp', 'tensor'), may hold values from -0.046875 to 0.046875
- mom_in: bfloat16 [7168, 14336], P('dp', 'tensor'), may hold values from -0.119628906 to 0.119628906
- mom_out: bfloat16 [7168, 14336], P('dp', 'tensor'), may hold values from -0.119628906 to 0.119628906
- hess_in: bfloat16 [7168, 14336], P('dp', 'tensor'), may hold values from 0.0099487305 to 1
- hess_out: bfloat16 [7168, 14336], P('dp', 'tensor'), may hold values from 0.0099487305 to 1
- probe_seed: int32 [2], replicated, may hold values from 0 to 1073741823
Outputs:
- new_mom_in: bfloat16 [7168, 14336], P('dp', 'tensor')
- new_hess_in: bfloat16 [7168, 14336], P('dp', 'tensor')
- step_in: bfloat16 [7168, 14336], P('dp', 'tensor')
- new_mom_out: bfloat16 [7168, 14336], P('dp', 'tensor')
- new_hess_out: bfloat16 [7168, 14336], P('dp', 'tensor')
- step_out: bfloat16 [7168, 14336], P('dp', 'tensor')
Inputs may be any that keep to these rules, and one draw needn't show every extreme that they name: `segment_ids`: document numbers never fall along the tokens; each document has at most 32 tokens, and one has exactly that many.
All inputs are finite; a program needn't handle non-finite values.
Results may differ from a plain program's by a relative error of at most 0.039.
Values may be sent and summed in bfloat16 or wider, within the bound.
No kernel may reach another device: no remote copies, remote signals or barrier semaphores. Data moves between devices by JAX's collectives and lax.ppermute only.
A program may use at most 64 MiB of HBM per device.

v0:
```python
import jax
import jax.numpy as jnp
from jax import lax
from jax.sharding import PartitionSpec as P

D = 7168
FF = 14336


BETA_ONE = 0.96
BETA_TWO = 0.99
SCALE_GAMMA = 0.05
FLOOR_EPS = 0.002
NORM_EPS = 1e-05
hash_factor = 73244475
contract_rows = (((0,), (0,)), ((), ()))
contract_cols = (((1,), (1,)), ((), ()))


def mixing(words):
    words = (words ^ words >> 16 & 65535) * hash_factor
    words = (words ^ words >> 16 & 65535) * hash_factor
    return words ^ words >> 16 & 65535


def probe_signs(seed_word, row_start, col_start, row_count, col_count, total_cols):
    rows_index = row_start + jnp.arange(row_count, dtype=jnp.int32)[:, None]
    cols_index = col_start + jnp.arange(col_count, dtype=jnp.int32)[None, :]
    hashed = mixing(rows_index * total_cols + cols_index ^ seed_word)
    return (1 - 2 * (hashed & 1)).astype(jnp.bfloat16)


def gelu_parts(preact):
    normal_cdf = 0.5 * (1.0 + lax.erf(preact * 0.7071067811865476))
    normal_pdf = jnp.exp(-0.5 * preact * preact) * 0.3989422804014327
    return (
        preact * normal_cdf,
        normal_cdf + preact * normal_pdf,
        normal_pdf * (2.0 - preact * preact),
    )


def token_weights(segment_ids):
    following = jnp.concatenate([segment_ids[1:], jnp.full((1,), -1, jnp.int32)])
    valid = (following == segment_ids).astype(jnp.float32)
    same_doc = (segment_ids[:, None] == segment_ids[None, :]).astype(jnp.float32)
    counts = jnp.dot(same_doc, valid, precision=lax.Precision.HIGHEST)
    return valid / jnp.maximum(counts, 1.0)


def sophia_update(moment_old, curve_old, gradient, product, probe):
    moment = BETA_ONE * moment_old.astype(jnp.float32) + (1.0 - BETA_ONE) * gradient
    curvature = (
        BETA_TWO * curve_old.astype(jnp.float32)
        + (1.0 - BETA_TWO) * probe.astype(jnp.float32) * product
    )
    stepped = jnp.clip(moment / jnp.maximum(SCALE_GAMMA * curvature, FLOOR_EPS), -1.0, 1.0)
    return (
        moment.astype(jnp.bfloat16),
        curvature.astype(jnp.bfloat16),
        stepped.astype(jnp.bfloat16),
    )


def body(inputs, ln_gain, segment_ids, w_in, w_out, mom_in, mom_out, hess_in, hess_out, probe_seed):
    features, length = inputs.shape
    hidden_width = w_in.shape[1]
    values = inputs.astype(jnp.float32)
    totals = lax.psum(jnp.sum(values, axis=0), "dp")
    mean_val = totals / D
    centered = values - mean_val
    variance = lax.psum(jnp.sum(centered * centered, axis=0), "dp") / D
    normed = (centered * lax.rsqrt(variance + NORM_EPS) * ln_gain[:, None]).astype(jnp.bfloat16)
    row_start = lax.axis_index("dp") * features
    col_start = lax.axis_index("tensor") * hidden_width
    probe_in = probe_signs(probe_seed[0], row_start, col_start, features, hidden_width, FF)
    probe_out = probe_signs(probe_seed[1], row_start, col_start, features, hidden_width, FF)
    token_block = normed
    plain_part = lax.dot_general(
        token_block, w_in, contract_rows, preferred_element_type=jnp.float32
    )
    tangent_part = lax.dot_general(
        token_block, probe_in, contract_rows, preferred_element_type=jnp.float32
    )
    shares = lax.psum_scatter(
        jnp.concatenate([plain_part, tangent_part], axis=1), "dp", scatter_dimension=0, tiled=True
    )
    pre_share = shares[:, :hidden_width]
    pre_dot_share = shares[:, hidden_width:]
    hidden_share, slope_share, curve_share = gelu_parts(pre_share)
    local_forward = jnp.concatenate([hidden_share, slope_share * pre_dot_share], axis=1).astype(
        jnp.bfloat16
    )
    gathered = lax.all_gather(local_forward, "dp", axis=0, tiled=True)
    hidden = gathered[:, :hidden_width]
    hidden_dot = gathered[:, hidden_width:]
    partial_out = lax.dot_general(w_out, hidden, contract_cols, preferred_element_type=jnp.float32)
    partial_dot = lax.dot_general(
        w_out, hidden_dot, contract_cols, preferred_element_type=jnp.float32
    ) + lax.dot_general(probe_out, hidden, contract_cols, preferred_element_type=jnp.float32)
    output, output_dot = (
        lax.psum(partial_out.astype(jnp.bfloat16), "tensor").astype(jnp.float32),
        lax.psum(partial_dot.astype(jnp.bfloat16), "tensor").astype(jnp.float32),
    )
    target = jnp.concatenate([values[:, 1:], jnp.zeros((features, 1), jnp.float32)], axis=1)
    weights = token_weights(segment_ids)
    cotangent = (weights * (output - target)).astype(jnp.bfloat16)
    cotangent_dot = (weights * output_dot).astype(jnp.bfloat16)
    grad_out = jnp.dot(cotangent, hidden, preferred_element_type=jnp.float32)
    hvp_out = jnp.dot(cotangent_dot, hidden, preferred_element_type=jnp.float32) + jnp.dot(
        cotangent, hidden_dot, preferred_element_type=jnp.float32
    )
    plain_part = lax.dot_general(
        cotangent, w_out, contract_rows, preferred_element_type=jnp.float32
    )
    tangent_part = lax.dot_general(
        cotangent_dot, w_out, contract_rows, preferred_element_type=jnp.float32
    ) + lax.dot_general(cotangent, probe_out, contract_rows, preferred_element_type=jnp.float32)
    hidden_back = lax.psum_scatter(
        jnp.concatenate([plain_part, tangent_part], axis=1), "dp", scatter_dimension=0, tiled=True
    )
    back_share = hidden_back[:, :hidden_width]
    back_dot_share = hidden_back[:, hidden_width:]
    local_backward = jnp.concatenate(
        [
            slope_share * back_share,
            curve_share * pre_dot_share * back_share + slope_share * back_dot_share,
        ],
        axis=1,
    ).astype(jnp.bfloat16)
    token_block = normed
    summed = jnp.dot(
        token_block,
        lax.all_gather(local_backward, "dp", axis=0, tiled=True),
        preferred_element_type=jnp.float32,
    )
    grad_in = summed[:, :hidden_width]
    hvp_in = summed[:, hidden_width:]
    new_mom_in, new_hess_in, step_in = sophia_update(mom_in, hess_in, grad_in, hvp_in, probe_in)
    new_mom_out, new_hess_out, step_out = sophia_update(
        mom_out, hess_out, grad_out, hvp_out, probe_out
    )
    return (new_mom_in, new_hess_in, step_in, new_mom_out, new_hess_out, step_out)


def solution(mesh):
    in_specs = (
        P("dp", None),
        P("dp"),
        P(),
        P("dp", "tensor"),
        P("dp", "tensor"),
        P("dp", "tensor"),
        P("dp", "tensor"),
        P("dp", "tensor"),
        P("dp", "tensor"),
        P(),
    )
    out_specs = (
        P("dp", "tensor"),
        P("dp", "tensor"),
        P("dp", "tensor"),
        P("dp", "tensor"),
        P("dp", "tensor"),
        P("dp", "tensor"),
    )
    return jax.shard_map(body, mesh=mesh, in_specs=in_specs, out_specs=out_specs, check_vma=False)
```

profile of v0, /device:TPU:32, one launch (start us, length us, event | category | flops | bytes accessed | tf_op | source)
XLA Modules:
  0.0 2076.2 jit_solution(14748512735968636804)
XLA Ops:
  7.3 1.3 fusion.62
  8.6 0.8 convert_reduce_fusion
  9.4 196.1 %psum.28 = f32[128]{0:T(128)S(1)} all-reduce(f32[128]{0:T(128)S(1)} %convert_reduce_fusion), channel_id=1, replica_groups=mesh['dp'=64,'tensor'=4] {'dp'}, use_global_device_ids=true, to_apply=%region_1.0 | all-reduce | flops 128 | bytes 1024 | tf_op jit(solution)/shard_map/psum | solution.py:69
  205.5 0.8 multiply_reduce_fusion
  206.3 186.1 %psum.29 = f32[128]{0:T(128)S(1)} all-reduce(f32[128]{0:T(128)S(1)} %multiply_reduce_fusion), channel_id=1, replica_groups=mesh['dp'=64,'tensor'=4] {'dp'}, use_global_device_ids=true, to_apply=%region_3.0 | all-reduce | flops 128 | bytes 1024 | tf_op jit(solution)/shard_map/psum | solution.py:72
  392.4 1.7 fusion.61
  394.1 1.7 fusion.28
  395.8 2.1 pad_maximum_fusion
  399.8 737.1 %all-reduce.7.cloned.1.call-done = f32[128,7168]{1,0:T(8,128)} async-done(((f32[128,7168]{1,0:T(8,128)}), f32[128,7168]{1,0:T(8,128)}) %all-reduce.7.cloned.1.call-update) | async-done | bytes 3670032
  1136.9 0.9 multiply_convert_fusion.5
  1137.8 1.1 multiply_convert_fusion.4
  1140.0 76.6 %all-gather.5.cloned.1.call-done = bf16[64,2,7168]{2,1,0:T(2,128)(2,1)} async-done(((bf16[1,2,7168]{2,1,0:T(2,128)(2,1)}), bf16[64,2,7168]{2,1,0:T(2,128)(2,1)}) %all-gather.5.cloned.1.call-update) | async-done | bytes 1835024 | tf_op jit(solution)/shard_map/all_gather | solution.py:94
  1216.6 4.1 reshape.31
  1221.5 1.6 fusion.21
  1223.1 11.1 all-reduce.3
  1235.1 1.8 convolution_add_fusion
  1236.9 2.2 pad_maximum_fusion.1
  1239.4 742.4 %all-reduce.9.cloned.1.call-done = f32[128,7168]{1,0:T(8,128)} async-done(((f32[128,7168]{1,0:T(8,128)}), f32[128,7168]{1,0:T(8,128)}) %all-reduce.9.cloned.1.call-update) | async-done | bytes 3670032
  1981.8 1.2 multiply_convert_fusion.3
  1984.8 1.9 fusion.1
  1986.8 2.2 clamp_convert_fusion
  1989.0 71.8 %all-gather.7.cloned.1.call-done = bf16[64,2,7168]{2,1,0:T(2,128)(2,1)} async-done(((bf16[1,2,7168]{2,1,0:T(2,128)(2,1)}), bf16[64,2,7168]{2,1,0:T(2,128)(2,1)}) %all-gather.7.cloned.1.call-update) | async-done | bytes 1835024 | tf_op jit(solution)/shard_map/all_gather | solution.py:134
  2060.8 4.1 reshape.33
  2066.3 3.4 clamp_convert_fusion.1
  (43 shorter events, 7.4 us)
Async XLA Ops:
  7.2 1213.5 %copy-start = (bf16[112,3584]{1,0:T(8,128)(2,1)S(1)}, bf16[112,3584]{1,0:T(8,128)(2,1)}, u32[]{:S(2)}) copy-start(bf16[112,3584]{1,0:T(8,128)(2,1)} %param.14) | copy-start | bytes 2408452
  7.2 386.9 %copy-start.1 = (bf16[112,128]{1,0:T(8,128)(2,1)S(1)}, bf16[112,128]{1,0:T(8,128)(2,1)}, u32[]{:S(2)}) copy-start(bf16[112,128]{1,0:T(8,128)(2,1)} %param.10) | copy-start | bytes 86020
  7.2 386.9 %copy-start.4 = (f32[112]{0:T(128)S(1)}, f32[112]{0:T(128)}, u32[]{:S(2)}) copy-start(f32[112]{0:T(128)} %param.11) | copy-start | bytes 1348
  7.2 1129.7 %all-reduce.7.cloned.1.call-start = ((), (), s32[]{:S(2)}) async-start(), calls=%async_computation.2 | async-start | bytes 7340032
  397.9 0.7 copy-start.8
  397.9 741.8 %copy-start.7 = (s32[128]{0:T(128)S(1)}, s32[128]{0:T(128)}, u32[]{:S(2)}) copy-start(s32[128]{0:T(128)} %param.12) | copy-start | bytes 1540
  397.9 818.7 %all-gather.5.cloned.1.call-start = ((), (), s32[]{:S(2)}) async-start(), calls=%async_computation | async-start | bytes 1863680 | tf_op jit(solution)/shard_map/all_gather | solution.py:94
  1139.6 842.2 %all-reduce.9.cloned.1.call-start = ((), (), s32[]{:S(2)}) async-start(), calls=%async_computation.3 | async-start | bytes 7340032
  1239.1 821.7 %all-gather.7.cloned.1.call-start = ((), (), s32[]{:S(2)}) async-start(), calls=%async_computation.1 | async-start | bytes 1863680 | tf_op jit(solution)/shard_map/all_gather | solution.py:134
  1983.7 1.1 copy-start.5
  1984.8 2.0 copy-start.6
  2064.9 1.1 copy-start.2
  2064.9 1.4 copy-start.3
Sparse Core Ops, SparseCore 0:
  398.0 738.8 all-reduce.6
  1141.3 75.2 all-gather.4
  1239.3 742.4 all-reduce.8
  1985.5 75.2 all-gather.6
where the time goes:
time: 2080 us
  waiting for transfers between devices  1630 us (78%)
  blocking collectives  393 us (19%)
    unnamed x6, waiting for transfers between devices  1480 us
    psum x1, blocking collectives, body(): totals = lax.psum(jnp.sum(values, axis=0), 'dp')  196 us
    psum x1, blocking collectives, body(): variance = lax.psum(jnp.sum(centered * centered, axis=0), 'dp') / D  186 us
    all_gather x1, waiting for transfers between devices, body(): gathered = lax.all_gather(local_forward, 'dp', axis=0, tiled=True)  76.6 us
    all_gather x1, waiting for transfers between devices, body(): lax.all_gather(local_backward, 'dp', axis=0, tiled=True)  71.8 us
  transfers between devices with their start and end apart: 4, of which 4 were waited for; matrix products, arithmetic and copies ran while one was open for 0% of the time, Pallas kernels for 0%

commit v1 on v0

v1 whole, which is shorter than its diff:
```python
import jax
import jax.numpy as jnp
from jax import lax
from jax.sharding import Mesh, PartitionSpec as P

D = 7168
FF = 14336


BETA_ONE = 0.96
BETA_TWO = 0.99
SCALE_GAMMA = 0.05
FLOOR_EPS = 0.002
NORM_EPS = 1e-05
hash_factor = 73244475
contract_rows = (((0,), (0,)), ((), ()))
contract_cols = (((1,), (1,)), ((), ()))
PLANE = ("y", "x")
DEPTH = ("h",)
DP = PLANE + DEPTH
TENSOR = ("l", "c")


def mixing(words):
    words = (words ^ words >> 16 & 65535) * hash_factor
    words = (words ^ words >> 16 & 65535) * hash_factor
    return words ^ words >> 16 & 65535


def probe_signs(seed_word, row_start, col_start, row_count, col_count, total_cols):
    rows_index = row_start + jnp.arange(row_count, dtype=jnp.int32)[:, None]
    cols_index = col_start + jnp.arange(col_count, dtype=jnp.int32)[None, :]
    hashed = mixing(rows_index * total_cols + cols_index ^ seed_word)
    return (1 - 2 * (hashed & 1)).astype(jnp.bfloat16)


def gelu_parts(preact):
    normal_cdf = 0.5 * (1.0 + lax.erf(preact * 0.7071067811865476))
    normal_pdf = jnp.exp(-0.5 * preact * preact) * 0.3989422804014327
    return (
        preact * normal_cdf,
        normal_cdf + preact * normal_pdf,
        normal_pdf * (2.0 - preact * preact),
    )


def token_weights(segment_ids):
    following = jnp.concatenate([segment_ids[1:], jnp.full((1,), -1, jnp.int32)])
    valid = (following == segment_ids).astype(jnp.float32)
    same_doc = (segment_ids[:, None] == segment_ids[None, :]).astype(jnp.float32)
    counts = jnp.dot(same_doc, valid, precision=lax.Precision.HIGHEST)
    return valid / jnp.maximum(counts, 1.0)


def sophia_update(moment_old, curve_old, gradient, product, probe):
    moment = BETA_ONE * moment_old.astype(jnp.float32) + (1.0 - BETA_ONE) * gradient
    curvature = (
        BETA_TWO * curve_old.astype(jnp.float32)
        + (1.0 - BETA_TWO) * probe.astype(jnp.float32) * product
    )
    stepped = jnp.clip(moment / jnp.maximum(SCALE_GAMMA * curvature, FLOOR_EPS), -1.0, 1.0)
    return (
        moment.astype(jnp.bfloat16),
        curvature.astype(jnp.bfloat16),
        stepped.astype(jnp.bfloat16),
    )


def swap(blocks, axes):
    return lax.all_to_all(blocks, axes, 0, 0, tiled=True)


def spread(block, axes):
    count = lax.axis_size(axes)
    return swap(jnp.broadcast_to(block[None], (count,) + block.shape), axes)


def norm_stats(values):
    features = values.shape[0]
    own_mean = jnp.sum(values, axis=0) / features
    own_centered = values - own_mean
    own_square = jnp.sum(own_centered * own_centered, axis=0)
    every = spread(jnp.stack([own_mean, own_square]), DP)
    mean_val = jnp.mean(every[:, 0], axis=0)
    apart = every[:, 0] - mean_val
    variance = jnp.sum(every[:, 1] + features * apart * apart, axis=0) / D
    return mean_val, variance


def summed_block(first, second):
    width, tokens = first.shape
    planes = lax.axis_size(PLANE)
    blocks = jnp.concatenate(
        [part.astype(jnp.bfloat16).reshape(planes, width // planes, tokens) for part in (first, second)],
        axis=1,
    )
    own = jnp.sum(swap(blocks, PLANE).astype(jnp.float32), axis=0).astype(jnp.bfloat16)
    total = jnp.sum(spread(own, DEPTH).astype(jnp.float32), axis=0)
    return total[: width // planes], total[width // planes :]


def gathered_pair(first, second):
    units, tokens = first.shape
    both = spread(jnp.concatenate([first, second], axis=0).astype(jnp.bfloat16), PLANE)
    return both[:, :units].reshape(-1, tokens), both[:, units:].reshape(-1, tokens)


def body(inputs, ln_gain, segment_ids, w_in, w_out, mom_in, mom_out, hess_in, hess_out, probe_seed):
    features, length = inputs.shape
    hidden_width = w_in.shape[1]
    values = inputs.astype(jnp.float32)
    mean_val, variance = norm_stats(values)
    centered = values - mean_val
    normed = (centered * lax.rsqrt(variance + NORM_EPS) * ln_gain[:, None]).astype(jnp.bfloat16)
    row_start = lax.axis_index(DP) * features
    col_start = lax.axis_index(TENSOR) * hidden_width
    probe_in = probe_signs(probe_seed[0], row_start, col_start, features, hidden_width, FF)
    probe_out = probe_signs(probe_seed[1], row_start, col_start, features, hidden_width, FF)

    def onto_hidden(weight, block):
        return lax.dot_general(weight, block, contract_rows, preferred_element_type=jnp.float32)

    def onto_features(weight, block):
        return jnp.dot(weight, block, preferred_element_type=jnp.float32)

    def onto_weight(left, right):
        return lax.dot_general(left, right, contract_cols, preferred_element_type=jnp.float32)

    pre, pre_dot = summed_block(onto_hidden(w_in, normed), onto_hidden(probe_in, normed))
    act, slope, curve = gelu_parts(pre)
    hidden, hidden_dot = gathered_pair(act, slope * pre_dot)
    partial = jnp.stack(
        [
            onto_features(w_out, hidden),
            onto_features(w_out, hidden_dot) + onto_features(probe_out, hidden),
        ]
    ).astype(jnp.bfloat16)
    output, output_dot = jnp.sum(lax.all_gather(partial, TENSOR).astype(jnp.float32), axis=0)
    target = jnp.concatenate([values[:, 1:], jnp.zeros((features, 1), jnp.float32)], axis=1)
    weights = token_weights(segment_ids)
    cotangent = (weights * (output - target)).astype(jnp.bfloat16)
    cotangent_dot = (weights * output_dot).astype(jnp.bfloat16)
    back, back_dot = summed_block(
        onto_hidden(w_out, cotangent),
        onto_hidden(w_out, cotangent_dot) + onto_hidden(probe_out, cotangent),
    )
    pre_grad, pre_grad_dot = gathered_pair(
        slope * back, curve * pre_dot * back + slope * back_dot
    )
    grad_out = onto_weight(cotangent, hidden)
    hvp_out = onto_weight(cotangent_dot, hidden) + onto_weight(cotangent, hidden_dot)
    grad_in = onto_weight(normed, pre_grad)
    hvp_in = onto_weight(normed, pre_grad_dot)
    new_mom_in, new_hess_in, step_in = sophia_update(mom_in, hess_in, grad_in, hvp_in, probe_in)
    new_mom_out, new_hess_out, step_out = sophia_update(
        mom_out, hess_out, grad_out, hvp_out, probe_out
    )
    return (new_mom_in, new_hess_in, step_in, new_mom_out, new_hess_out, step_out)


def solution(mesh):
    torus = Mesh(mesh.devices.reshape(4, 4, 4, 2, 2), ("y", "x", "h", "l", "c"))
    matrix = P(DP, TENSOR)
    in_specs = (P(DP, None), P(DP), P()) + (matrix,) * 6 + (P(),)
    return jax.shard_map(
        body, mesh=torus, in_specs=in_specs, out_specs=(matrix,) * 6, check_vma=False
    )
```

time: 2080 us -> 211 us (0.10)
  waiting for transfers between devices: 1630 us -> 51.4 us
  blocking collectives: 393 us -> 97.1 us
  starting transfers between devices: 0.34 us -> 21.4 us
    unnamed x6 -> x0, waiting for transfers between devices: 1480 us -> none
    psum x3 -> x0, blocking collectives: 393 us -> none  [the longest x1 196 us: body(): totals = lax.psum(jnp.sum(values, axis=0), 'dp')]
    all_gather x2 -> x0, waiting for transfers between devices: 148 us -> none  [the longest x1 76.6 us: body(): gathered = lax.all_gather(local_forward, 'dp', axis=0, tiled=True)]
    all_to_all x0 -> x4, blocking collectives: none -> 91.3 us  [swap(): return lax.all_to_all(blocks, axes, 0, 0, tiled=True)]
    all_to_all x0 -> x3, waiting for transfers between devices: none -> 51.4 us  [swap(): return lax.all_to_all(blocks, axes, 0, 0, tiled=True)]
    all_to_all x0 -> x3, starting transfers between devices: none -> 21.4 us  [swap(): return lax.all_to_all(blocks, axes, 0, 0, tiled=True)]
  transfers between devices with their start and end apart: 4 -> 3, of which waited for: 4 -> 3; matrix products, arithmetic and copies ran while one was open for 0% -> 4% of each run, Pallas kernels for 0% -> 0%
where the time goes in v1:
time: 211 us; the launch traced here: 209 us
  blocking collectives  97.1 us (46%)
  waiting for transfers between devices  51.4 us (24%)
  matrix products  22.3 us (11%)
  starting transfers between devices  21.4 us (10%)
  local copies, waits for them, and re-layouts  12 us (6%)
  other arithmetic  3.59 us (2%)
    all_to_all x4, blocking collectives, swap(): return lax.all_to_all(blocks, axes, 0, 0, tiled=True)  91.3 us
    all_to_all x3, waiting for transfers between devices, swap(): return lax.all_to_all(blocks, axes, 0, 0, tiled=True)  51.4 us
    all_to_all x3, starting transfers between devices, swap(): return lax.all_to_all(blocks, axes, 0, 0, tiled=True)  21.4 us
    dot_general x5, matrix products, onto_hidden(): lax.dot_general(weight, block, contract_rows, preferred_element_type=jnp....  9.7 us
    dot_general x5, matrix products, onto_weight(): lax.dot_general(left, right, contract_cols, preferred_element_type=jnp.fl...  9.5 us
    all_gather x1, blocking collectives, body(): lax.all_gather(partial, TENSOR).astype(jnp.float32)  5.83 us
    broadcast_in_dim x5, local copies, waits for them, and re-layouts, spread(): return swap(jnp.broadcast_to(block[None], (count,) + block.shape), axes)  4.98 us
  transfers between devices with their start and end apart: 3, of which 3 were waited for; matrix products, arithmetic and copies ran while one was open for 4% of the time, Pallas kernels for 0%

profile of v1, /device:TPU:32, one launch (start us, length us, event | category | flops | bytes accessed | tf_op | source)
XLA Modules:
  0.0 209.0 jit_solution(5687259945267221546)
XLA Ops:
  2.9 13.7 %all-to-all-start = ((f32[64,2,128]{2,1,0:T(2,128)}), f32[64,2,128]{2,1,0:T(2,128)S(1)}, u32[]{:S(2)}, u32[]{:S(2)}) async-start(f32[64,2,128]{2,1,0:T(2,128)} %broadcast_in_dim.10), calls=%async_computation | async-start | bytes 131072 | tf_op jit(solution)/shard_map/all_to_all | solution.py:70
  16.6 1.3 fusion.76
  18.0 10.8 %all-to-all-done = f32[64,2,128]{2,1,0:T(2,128)S(1)} async-done(((f32[64,2,128]{2,1,0:T(2,128)}), f32[64,2,128]{2,1,0:T(2,128)S(1)}, u32[]{:S(2)}, u32[]{:S(2)}) %all-to-all-start) | async-done | bytes 65568 | tf_op jit(solution)/shard_map/all_to_all | solution.py:70
  28.9 1.7 fusion.6
  31.3 1.7 convolution_convert_fusion.1
  33.2 28.1 %all_to_all.35 = bf16[16,448,128]{2,1,0:T(8,128)(2,1)S(1)} all-to-all(bf16[16,448,128]{2,1,0:T(8,128)(2,1)S(1)} %pad_maximum_fusion), channel_id=1, replica_groups=mesh['y'=4,'x'=4,'h'=4,'l'=2,'c'=2] {'y','x'}, dimensions={0} | all-to-all | bytes 3670016 | tf_op jit(solution)/shard_map/all_to_all | solution.py:70
  61.6 15.5 %all_to_all.36 = bf16[4,448,128]{2,1,0:T(8,128)(2,1)S(1)} all-to-all(bf16[4,448,128]{2,1,0:T(8,128)(2,1)S(1)} %broadcast_in_dim.11), channel_id=1, replica_groups=mesh['y'=4,'x'=4,'h'=4,'l'=2,'c'=2] {'h'}, dimensions={0} | all-to-all | bytes 917504 | tf_op jit(solution)/shard_map/all_to_all | solution.py:70
  77.9 1.6 broadcast_in_dim.12
  79.5 3.8 %all-to-all-start.3 = ((bf16[16,448,128]{2,1,0:T(8,128)(2,1)}), bf16[16,448,128]{2,1,0:T(8,128)(2,1)S(1)}, u32[]{:S(2)}, u32[]{:S(2)}) async-start(bf16[16,448,128]{2,1,0:T(8,128)(2,1)} %broadcast_in_dim.12), calls=%async_computation.3 | async-start | bytes 3670016 | tf_op jit(solution)/shard_map/all_to_all | solution.py:70
  85.0 21.9 %all-to-all-done.3 = bf16[16,448,128]{2,1,0:T(8,128)(2,1)S(1)} async-done(((bf16[16,448,128]{2,1,0:T(8,128)(2,1)}), bf16[16,448,128]{2,1,0:T(8,128)(2,1)S(1)}, u32[]{:S(2)}, u32[]{:S(2)}) %all-to-all-start.3) | async-done | bytes 1835040 | tf_op jit(solution)/shard_map/all_to_all | solution.py:70
  107.8 1.6 fusion.30
  109.8 5.8 %all_gather.4 = bf16[4,2,112,128]{3,2,1,0:T(8,128)(2,1)S(1)} all-gather(bf16[1,2,112,128]{3,2,1,0:T(8,128)(2,1)S(1)} %pad_maximum_fusion.4), channel_id=1, replica_groups=mesh['y'=4,'x'=4,'h'=4,'l'=2,'c'=2] {'l','c'}, dimensions={0}, use_global_device_ids=true | all-gather | bytes 286720 | tf_op jit(solution)/shard_map/all_gather | solution.py:138
  115.7 1.7 convolution_bitcast_fusion
  119.1 4.2 %fusion.5 = bf16[3584,128]{0,1:T(8,128)(2,1)} fusion(f32[3584,128]{0,1:T(8,128)} %convolution_bitcast_fusion, bf16[112,128]{1,0:T(8,128)(2,1)} %copy-done.12, s32[]{:T(128)} %bitcast.15, s32[3584]{0:T(1024)} %copy-done.14, s32[112]{0:T(128)} %copy-done.30), kind=kOutput, calls=%fused_computation.11 | convolution fusion | flops 110501888 | bytes 2795972 | tf_op jit(solution)/shard_map/dot_general | solution.py:121
  123.3 1.5 copy.37
  125.0 29.1 %all_to_all.37 = bf16[16,448,128]{2,1,0:T(8,128)(2,1)S(1)} all-to-all(bf16[16,448,128]{2,1,0:T(8,128)(2,1)S(1)} %pad_maximum_fusion.1), channel_id=1, replica_groups=mesh['y'=4,'x'=4,'h'=4,'l'=2,'c'=2] {'y','x'}, dimensions={0} | all-to-all | bytes 3670016 | tf_op jit(solution)/shard_map/all_to_all | solution.py:70
  156.0 18.6 %all_to_all.38 = bf16[4,448,128]{2,1,0:T(8,128)(2,1)S(1)} all-to-all(bf16[4,448,128]{2,1,0:T(8,128)(2,1)S(1)} %broadcast_in_dim.13), channel_id=1, replica_groups=mesh['y'=4,'x'=4,'h'=4,'l'=2,'c'=2] {'h'}, dimensions={0} | all-to-all | bytes 917504 | tf_op jit(solution)/shard_map/all_to_all | solution.py:70
  174.8 1.6 broadcast_in_dim.14
  176.4 3.9 %all-to-all-start.6 = ((bf16[16,448,128]{2,1,0:T(8,128)(2,1)}), bf16[16,448,128]{2,1,0:T(8,128)(2,1)S(1)}, u32[]{:S(2)}, u32[]{:S(2)}) async-start(bf16[16,448,128]{2,1,0:T(8,128)(2,1)} %broadcast_in_dim.14), calls=%async_computation.6 | async-start | bytes 3670016 | tf_op jit(solution)/shard_map/all_to_all | solution.py:70
  181.8 1.9 fusion.1
  183.8 2.2 %clamp_convert_fusion = (bf16[112,3584]{1,0:T(8,128)(2,1)}, bf16[112,3584]{1,0:T(8,128)(2,1)}, bf16[112,3584]{1,0:T(8,128)(2,1)}) fusion(f32[112,3584]{1,0:T(8,128)S(1)} %fusion.1, bf16[112,128]{1,0:T(8,128)(2,1)S(1)} %copy-done.13, bf16[3584,128]{1,0:T(8,128)(2,1)S(1)} %bitcast.82, bf16[112,3584]{1,0:T(8,128)(2,1)S(1)} %copy-done.26), kind=kOutput, calls=%fused_computation.37 | convolution fusion | flops 107175936 | bytes 5763072 | tf_op jit(solution)/shard_map/dot_general | solution.py:127
  186.0 18.8 %all-to-all-done.6 = bf16[16,448,128]{2,1,0:T(8,128)(2,1)S(1)} async-done(((bf16[16,448,128]{2,1,0:T(8,128)(2,1)}), bf16[16,448,128]{2,1,0:T(8,128)(2,1)S(1)}, u32[]{:S(2)}, u32[]{:S(2)}) %all-to-all-start.6) | async-done | bytes 1835040 | tf_op jit(solution)/shard_map/all_to_all | solution.py:70
  204.9 1.9 fusion.3
  206.8 2.2 %clamp_convert_fusion.1 = (bf16[112,3584]{1,0:T(8,128)(2,1)}, bf16[112,3584]{1,0:T(8,128)(2,1)}, bf16[112,3584]{1,0:T(8,128)(2,1)}) fusion(f32[112,3584]{1,0:T(8,128)S(1)} %fusion.3, bf16[3584,128]{1,0:T(8,128)(2,1)S(1)} %bitcast.88, bf16[112,128]{1,0:T(8,128)(2,1)S(1)} %copy-done.9, f32[112]{0:T(128)S(1)} %copy-done.22, f32[128]{0:T(128)S(1)} %copy-done.24, ...), kind=kOutput, calls=%fused_computation.38 | convolution fusion | flops 107247616 | bytes 5764544 | tf_op jit(solution)/shard_map/dot_general | solution.py:127
  (107 shorter events, 12.7 us)
Async XLA Ops:
  0.6 106.4 %copy-start = (bf16[112,3584]{1,0:T(8,128)(2,1)S(1)}, bf16[112,3584]{1,0:T(8,128)(2,1)}, u32[]{:S(2)}) copy-start(bf16[112,3584]{1,0:T(8,128)(2,1)} %param.14) | copy-start | bytes 2408452
  2.9 25.8 %all-to-all-start = ((f32[64,2,128]{2,1,0:T(2,128)}), f32[64,2,128]{2,1,0:T(2,128)S(1)}, u32[]{:S(2)}, u32[]{:S(2)}) async-start(f32[64,2,128]{2,1,0:T(2,128)} %broadcast_in_dim.10), calls=%async_computation | async-start | bytes 131072 | tf_op jit(solution)/shard_map/all_to_all | solution.py:70
  18.0 13.3 %copy-start.30 = (s32[112]{0:T(128)}, s32[112]{0:T(128)S(1)}, u32[]{:S(2)}) copy-start(s32[112]{0:T(128)S(1)} %add_multiply_fusion.1) | copy-start | bytes 1348
  18.0 13.3 %copy-start.14 = (s32[3584]{0:T(1024)}, s32[3584]{0:T(1024)S(1)}, u32[]{:S(2)}) copy-start(s32[3584]{0:T(1024)S(1)} %iota_add_fusion) | copy-start | bytes 43012
  28.9 2.4 %copy-start.19 = (f32[128]{0:T(128)}, f32[128]{0:T(128)S(1)}, u32[]{:S(2)}) copy-start(f32[128]{0:T(128)S(1)} %broadcast_multiply_fusion) | copy-start | bytes 1540
  28.9 2.4 %copy-start.23 = (f32[128]{0:T(128)}, f32[128]{0:T(128)S(1)}, u32[]{:S(2)}) copy-start(f32[128]{0:T(128)S(1)} %add_rsqrt_fusion) | copy-start | bytes 1540
  28.9 2.4 %copy-start.7 = (bf16[112,128]{1,0:T(8,128)(2,1)S(1)}, bf16[112,128]{1,0:T(8,128)(2,1)}, u32[]{:S(2)}) copy-start(bf16[112,128]{1,0:T(8,128)(2,1)} %param.10) | copy-start | bytes 86020
  28.9 2.4 %copy-start.21 = (f32[112]{0:T(128)S(1)}, f32[112]{0:T(128)}, u32[]{:S(2)}) copy-start(f32[112]{0:T(128)} %param.11) | copy-start | bytes 1348
  79.5 3.9 %copy-start.8 = (bf16[112,128]{1,0:T(8,128)(2,1)S(1)}, bf16[112,128]{1,0:T(8,128)(2,1)}, u32[]{:S(2)}) copy-start(bf16[112,128]{1,0:T(8,128)(2,1)} %param.10) | copy-start | bytes 86020
  79.5 4.6 %copy-start.29 = (s32[128]{0:T(128)S(1)}, s32[128]{0:T(128)}, u32[]{:S(2)}) copy-start(s32[128]{0:T(128)} %param.12) | copy-start | bytes 1540
  79.5 27.3 %all-to-all-start.3 = ((bf16[16,448,128]{2,1,0:T(8,128)(2,1)}), bf16[16,448,128]{2,1,0:T(8,128)(2,1)S(1)}, u32[]{:S(2)}, u32[]{:S(2)}) async-start(bf16[16,448,128]{2,1,0:T(8,128)(2,1)} %broadcast_in_dim.12), calls=%async_computation.3 | async-start | bytes 3670016 | tf_op jit(solution)/shard_map/all_to_all | solution.py:70
  107.0 2.4 %copy-start.1 = (bf16[16,224,128]{2,1,0:T(8,128)(2,1)}, bf16[16,224,128]{2,1,0:T(8,128)(2,1)S(1)}, u32[]{:S(2)}) copy-start(bf16[16,224,128]{2,1,0:T(8,128)(2,1)S(1)} %get-tuple-element.10) | copy-start | bytes 2752516
  109.4 6.3 %copy-start.18 = (f32[128]{0:T(128)S(1)}, f32[128]{0:T(128)}, u32[]{:S(2)}) copy-start(f32[128]{0:T(128)} %fusion.29) | copy-start | bytes 1540
  109.8 7.6 %copy-start.11 = (f32[112,127]{1,0:T(8,128)S(1)}, f32[112,127]{1,0:T(8,128)}, u32[]{:S(2)}) copy-start(f32[112,127]{1,0:T(8,128)} %slice.63) | copy-start | bytes 170692
  155.0 19.7 %copy-start.4 = (f32[448,128]{1,0:T(8,128)S(1)}, f32[448,128]{1,0:T(8,128)}, u32[]{:S(2)}) copy-start(f32[448,128]{1,0:T(8,128)} %copy-done.3) | copy-start | bytes 688132
  155.0 19.7 %copy-start.6 = (f32[224,128]{1,0:T(8,128)S(1)}, f32[224,128]{1,0:T(8,128)}, u32[]{:S(2)}) copy-start(f32[224,128]{1,0:T(8,128)} %copy-done.5) | copy-start | bytes 344068
  176.4 28.3 %all-to-all-start.6 = ((bf16[16,448,128]{2,1,0:T(8,128)(2,1)}), bf16[16,448,128]{2,1,0:T(8,128)(2,1)S(1)}, u32[]{:S(2)}, u32[]{:S(2)}) async-start(bf16[16,448,128]{2,1,0:T(8,128)(2,1)} %broadcast_in_dim.14), calls=%async_computation.6 | async-start | bytes 3670016 | tf_op jit(solution)/shard_map/all_to_all | solution.py:70
  185.9 18.9 %copy-start.9 = (bf16[112,128]{1,0:T(8,128)(2,1)S(1)}, bf16[112,128]{1,0:T(8,128)(2,1)}, u32[]{:S(2)}) copy-start(bf16[112,128]{1,0:T(8,128)(2,1)} %param.10) | copy-start | bytes 86020
  185.9 18.9 %copy-start.17 = (s32[3584]{0:T(1024)S(1)}, s32[3584]{0:T(1024)}, u32[]{:S(2)}) copy-start(s32[3584]{0:T(1024)} %copy-done.14) | copy-start | bytes 43012
  185.9 18.9 %copy-start.20 = (f32[128]{0:T(128)S(1)}, f32[128]{0:T(128)}, u32[]{:S(2)}) copy-start(f32[128]{0:T(128)} %copy-done.19) | copy-start | bytes 1540
  185.9 18.9 %copy-start.22 = (f32[112]{0:T(128)S(1)}, f32[112]{0:T(128)}, u32[]{:S(2)}) copy-start(f32[112]{0:T(128)} %param.11) | copy-start | bytes 1348
  185.9 18.9 %copy-start.24 = (f32[128]{0:T(128)S(1)}, f32[128]{0:T(128)}, u32[]{:S(2)}) copy-start(f32[128]{0:T(128)} %copy-done.23) | copy-start | bytes 1540
  185.9 18.9 %copy-start.27 = (bf16[112,3584]{1,0:T(8,128)(2,1)S(1)}, bf16[112,3584]{1,0:T(8,128)(2,1)}, u32[]{:S(2)}) copy-start(bf16[112,3584]{1,0:T(8,128)(2,1)} %param.17) | copy-start | bytes 2408452
  186.0 18.9 %copy-start.33 = (s32[112]{0:T(128)S(1)}, s32[112]{0:T(128)}, u32[]{:S(2)}) copy-start(s32[112]{0:T(128)} %copy-done.30) | copy-start | bytes 1348
  (13 other events, 16.1 us)

commit v2 on v1

v2 whole, which is shorter than its diff:
```python
import jax
import jax.numpy as jnp
from jax import lax
from jax.sharding import Mesh, PartitionSpec as P

D = 7168
FF = 14336


BETA_ONE = 0.96
BETA_TWO = 0.99
SCALE_GAMMA = 0.05
FLOOR_EPS = 0.002
NORM_EPS = 1e-05
hash_factor = 73244475
contract_rows = (((0,), (0,)), ((), ()))
contract_cols = (((1,), (1,)), ((), ()))
PLANE = ("y", "x")
DEPTH = ("h",)
DP = PLANE + DEPTH
TENSOR = ("l", "c")


def mixing(words):
    words = (words ^ words >> 16 & 65535) * hash_factor
    words = (words ^ words >> 16 & 65535) * hash_factor
    return words ^ words >> 16 & 65535


def probe_signs(seed_word, rows_index, col_start, col_count):
    cols_index = col_start + jnp.arange(col_count, dtype=jnp.int32)[None, :]
    hashed = mixing(rows_index[:, None] * FF + cols_index ^ seed_word)
    return (1 - 2 * (hashed & 1)).astype(jnp.bfloat16)


def gelu_parts(preact):
    normal_cdf = 0.5 * (1.0 + lax.erf(preact * 0.7071067811865476))
    normal_pdf = jnp.exp(-0.5 * preact * preact) * 0.3989422804014327
    return (
        preact * normal_cdf,
        normal_cdf + preact * normal_pdf,
        normal_pdf * (2.0 - preact * preact),
    )


def token_weights(segment_ids):
    following = jnp.concatenate([segment_ids[1:], jnp.full((1,), -1, jnp.int32)])
    valid = (following == segment_ids).astype(jnp.float32)
    same_doc = (segment_ids[:, None] == segment_ids[None, :]).astype(jnp.float32)
    counts = jnp.dot(same_doc, valid, precision=lax.Precision.HIGHEST)
    return valid / jnp.maximum(counts, 1.0)


def sophia_update(moment_old, curve_old, gradient, product, probe):
    moment = BETA_ONE * moment_old.astype(jnp.float32) + (1.0 - BETA_ONE) * gradient
    curvature = (
        BETA_TWO * curve_old.astype(jnp.float32)
        + (1.0 - BETA_TWO) * probe.astype(jnp.float32) * product
    )
    stepped = jnp.clip(moment / jnp.maximum(SCALE_GAMMA * curvature, FLOOR_EPS), -1.0, 1.0)
    return (
        moment.astype(jnp.bfloat16),
        curvature.astype(jnp.bfloat16),
        stepped.astype(jnp.bfloat16),
    )


def swap(blocks, axes):
    return lax.all_to_all(blocks, axes, 0, 0, tiled=True)


def spread(block, axes):
    count = lax.axis_size(axes)
    return swap(jnp.broadcast_to(block[None], (count,) + block.shape), axes)


def turns(block):
    count = lax.axis_size(DEPTH)
    return [block] + [
        lax.ppermute(block, DEPTH, [(at, (at + shift) % count) for at in range(count)])
        for shift in range(1, count)
    ]


def three_terms(value):
    terms, rest = [], value
    for _ in range(3):
        terms.append(rest.astype(jnp.bfloat16))
        rest = rest - terms[-1].astype(jnp.float32)
    return terms


def column_blocks(matrix, count):
    rows, cols = matrix.shape
    return matrix.reshape(rows, count, cols // count).transpose(1, 0, 2)


def dot_rows(left, right, **options):
    return lax.dot_general(left, right, contract_rows, preferred_element_type=jnp.float32, **options)


def dot_cols(left, right):
    return lax.dot_general(left, right, contract_cols, preferred_element_type=jnp.float32)


def dot_plain(left, right):
    return jnp.dot(left, right, preferred_element_type=jnp.float32)


def body(inputs, ln_gain, segment_ids, w_in, w_out, mom_in, mom_out, hess_in, hess_out, probe_seed):
    features, length = inputs.shape
    hidden_width = w_in.shape[1]
    planes = lax.axis_size(PLANE)
    deep = lax.axis_size(DEPTH)
    units = hidden_width // planes
    plane_rows = planes * features
    padded = -(-units // length) * length
    values = inputs.astype(jnp.float32)

    row_index = lax.axis_index(DP) * features + jnp.arange(features, dtype=jnp.int32)
    col_start = lax.axis_index(TENSOR) * hidden_width
    plane_index = (
        (jnp.arange(planes, dtype=jnp.int32)[:, None] * deep + lax.axis_index(DEPTH)) * features
        + jnp.arange(features, dtype=jnp.int32)[None, :]
    ).reshape(plane_rows)
    unit_start = col_start + lax.axis_index(PLANE) * units

    gain_terms = jnp.stack(three_terms(ln_gain), axis=1)
    side = jnp.concatenate(
        [gain_terms, jnp.zeros((features, padded - units - 3), jnp.bfloat16), inputs], axis=1
    )
    sent = jnp.concatenate(
        [column_blocks(w_in, planes), jnp.broadcast_to(side[None], (planes,) + side.shape)], axis=2
    )
    got = swap(sent, PLANE).reshape(plane_rows, padded + length)
    plane_in = got[:, :units]
    gain_cols = got[:, units : units + 3]
    plane_gain = jnp.sum(gain_cols.astype(jnp.float32), axis=1, keepdims=True)
    plane_values = got[:, padded:].astype(jnp.float32)
    plane_out = swap(column_blocks(w_out, planes), PLANE).reshape(plane_rows, units)
    plane_probe_in = probe_signs(probe_seed[0], plane_index, unit_start, units)
    plane_probe_out = probe_signs(probe_seed[1], plane_index, unit_start, units)

    plane_mean = jnp.mean(plane_values, axis=0)
    plane_centered = plane_values - plane_mean
    plane_square = jnp.sum(plane_centered * plane_centered, axis=0)
    scaled = (plane_centered * plane_gain).astype(jnp.bfloat16)
    gain_sum = jnp.concatenate(
        [
            jnp.pad(jnp.sum(dot_rows(gain_cols, part), axis=0), (0, padded - units))
            for part in (plane_in, plane_probe_in)
        ]
    ).reshape(-1, length)
    extras = jnp.concatenate(
        [gain_sum.astype(jnp.bfloat16)]
        + [term[None] for term in three_terms(plane_mean) + three_terms(plane_square)],
        axis=0,
    )
    extra_rows = extras.shape[0]
    extras = jnp.pad(extras, ((0, -extra_rows % 16), (0, 0)))
    every = turns(
        jnp.concatenate(
            [
                dot_rows(plane_in, scaled).astype(jnp.bfloat16),
                dot_rows(plane_probe_in, scaled).astype(jnp.bfloat16),
                extras,
            ],
            axis=0,
        )
    )
    every = [part.astype(jnp.float32) for part in every]
    tails = jnp.stack([part[2 * units : 2 * units + extra_rows] for part in every])
    sums = tails[:, : 2 * padded // length].reshape(deep, 2, padded)[:, :, :units]
    stats = jnp.sum(tails[:, 2 * padded // length :].reshape(deep, 2, 3, length), axis=2)
    mean_val = jnp.mean(stats[:, 0], axis=0)
    apart = stats[:, 0] - mean_val
    variance = jnp.sum(stats[:, 1] + plane_rows * apart * apart, axis=0) / D
    scale = lax.rsqrt(variance + NORM_EPS)
    totals = sum(part[: 2 * units] for part in every)
    pre, pre_dot = (
        scale
        * (
            totals[at * units : (at + 1) * units]
            + dot_rows(sums[:, at], apart, precision=lax.Precision.HIGHEST)
        )
        for at in range(2)
    )

    act, slope, curve = gelu_parts(pre)
    hidden = act.astype(jnp.bfloat16)
    hidden_dot = (slope * pre_dot).astype(jnp.bfloat16)
    all_hidden = lax.all_gather(jnp.stack([hidden, hidden_dot]), PLANE, axis=1)
    all_hidden = all_hidden.reshape(2, hidden_width, length)

    parts = jnp.concatenate(
        [
            dot_plain(plane_out, hidden).astype(jnp.bfloat16).reshape(planes, features, length),
            (dot_plain(plane_out, hidden_dot) + dot_plain(plane_probe_out, hidden))
            .astype(jnp.bfloat16)
            .reshape(planes, features, length),
        ],
        axis=1,
    )
    share = jnp.sum(swap(parts, PLANE).astype(jnp.float32), axis=0).astype(jnp.bfloat16)
    share = share.reshape(2, features, length)
    output, output_dot = jnp.sum(lax.all_gather(share, TENSOR).astype(jnp.float32), axis=0)
    target = jnp.concatenate([values[:, 1:], jnp.zeros((features, 1), jnp.float32)], axis=1)
    weights = token_weights(segment_ids)
    cotangent = (weights * (output - target)).astype(jnp.bfloat16)
    cotangent_dot = (weights * output_dot).astype(jnp.bfloat16)

    plane_cot = spread(jnp.concatenate([cotangent, cotangent_dot], axis=0), PLANE)
    plane_cot_dot = plane_cot[:, features:].reshape(plane_rows, length)
    plane_cot = plane_cot[:, :features].reshape(plane_rows, length)
    back_parts = turns(
        jnp.concatenate(
            [
                dot_rows(plane_out, plane_cot),
                dot_rows(plane_out, plane_cot_dot) + dot_rows(plane_probe_out, plane_cot),
            ],
            axis=0,
        ).astype(jnp.bfloat16)
    )
    back_total = sum(part.astype(jnp.float32) for part in back_parts)
    back, back_dot = back_total[:units], back_total[units:]
    grads = spread(
        jnp.concatenate(
            [slope * back, curve * pre_dot * back + slope * back_dot], axis=0
        ).astype(jnp.bfloat16),
        PLANE,
    )
    pre_grad = grads[:, :units].reshape(hidden_width, length)
    pre_grad_dot = grads[:, units:].reshape(hidden_width, length)

    normed = ((values - mean_val) * scale * ln_gain[:, None]).astype(jnp.bfloat16)
    probe_in = probe_signs(probe_seed[0], row_index, col_start, hidden_width)
    probe_out = probe_signs(probe_seed[1], row_index, col_start, hidden_width)
    grad_out = dot_cols(cotangent, all_hidden[0])
    hvp_out = dot_cols(cotangent_dot, all_hidden[0]) + dot_cols(cotangent, all_hidden[1])
    grad_in = dot_cols(normed, pre_grad)
    hvp_in = dot_cols(normed, pre_grad_dot)
    new_mom_in, new_hess_in, step_in = sophia_update(mom_in, hess_in, grad_in, hvp_in, probe_in)
    new_mom_out, new_hess_out, step_out = sophia_update(
        mom_out, hess_out, grad_out, hvp_out, probe_out
    )
    return (new_mom_in, new_hess_in, step_in, new_mom_out, new_hess_out, step_out)


def solution(mesh):
    torus = Mesh(mesh.devices.reshape(4, 4, 4, 2, 2), ("y", "x", "h", "l", "c"))
    matrix = P(DP, TENSOR)
    in_specs = (P(DP, None), P(DP), P()) + (matrix,) * 6 + (P(),)
    return jax.shard_map(
        body, mesh=torus, in_specs=in_specs, out_specs=(matrix,) * 6, check_vma=False
    )
```

time: 211 us -> 196 us (0.929)
  blocking collectives: 97.1 us -> 25.6 us
  waiting for transfers between devices: 51.4 us -> 77.3 us
  starting transfers between devices: 21.4 us -> 38.2 us
  between operations: 1.24 us -> 14.5 us
    all_to_all x4 -> x1, blocking collectives: 91.3 us -> 19.4 us  [swap(): return lax.all_to_all(blocks, axes, 0, 0, tiled=True)]
    ppermute x0 -> x6, starting transfers between devices: none -> 19 us  [turns(): lax.ppermute(block, DEPTH, [(at, (at + shift) % count) for at in range(co...]
    all_to_all x3 -> x4, waiting for transfers between devices: 51.4 us -> 65.5 us  [swap(): return lax.all_to_all(blocks, axes, 0, 0, tiled=True)]
    ppermute x0 -> x6, waiting for transfers between devices: none -> 11.7 us  [turns(): lax.ppermute(block, DEPTH, [(at, (at + shift) % count) for at in range(co...]
    reshape x0 -> x3, local copies, waits for them, and re-layouts: none -> 3.39 us  [the longest x1 2.11 us: body(): swap(column_blocks(w_out, planes), PLANE).reshape(plane_rows, units)]
    broadcast_in_dim x5 -> x2, local copies, waits for them, and re-layouts: 4.98 us -> 1.72 us  [spread(): return swap(jnp.broadcast_to(block[None], (count,) + block.shape), axes)]
    convert_element_type x3 -> x2, local copies, waits for them, and re-layouts: 2.78 us -> 0.51 us  [the longest x1 0.26 us: body(): dot_plain(plane_out, hidden).astype(jnp.bfloat16)]
    all_to_all x3 -> x4, starting transfers between devices: 21.4 us -> 19.2 us  [swap(): return lax.all_to_all(blocks, axes, 0, 0, tiled=True)]
  transfers between devices with their start and end apart: 3 -> 11, of which waited for: 3 -> 8; matrix products, arithmetic and copies ran while one was open for 4% -> 10% of each run, Pallas kernels for 0% -> 0%
where the time goes in v2:
time: 196 us; the launch traced here: 194 us
  waiting for transfers between devices  77.3 us (39%)
  starting transfers between devices  38.2 us (19%)
  blocking collectives  25.6 us (13%)
  matrix products  21.4 us (11%)
  between operations  14.5 us (7%)
  local copies, waits for them, and re-layouts  13.3 us (7%)
  other arithmetic  3.81 us (2%)
    all_to_all x4, waiting for transfers between devices, swap(): return lax.all_to_all(blocks, axes, 0, 0, tiled=True)  65.5 us
    all_to_all x1, blocking collectives, swap(): return lax.all_to_all(blocks, axes, 0, 0, tiled=True)  19.4 us
    all_to_all x4, starting transfers between devices, swap(): return lax.all_to_all(blocks, axes, 0, 0, tiled=True)  19.2 us
    ppermute x6, starting transfers between devices, turns(): lax.ppermute(block, DEPTH, [(at, (at + shift) % count) for at in range(co...  19 us
    ppermute x6, waiting for transfers between devices, turns(): lax.ppermute(block, DEPTH, [(at, (at + shift) % count) for at in range(co...  11.7 us
    dot_general x5, matrix products, dot_cols(): lax.dot_general(left, right, contract_cols, preferred_element_type=jnp.fl...  9.91 us
    dot_general x9, matrix products, dot_rows(): lax.dot_general(left, right, contract_rows, preferred_element_type=jnp.fl...  8.54 us
    all_gather x1, blocking collectives, body(): lax.all_gather(share, TENSOR).astype(jnp.float32)  6.2 us
  transfers between devices with their start and end apart: 11, of which 8 were waited for; matrix products, arithmetic and copies ran while one was open for 10% of the time, Pallas kernels for 0%

profile of v2, /device:TPU:32, one launch (start us, length us, event | category | flops | bytes accessed | tf_op | source)
XLA Modules:
  0.0 194.1 jit_solution(9198435135652409191)
XLA Ops:
  7.2 2.3 %copy.48 = bf16[112,3584]{0,1:T(8,128)(2,1)} copy(bf16[112,3584]{1,0:T(8,128)(2,1)} %param.14) | data formatting | bytes 1605632 | tf_op args[4]
  9.5 7.2 %all-to-all-start.1 = ((bf16[16,112,224]{1,2,0:T(8,128)(2,1)}), bf16[16,112,224]{1,2,0:T(8,128)(2,1)S(1)}, u32[]{:S(2)}, u32[]{:S(2)}) async-start(bf16[16,112,224]{1,2,0:T(8,128)(2,1)} %bitcast.21), calls=%async_computation.1 | async-start | bytes 1835008 | tf_op jit(solution)/shard_map/all_to_all | solution.py:69
  20.5 12.2 %all-to-all-done.1 = bf16[16,112,224]{1,2,0:T(8,128)(2,1)S(1)} async-done(((bf16[16,112,224]{1,2,0:T(8,128)(2,1)}), bf16[16,112,224]{1,2,0:T(8,128)(2,1)S(1)}, u32[]{:S(2)}, u32[]{:S(2)}) %all-to-all-start.1) | async-done | bytes 802848 | tf_op jit(solution)/shard_map/all_to_all | solution.py:69
  32.7 3.7 %all-to-all-start = ((bf16[16,112,384]{2,1,0:T(8,128)(2,1)}), bf16[16,112,384]{2,1,0:T(8,128)(2,1)S(1)}, u32[]{:S(2)}, u32[]{:S(2)}) async-start(bf16[16,112,384]{2,1,0:T(8,128)(2,1)} %copy.46), calls=%async_computation | async-start | bytes 2752512 | tf_op jit(solution)/shard_map/all_to_all | solution.py:69
  38.5 2.1 %reshape.226 = bf16[1792,224]{0,1:T(8,128)(2,1)S(1)} reshape(bf16[16,112,224]{1,0,2:T(8,128)(2,1)} %copy.49) | data formatting | bytes 1605632 | tf_op jit(solution)/shard_map/reshape | solution.py:140
  40.6 15.8 %all-to-all-done = bf16[16,112,384]{2,1,0:T(8,128)(2,1)S(1)} async-done(((bf16[16,112,384]{2,1,0:T(8,128)(2,1)}), bf16[16,112,384]{2,1,0:T(8,128)(2,1)S(1)}, u32[]{:S(2)}, u32[]{:S(2)}) %all-to-all-start) | async-done | bytes 1376288 | tf_op jit(solution)/shard_map/all_to_all | solution.py:69
  59.7 1.9 %convolution_convert_fusion.1 = bf16[224,128]{1,0:T(8,128)(2,1)S(1)} fusion(s32[]{:T(128)} %bitcast.5, s32[224]{0:T(256)S(1)} %iota_add_fusion.1, s32[1792]{0:T(1024)S(1)} %mul.259, f32[1792]{0:T(1024)S(1)} %convert_reduce_fusion.1, f32[128]{0:T(128)S(1)} %get-tuple-element.28, bf16[1792,384]{1,0:T(8,128)(2,1)S(1)} %bitcast.153), kind=kOutput, calls=%fused_computation.63 | convolution fusion | flops 110530560 | bytes 534020 | tf_op jit(solution)/shard_map/dot_general | solution.py:99
  62.5 6.4 %collective-permute-start.1 = (bf16[464,128]{1,0:T(8,128)(2,1)S(1)}, bf16[464,128]{1,0:T(8,128)(2,1)S(1)}, u32[]{:S(2)}, u32[]{:S(2)}) collective-permute-start(bf16[464,128]{1,0:T(8,128)(2,1)S(1)} %get-tuple-element.17), channel_id=1, source_target_pairs={{0,8},{4,12},{8,0},{12,4},{1,9},{5,13},{9,1},{13,5},{2,10},{6,14},... | collective-permute-start | bytes 356360 | tf_op jit(solution)/shard_map/ppermute | solution.py:80
  70.4 2.7 %collective-permute-start.2 = (bf16[464,128]{1,0:T(8,128)(2,1)S(1)}, bf16[464,128]{1,0:T(8,128)(2,1)S(1)}, u32[]{:S(2)}, u32[]{:S(2)}) collective-permute-start(bf16[464,128]{1,0:T(8,128)(2,1)S(1)} %get-tuple-element.17), channel_id=1, source_target_pairs={{0,12},{4,0},{8,4},{12,8},{1,13},{5,1},{9,5},{13,9},{2,14},{6,2},{... | collective-permute-start | bytes 356360 | tf_op jit(solution)/shard_map/ppermute | solution.py:80
  74.8 2.8 %collective-permute-done = bf16[464,128]{1,0:T(8,128)(2,1)S(1)} collective-permute-done((bf16[464,128]{1,0:T(8,128)(2,1)S(1)}, bf16[464,128]{1,0:T(8,128)(2,1)S(1)}, u32[]{:S(2)}, u32[]{:S(2)}) %collective-permute-start) | collective-permute-done | bytes 118816 | tf_op jit(solution)/shard_map/ppermute | solution.py:80
  79.7 2.1 %fusion.9 = bf16[1792,128]{0,1:T(8,128)(2,1)S(1)} fusion(f32[1792,128]{0,1:T(8,128)S(1)} %convolution_bitcast_fusion, bf16[224,128]{1,0:T(8,128)(2,1)S(1)} %get-tuple-element.20, s32[]{:T(128)} %bitcast.25, s32[224]{0:T(256)S(1)} %iota_add_fusion.1, s32[1792]{0:T(1024)S(1)} %mul.259), kind=kOutput, calls=%fused_computation.17 | convolution fusion | flops 110043136 | bytes 1441668 | tf_op jit(solution)/shard_map/dot_general | solution.py:107
  83.0 4.2 %all-to-all-start.2 = ((bf16[16,224,128]{2,1,0:T(8,128)(2,1)}), bf16[16,224,128]{2,1,0:T(8,128)(2,1)S(1)}, u32[]{:S(2)}, u32[]{:S(2)}) async-start(bf16[16,224,128]{2,1,0:T(8,128)(2,1)} %pad_maximum_fusion.1), calls=%async_computation.2 | async-start | bytes 1835008 | tf_op jit(solution)/shard_map/all_to_all | solution.py:69
  88.4 14.6 %all-to-all-done.2 = bf16[16,224,128]{2,1,0:T(8,128)(2,1)S(1)} async-done(((bf16[16,224,128]{2,1,0:T(8,128)(2,1)}), bf16[16,224,128]{2,1,0:T(8,128)(2,1)S(1)}, u32[]{:S(2)}, u32[]{:S(2)}) %all-to-all-start.2) | async-done | bytes 917536 | tf_op jit(solution)/shard_map/all_to_all | solution.py:69
  103.1 6.2 %all_gather.9 = bf16[4,2,112,128]{3,2,1,0:T(8,128)(2,1)S(1)} all-gather(bf16[1,2,112,128]{3,2,1,0:T(8,128)(2,1)S(1)} %bitcast.163), channel_id=1, replica_groups=mesh['y'=4,'x'=4,'h'=4,'l'=2,'c'=2] {'l','c'}, dimensions={0}, use_global_device_ids=true | all-gather | bytes 286720 | tf_op jit(solution)/shard_map/all_gather | solution.py:206
  109.5 19.4 %all_to_all.25 = bf16[16,224,128]{2,1,0:T(8,128)(2,1)S(1)} all-to-all(bf16[16,224,128]{2,1,0:T(8,128)(2,1)S(1)} %broadcast_in_dim.10), channel_id=1, replica_groups=mesh['y'=4,'x'=4,'h'=4,'l'=2,'c'=2] {'y','x'}, dimensions={0} | all-to-all | bytes 1835008 | tf_op jit(solution)/shard_map/all_to_all | solution.py:69
  131.6 4.4 %collective-permute-start.4 = (bf16[448,128]{1,0:T(8,128)(2,1)S(1)}, bf16[448,128]{1,0:T(8,128)(2,1)S(1)}, u32[]{:S(2)}, u32[]{:S(2)}) collective-permute-start(bf16[448,128]{1,0:T(8,128)(2,1)S(1)} %pad_maximum_fusion.2), channel_id=1, source_target_pairs={{0,8},{4,12},{8,0},{12,4},{1,9},{5,13},{9,1},{13,5},{2,10},{6,14},... | collective-permute-start | bytes 344072 | tf_op jit(solution)/shard_map/ppermute | solution.py:80
  137.4 2.7 %collective-permute-start.5 = (bf16[448,128]{1,0:T(8,128)(2,1)S(1)}, bf16[448,128]{1,0:T(8,128)(2,1)S(1)}, u32[]{:S(2)}, u32[]{:S(2)}) collective-permute-start(bf16[448,128]{1,0:T(8,128)(2,1)S(1)} %pad_maximum_fusion.2), channel_id=1, source_target_pairs={{0,12},{4,0},{8,4},{12,8},{1,13},{5,1},{9,5},{13,9},{2,14},{6,2},{... | collective-permute-start | bytes 344072 | tf_op jit(solution)/shard_map/ppermute | solution.py:80
  140.2 3.1 %collective-permute-done.4 = bf16[448,128]{1,0:T(8,128)(2,1)S(1)} collective-permute-done((bf16[448,128]{1,0:T(8,128)(2,1)S(1)}, bf16[448,128]{1,0:T(8,128)(2,1)S(1)}, u32[]{:S(2)}, u32[]{:S(2)}) %collective-permute-start.4) | collective-permute-done | bytes 114720 | tf_op jit(solution)/shard_map/ppermute | solution.py:80
  143.3 4.0 %collective-permute-done.3 = bf16[448,128]{1,0:T(8,128)(2,1)S(1)} collective-permute-done((bf16[448,128]{1,0:T(8,128)(2,1)S(1)}, bf16[448,128]{1,0:T(8,128)(2,1)S(1)}, u32[]{:S(2)}, u32[]{:S(2)}) %collective-permute-start.3) | collective-permute-done | bytes 114720 | tf_op jit(solution)/shard_map/ppermute | solution.py:80
  149.1 4.1 %all-to-all-start.4 = ((bf16[16,448,128]{2,1,0:T(8,128)(2,1)}), bf16[16,448,128]{2,1,0:T(8,128)(2,1)S(1)}, u32[]{:S(2)}, u32[]{:S(2)}) async-start(bf16[16,448,128]{2,1,0:T(8,128)(2,1)} %broadcast_in_dim.11), calls=%async_computation.4 | async-start | bytes 3670016 | tf_op jit(solution)/shard_map/all_to_all | solution.py:69
  155.0 1.9 fusion.1
  157.0 2.2 %clamp_convert_fusion = (bf16[112,3584]{1,0:T(8,128)(2,1)}, bf16[112,3584]{1,0:T(8,128)(2,1)}, bf16[112,3584]{1,0:T(8,128)(2,1)}) fusion(f32[112,3584]{1,0:T(8,128)S(1)} %fusion.1, bf16[112,128]{1,0:T(8,128)(2,1)S(1)} %get-tuple-element.18, bf16[2,3584,128]{2,1,0:T(8,128)(2,1)S(1)} %copy-done.1, bf16[112,3584]{1,0:T(8,128)(2,1)S(1)} %copy-done.6), kind=kOutput, calls=%fused_computation.52 | convolution fusion | flops 107175936 | bytes 5763072 | tf_op jit(solution)/shard_map/dot_general | solution.py:103
  159.2 22.9 %all-to-all-done.4 = bf16[16,448,128]{2,1,0:T(8,128)(2,1)S(1)} async-done(((bf16[16,448,128]{2,1,0:T(8,128)(2,1)}), bf16[16,448,128]{2,1,0:T(8,128)(2,1)S(1)}, u32[]{:S(2)}, u32[]{:S(2)}) %all-to-all-start.4) | async-done | bytes 1835040 | tf_op jit(solution)/shard_map/all_to_all | solution.py:69
  185.1 2.2 %clamp_convert_fusion.1 = (bf16[112,3584]{1,0:T(8,128)(2,1)}, bf16[112,3584]{1,0:T(8,128)(2,1)}, bf16[112,3584]{1,0:T(8,128)(2,1)}) fusion(f32[112,3584]{1,0:T(8,128)S(1)} %fusion.3, bf16[3584,128]{1,0:T(8,128)(2,1)S(1)} %bitcast.158, f32[112]{0:T(128)S(1)} %copy-done.4, f32[128]{0:T(128)S(1)} %add_rsqrt_fusion, f32[128]{0:T(128)S(1)} %broadcast_multiply_fusion, ...), kind=kOutput, calls=%fused_computation.54 | convolution fusion | flops 107247616 | bytes 5764544 | tf_op jit(solution)/shard_map/dot_general | solution.py:103
  (105 shorter events, 28.5 us)
Async XLA Ops:
  7.2 9.5 %copy-start.4 = (f32[112]{0:T(128)S(1)}, f32[112]{0:T(128)}, u32[]{:S(2)}) copy-start(f32[112]{0:T(128)} %param.11) | copy-start | bytes 1348
  7.2 9.9 %copy-start = (bf16[112,3584]{1,0:T(8,128)(2,1)S(1)}, bf16[112,3584]{1,0:T(8,128)(2,1)}, u32[]{:S(2)}) copy-start(bf16[112,3584]{1,0:T(8,128)(2,1)} %param.13) | copy-start | bytes 2408452
  9.5 8.9 %copy-start.2 = (bf16[112,128]{1,0:T(8,128)(2,1)S(1)}, bf16[112,128]{1,0:T(8,128)(2,1)}, u32[]{:S(2)}) copy-start(bf16[112,128]{1,0:T(8,128)(2,1)} %param.10) | copy-start | bytes 86020
  9.5 23.2 %all-to-all-start.1 = ((bf16[16,112,224]{1,2,0:T(8,128)(2,1)}), bf16[16,112,224]{1,2,0:T(8,128)(2,1)S(1)}, u32[]{:S(2)}, u32[]{:S(2)}) async-start(bf16[16,112,224]{1,2,0:T(8,128)(2,1)} %bitcast.21), calls=%async_computation.1 | async-start | bytes 1835008 | tf_op jit(solution)/shard_map/all_to_all | solution.py:69
  20.5 16.1 %copy-start.3 = (s32[2]{0:T(128)S(1)}, s32[2]{0:T(128)}, u32[]{:S(2)}) copy-start(s32[2]{0:T(128)} %param.19) | copy-start | bytes 28
  32.7 23.7 %all-to-all-start = ((bf16[16,112,384]{2,1,0:T(8,128)(2,1)}), bf16[16,112,384]{2,1,0:T(8,128)(2,1)S(1)}, u32[]{:S(2)}, u32[]{:S(2)}) async-start(bf16[16,112,384]{2,1,0:T(8,128)(2,1)} %copy.46), calls=%async_computation | async-start | bytes 2752512 | tf_op jit(solution)/shard_map/all_to_all | solution.py:69
  62.5 12.3 %collective-permute-start.1 = (bf16[464,128]{1,0:T(8,128)(2,1)S(1)}, bf16[464,128]{1,0:T(8,128)(2,1)S(1)}, u32[]{:S(2)}, u32[]{:S(2)}) collective-permute-start(bf16[464,128]{1,0:T(8,128)(2,1)S(1)} %get-tuple-element.17), channel_id=1, source_target_pairs={{0,8},{4,12},{8,0},{12,4},{1,9},{5,13},{9,1},{13,5},{2,10},{6,14},... | collective-permute-start | bytes 356360 | tf_op jit(solution)/shard_map/ppermute | solution.py:80
  68.9 8.7 %collective-permute-start = (bf16[464,128]{1,0:T(8,128)(2,1)S(1)}, bf16[464,128]{1,0:T(8,128)(2,1)S(1)}, u32[]{:S(2)}, u32[]{:S(2)}) collective-permute-start(bf16[464,128]{1,0:T(8,128)(2,1)S(1)} %get-tuple-element.17), channel_id=1, source_target_pairs={{0,4},{4,8},{8,12},{12,0},{1,5},{5,9},{9,13},{13,1},{2,6},{6,10},{... | collective-permute-start | bytes 356360 | tf_op jit(solution)/shard_map/ppermute | solution.py:80
  70.4 7.3 %collective-permute-start.2 = (bf16[464,128]{1,0:T(8,128)(2,1)S(1)}, bf16[464,128]{1,0:T(8,128)(2,1)S(1)}, u32[]{:S(2)}, u32[]{:S(2)}) collective-permute-start(bf16[464,128]{1,0:T(8,128)(2,1)S(1)} %get-tuple-element.17), channel_id=1, source_target_pairs={{0,12},{4,0},{8,4},{12,8},{1,13},{5,1},{9,5},{13,9},{2,14},{6,2},{... | collective-permute-start | bytes 356360 | tf_op jit(solution)/shard_map/ppermute | solution.py:80
  82.0 5.4 %copy-start.9 = (s32[128]{0:T(128)S(1)}, s32[128]{0:T(128)}, u32[]{:S(2)}) copy-start(s32[128]{0:T(128)} %param.12) | copy-start | bytes 1540
  83.0 19.9 %all-to-all-start.2 = ((bf16[16,224,128]{2,1,0:T(8,128)(2,1)}), bf16[16,224,128]{2,1,0:T(8,128)(2,1)S(1)}, u32[]{:S(2)}, u32[]{:S(2)}) async-start(bf16[16,224,128]{2,1,0:T(8,128)(2,1)} %pad_maximum_fusion.1), calls=%async_computation.2 | async-start | bytes 1835008 | tf_op jit(solution)/shard_map/all_to_all | solution.py:69
  87.2 66.0 %all-gather.3.cloned.1.call-start = ((), (), s32[]{:S(2)}) async-start(), calls=%async_computation.5 | async-start | bytes 1949696 | tf_op jit(solution)/shard_map/all_gather | solution.py:192
  131.6 11.7 %collective-permute-start.4 = (bf16[448,128]{1,0:T(8,128)(2,1)S(1)}, bf16[448,128]{1,0:T(8,128)(2,1)S(1)}, u32[]{:S(2)}, u32[]{:S(2)}) collective-permute-start(bf16[448,128]{1,0:T(8,128)(2,1)S(1)} %pad_maximum_fusion.2), channel_id=1, source_target_pairs={{0,8},{4,12},{8,0},{12,4},{1,9},{5,13},{9,1},{13,5},{2,10},{6,14},... | collective-permute-start | bytes 344072 | tf_op jit(solution)/shard_map/ppermute | solution.py:80
  136.0 11.3 %collective-permute-start.3 = (bf16[448,128]{1,0:T(8,128)(2,1)S(1)}, bf16[448,128]{1,0:T(8,128)(2,1)S(1)}, u32[]{:S(2)}, u32[]{:S(2)}) collective-permute-start(bf16[448,128]{1,0:T(8,128)(2,1)S(1)} %pad_maximum_fusion.2), channel_id=1, source_target_pairs={{0,4},{4,8},{8,12},{12,0},{1,5},{5,9},{9,13},{13,1},{2,6},{6,10},{... | collective-permute-start | bytes 344072 | tf_op jit(solution)/shard_map/ppermute | solution.py:80
  137.4 9.9 %collective-permute-start.5 = (bf16[448,128]{1,0:T(8,128)(2,1)S(1)}, bf16[448,128]{1,0:T(8,128)(2,1)S(1)}, u32[]{:S(2)}, u32[]{:S(2)}) collective-permute-start(bf16[448,128]{1,0:T(8,128)(2,1)S(1)} %pad_maximum_fusion.2), channel_id=1, source_target_pairs={{0,12},{4,0},{8,4},{12,8},{1,13},{5,1},{9,5},{13,9},{2,14},{6,2},{... | collective-permute-start | bytes 344072 | tf_op jit(solution)/shard_map/ppermute | solution.py:80
  149.1 5.9 %copy-start.5 = (bf16[112,3584]{1,0:T(8,128)(2,1)S(1)}, bf16[112,3584]{1,0:T(8,128)(2,1)}, u32[]{:S(2)}) copy-start(bf16[112,3584]{1,0:T(8,128)(2,1)} %param.18) | copy-start | bytes 2408452
  149.1 32.9 %all-to-all-start.4 = ((bf16[16,448,128]{2,1,0:T(8,128)(2,1)}), bf16[16,448,128]{2,1,0:T(8,128)(2,1)S(1)}, u32[]{:S(2)}, u32[]{:S(2)}) async-start(bf16[16,448,128]{2,1,0:T(8,128)(2,1)} %broadcast_in_dim.11), calls=%async_computation.4 | async-start | bytes 3670016 | tf_op jit(solution)/shard_map/all_to_all | solution.py:69
  153.3 1.8 copy-start.1
  155.0 2.0 %copy-start.6 = (bf16[112,3584]{1,0:T(8,128)(2,1)S(1)}, bf16[112,3584]{1,0:T(8,128)(2,1)}, u32[]{:S(2)}) copy-start(bf16[112,3584]{1,0:T(8,128)(2,1)} %param.16) | copy-start | bytes 2408452
  182.0 1.1 copy-start.7
  183.1 1.9 copy-start.8
Sparse Core Ops, SparseCore 0:
  91.1 55.1 all-gather.2

commit v3 on v2

--- a/solution.py
+++ b/solution.py
@@ -132,12 +132,14 @@
     sent = jnp.concatenate(
         [column_blocks(w_in, planes), jnp.broadcast_to(side[None], (planes,) + side.shape)], axis=2
     )
-    got = swap(sent, PLANE).reshape(plane_rows, padded + length)
+    got = swap(sent, PLANE)
+    out_blocks, got = lax.optimization_barrier((column_blocks(w_out, planes), got))
+    plane_out = swap(out_blocks, PLANE).reshape(plane_rows, units)
+    got = got.reshape(plane_rows, padded + length)
     plane_in = got[:, :units]
     gain_cols = got[:, units : units + 3]
     plane_gain = jnp.sum(gain_cols.astype(jnp.float32), axis=1, keepdims=True)
     plane_values = got[:, padded:].astype(jnp.float32)
-    plane_out = swap(column_blocks(w_out, planes), PLANE).reshape(plane_rows, units)
     plane_probe_in = probe_signs(probe_seed[0], plane_index, unit_start, units)
     plane_probe_out = probe_signs(probe_seed[1], plane_index, unit_start, units)
 
@@ -168,6 +170,7 @@
             axis=0,
         )
     )
+    every, plane_out = lax.optimization_barrier((every, plane_out))
     every = [part.astype(jnp.float32) for part in every]
     tails = jnp.stack([part[2 * units : 2 * units + extra_rows] for part in every])
     sums = tails[:, : 2 * padded // length].reshape(deep, 2, padded)[:, :, :units]
@@ -187,22 +190,18 @@
     )
 
     act, slope, curve = gelu_parts(pre)
-    hidden = act.astype(jnp.bfloat16)
-    hidden_dot = (slope * pre_dot).astype(jnp.bfloat16)
-    all_hidden = lax.all_gather(jnp.stack([hidden, hidden_dot]), PLANE, axis=1)
-    all_hidden = all_hidden.reshape(2, hidden_width, length)
-
-    parts = jnp.concatenate(
+    both = spread(jnp.concatenate([act, slope * pre_dot], axis=0).astype(jnp.bfloat16), PLANE)
+    hidden = both[:, :units].reshape(hidden_width, length)
+    hidden_dot = both[:, units:].reshape(hidden_width, length)
+
+    probe_in = probe_signs(probe_seed[0], row_index, col_start, hidden_width)
+    probe_out = probe_signs(probe_seed[1], row_index, col_start, hidden_width)
+    share = jnp.stack(
         [
-            dot_plain(plane_out, hidden).astype(jnp.bfloat16).reshape(planes, features, length),
-            (dot_plain(plane_out, hidden_dot) + dot_plain(plane_probe_out, hidden))
-            .astype(jnp.bfloat16)
-            .reshape(planes, features, length),
-        ],
-        axis=1,
-    )
-    share = jnp.sum(swap(parts, PLANE).astype(jnp.float32), axis=0).astype(jnp.bfloat16)
-    share = share.reshape(2, features, length)
+            dot_plain(w_out, hidden),
+            dot_plain(w_out, hidden_dot) + dot_plain(probe_out, hidden),
+        ]
+    ).astype(jnp.bfloat16)
     output, output_dot = jnp.sum(lax.all_gather(share, TENSOR).astype(jnp.float32), axis=0)
     target = jnp.concatenate([values[:, 1:], jnp.zeros((features, 1), jnp.float32)], axis=1)
     weights = token_weights(segment_ids)
@@ -233,10 +232,8 @@
     pre_grad_dot = grads[:, units:].reshape(hidden_width, length)
 
     normed = ((values - mean_val) * scale * ln_gain[:, None]).astype(jnp.bfloat16)
-    probe_in = probe_signs(probe_seed[0], row_index, col_start, hidden_width)
-    probe_out = probe_signs(probe_seed[1], row_index, col_start, hidden_width)
-    grad_out = dot_cols(cotangent, all_hidden[0])
-    hvp_out = dot_cols(cotangent_dot, all_hidden[0]) + dot_cols(cotangent, all_hidden[1])
+    grad_out = dot_cols(cotangent, hidden)
+    hvp_out = dot_cols(cotangent_dot, hidden) + dot_cols(cotangent, hidden_dot)
     grad_in = dot_cols(normed, pre_grad)
     hvp_in = dot_cols(normed, pre_grad_dot)
     new_mom_in, new_hess_in, step_in = sophia_update(mom_in, hess_in, grad_in, hvp_in, probe_in)

time: 196 us -> 187 us (0.954)
  between operations: 14.5 us -> 1.38 us
  starting transfers between devices: 38.2 us -> 41.2 us
    all_to_all x4, starting transfers between devices: 19.2 us -> 22 us  [swap(): return lax.all_to_all(blocks, axes, 0, 0, tiled=True)]
  transfers between devices with their start and end apart: 11 -> 10, of which waited for: 8 -> 8; matrix products, arithmetic and copies ran while one was open for 10% -> 9% of each run, Pallas kernels for 0% -> 0%
where the time goes in v3:
time: 187 us; the launch traced here: 183 us
  waiting for transfers between devices  76.5 us (41%)
  starting transfers between devices  41.2 us (22%)
  blocking collectives  24.8 us (13%)
  matrix products  20.7 us (11%)
  local copies, waits for them, and re-layouts  14.8 us (8%)
  other arithmetic  3.81 us (2%)
    all_to_all x4, waiting for transfers between devices, swap(): return lax.all_to_all(blocks, axes, 0, 0, tiled=True)  66.6 us
    all_to_all x4, starting transfers between devices, swap(): return lax.all_to_all(blocks, axes, 0, 0, tiled=True)  22 us
    ppermute x6, starting transfers between devices, turns(): lax.ppermute(block, DEPTH, [(at, (at + shift) % count) for at in range(co...  19.2 us
    all_to_all x1, blocking collectives, swap(): return lax.all_to_all(blocks, axes, 0, 0, tiled=True)  19.1 us
    ppermute x6, waiting for transfers between devices, turns(): lax.ppermute(block, DEPTH, [(at, (at + shift) % count) for at in range(co...  9.91 us
    dot_general x9, matrix products, dot_rows(): lax.dot_general(left, right, contract_rows, preferred_element_type=jnp.fl...  8.95 us
    dot_general x5, matrix products, dot_cols(): lax.dot_general(left, right, contract_cols, preferred_element_type=jnp.fl...  8.55 us
    all_gather x1, blocking collectives, body(): lax.all_gather(share, TENSOR).astype(jnp.float32)  5.7 us
  transfers between devices with their start and end apart: 10, of which 8 were waited for; matrix products, arithmetic and copies ran while one was open for 9% of the time, Pallas kernels for 0%

profile of v3, /device:TPU:32, one launch (start us, length us, event | category | flops | bytes accessed | tf_op | source)
XLA Modules:
  0.0 183.3 jit_solution(9601371213553699896)
XLA Ops:
  1.8 2.4 %reshape.267 = bf16[112,16,224]{2,1,0:T(8,128)(2,1)S(1)} reshape(bf16[112,3584]{1,0:T(8,128)(2,1)} %param.13) | data formatting | bytes 1605632 | tf_op jit(solution)/shard_map/reshape | solution.py:95
  6.4 7.2 %all-to-all-start = ((bf16[16,112,384]{2,1,0:T(8,128)(2,1)}), bf16[16,112,384]{2,1,0:T(8,128)(2,1)S(1)}, u32[]{:S(2)}, u32[]{:S(2)}) async-start(bf16[16,112,384]{2,1,0:T(8,128)(2,1)} %copy.37), calls=%async_computation | async-start | bytes 2752512 | tf_op jit(solution)/shard_map/all_to_all | solution.py:69
  15.7 19.6 %all-to-all-done = bf16[16,112,384]{2,1,0:T(8,128)(2,1)S(1)} async-done(((bf16[16,112,384]{2,1,0:T(8,128)(2,1)}), bf16[16,112,384]{2,1,0:T(8,128)(2,1)S(1)}, u32[]{:S(2)}, u32[]{:S(2)}) %all-to-all-start) | async-done | bytes 1376288 | tf_op jit(solution)/shard_map/all_to_all | solution.py:69
  36.8 3.6 %all-to-all-start.1 = ((bf16[16,112,224]{1,2,0:T(8,128)(2,1)}), bf16[16,112,224]{1,2,0:T(8,128)(2,1)S(1)}, u32[]{:S(2)}, u32[]{:S(2)}) async-start(bf16[16,112,224]{1,2,0:T(8,128)(2,1)} %bitcast.151), calls=%async_computation.1 | async-start | bytes 1835008 | tf_op jit(solution)/shard_map/all_to_all | solution.py:69
  43.0 1.8 %convolution_convert_fusion = bf16[224,128]{1,0:T(8,128)(2,1)S(1)} fusion(s32[]{:T(128)} %bitcast.7, s32[224]{0:T(256)S(1)} %iota_add_fusion.1, s32[1792]{0:T(1024)S(1)} %mul.259, f32[1792]{0:T(1024)S(1)} %convert_reduce_fusion.1, f32[128]{0:T(128)S(1)} %get-tuple-element.44, bf16[1792,384]{1,0:T(8,128)(2,1)S(1)} %bitcast.144), kind=kOutput, calls=%fused_computation.60 | convolution fusion | flops 110530560 | bytes 534020 | tf_op jit(solution)/shard_map/dot_general | solution.py:99
  44.9 5.5 %collective-permute-start.2 = (bf16[464,128]{1,0:T(8,128)(2,1)S(1)}, bf16[464,128]{1,0:T(8,128)(2,1)S(1)}, u32[]{:S(2)}, u32[]{:S(2)}) collective-permute-start(bf16[464,128]{1,0:T(8,128)(2,1)S(1)} %fusion.57), channel_id=1, source_target_pairs={{0,12},{4,0},{8,4},{12,8},{1,13},{5,1},{9,5},{13,9},{2,14},{6,2},{... | collective-permute-start | bytes 356360 | tf_op jit(solution)/shard_map/ppermute | solution.py:80
  51.8 2.4 %collective-permute-start = (bf16[464,128]{1,0:T(8,128)(2,1)S(1)}, bf16[464,128]{1,0:T(8,128)(2,1)S(1)}, u32[]{:S(2)}, u32[]{:S(2)}) collective-permute-start(bf16[464,128]{1,0:T(8,128)(2,1)S(1)} %fusion.57), channel_id=1, source_target_pairs={{0,4},{4,8},{8,12},{12,0},{1,5},{5,9},{9,13},{13,1},{2,6},{6,10},{... | collective-permute-start | bytes 356360 | tf_op jit(solution)/shard_map/ppermute | solution.py:80
  54.1 2.0 %all-to-all-done.1 = bf16[16,112,224]{1,2,0:T(8,128)(2,1)S(1)} async-done(((bf16[16,112,224]{1,2,0:T(8,128)(2,1)}), bf16[16,112,224]{1,2,0:T(8,128)(2,1)S(1)}, u32[]{:S(2)}, u32[]{:S(2)}) %all-to-all-start.1) | async-done | bytes 802848 | tf_op jit(solution)/shard_map/all_to_all | solution.py:69
  56.5 2.0 %reshape.269 = bf16[1792,224]{0,1:T(8,128)(2,1)} reshape(bf16[16,112,224]{1,0,2:T(8,128)(2,1)S(1)} %copy.38) | data formatting | bytes 1605632 | tf_op jit(solution)/shard_map/reshape | solution.py:137
  58.5 3.4 %collective-permute-done.1 = bf16[464,128]{1,0:T(8,128)(2,1)S(1)} collective-permute-done((bf16[464,128]{1,0:T(8,128)(2,1)S(1)}, bf16[464,128]{1,0:T(8,128)(2,1)S(1)}, u32[]{:S(2)}, u32[]{:S(2)}) %collective-permute-start.1) | collective-permute-done | bytes 118816 | tf_op jit(solution)/shard_map/ppermute | solution.py:80
  66.3 7.1 %all-to-all-start.2 = ((bf16[16,448,128]{2,1,0:T(8,128)(2,1)}), bf16[16,448,128]{2,1,0:T(8,128)(2,1)S(1)}, u32[]{:S(2)}, u32[]{:S(2)}) async-start(bf16[16,448,128]{2,1,0:T(8,128)(2,1)} %broadcast_in_dim.12), calls=%async_computation.2 | async-start | bytes 3670016 | tf_op jit(solution)/shard_map/all_to_all | solution.py:69
  76.2 23.0 %all-to-all-done.2 = bf16[16,448,128]{2,1,0:T(8,128)(2,1)S(1)} async-done(((bf16[16,448,128]{2,1,0:T(8,128)(2,1)}), bf16[16,448,128]{2,1,0:T(8,128)(2,1)S(1)}, u32[]{:S(2)}, u32[]{:S(2)}) %all-to-all-start.2) | async-done | bytes 1835040 | tf_op jit(solution)/shard_map/all_to_all | solution.py:69
  102.1 5.7 %all_gather.4 = bf16[4,2,112,128]{3,2,1,0:T(8,128)(2,1)S(1)} all-gather(bf16[1,2,112,128]{3,2,1,0:T(8,128)(2,1)S(1)} %pad_maximum_fusion.4), channel_id=1, replica_groups=mesh['y'=4,'x'=4,'h'=4,'l'=2,'c'=2] {'l','c'}, dimensions={0}, use_global_device_ids=true | all-gather | bytes 286720 | tf_op jit(solution)/shard_map/all_gather | solution.py:205
  108.1 19.1 %all_to_all.25 = bf16[16,224,128]{2,1,0:T(8,128)(2,1)S(1)} all-to-all(bf16[16,224,128]{2,1,0:T(8,128)(2,1)S(1)} %broadcast_in_dim.13), channel_id=1, replica_groups=mesh['y'=4,'x'=4,'h'=4,'l'=2,'c'=2] {'y','x'}, dimensions={0} | all-to-all | bytes 1835008 | tf_op jit(solution)/shard_map/all_to_all | solution.py:69
  127.3 1.9 %fusion.50 = f32[224,128]{1,0:T(8,128)S(1)} fusion(bf16[1792,128]{1,0:T(8,128)(2,1)S(1)} %bitcast.153, s32[]{:T(128)} %bitcast.27, s32[224]{0:T(256)S(1)} %copy-done.33, s32[1792]{0:T(1024)S(1)} %copy-done.18), kind=kOutput, calls=%fused_computation.78 | convolution fusion | flops 109584384 | bytes 581508 | tf_op jit(solution)/shard_map/dot_general | solution.py:99
  130.1 5.8 %collective-permute-start.4 = (bf16[448,128]{1,0:T(8,128)(2,1)S(1)}, bf16[448,128]{1,0:T(8,128)(2,1)S(1)}, u32[]{:S(2)}, u32[]{:S(2)}) collective-permute-start(bf16[448,128]{1,0:T(8,128)(2,1)S(1)} %pad_maximum_fusion.2), channel_id=1, source_target_pairs={{0,8},{4,12},{8,0},{12,4},{1,9},{5,13},{9,1},{13,5},{2,10},{6,14},... | collective-permute-start | bytes 344072 | tf_op jit(solution)/shard_map/ppermute | solution.py:80
  135.9 2.0 %collective-permute-start.3 = (bf16[448,128]{1,0:T(8,128)(2,1)S(1)}, bf16[448,128]{1,0:T(8,128)(2,1)S(1)}, u32[]{:S(2)}, u32[]{:S(2)}) collective-permute-start(bf16[448,128]{1,0:T(8,128)(2,1)S(1)} %pad_maximum_fusion.2), channel_id=1, source_target_pairs={{0,4},{4,8},{8,12},{12,0},{1,5},{5,9},{9,13},{13,1},{2,6},{6,10},{... | collective-permute-start | bytes 344072 | tf_op jit(solution)/shard_map/ppermute | solution.py:80
  137.9 2.2 %collective-permute-start.5 = (bf16[448,128]{1,0:T(8,128)(2,1)S(1)}, bf16[448,128]{1,0:T(8,128)(2,1)S(1)}, u32[]{:S(2)}, u32[]{:S(2)}) collective-permute-start(bf16[448,128]{1,0:T(8,128)(2,1)S(1)} %pad_maximum_fusion.2), channel_id=1, source_target_pairs={{0,12},{4,0},{8,4},{12,8},{1,13},{5,1},{9,5},{13,9},{2,14},{6,2},{... | collective-permute-start | bytes 344072 | tf_op jit(solution)/shard_map/ppermute | solution.py:80
  140.3 5.2 %collective-permute-done.3 = bf16[448,128]{1,0:T(8,128)(2,1)S(1)} collective-permute-done((bf16[448,128]{1,0:T(8,128)(2,1)S(1)}, bf16[448,128]{1,0:T(8,128)(2,1)S(1)}, u32[]{:S(2)}, u32[]{:S(2)}) %collective-permute-start.3) | collective-permute-done | bytes 114720 | tf_op jit(solution)/shard_map/ppermute | solution.py:80
  147.4 4.1 %all-to-all-start.4 = ((bf16[16,448,128]{2,1,0:T(8,128)(2,1)}), bf16[16,448,128]{2,1,0:T(8,128)(2,1)S(1)}, u32[]{:S(2)}, u32[]{:S(2)}) async-start(bf16[16,448,128]{2,1,0:T(8,128)(2,1)} %broadcast_in_dim.14), calls=%async_computation.4 | async-start | bytes 3670016 | tf_op jit(solution)/shard_map/all_to_all | solution.py:69
  152.9 2.0 %fusion.1 = f32[112,3584]{1,0:T(8,128)S(1)} fusion(f32[112,3584]{1,0:T(8,128)S(1)} %fusion.77, bf16[112,128]{1,0:T(8,128)(2,1)S(1)} %copy-done.13, bf16[3584,128]{1,0:T(8,128)(2,1)S(1)} %bitcast.150, bf16[112,3584]{1,0:T(8,128)(2,1)S(1)} %copy-done.27, s32[]{:T(128)} %bitcast.27, s32[3584]{0:T(1024)S(1)} %copy-done.16, s32[112]{0:T(128)S(1)} %copy-done.35), kind=kOutput, calls=%fused_computation.2 | convolution fusion | flops 112394240 | bytes 4975044 | tf_op jit(solution)/shard_map/dot_general | solution.py:103
  154.9 2.2 %clamp_convert_fusion = (bf16[112,3584]{1,0:T(8,128)(2,1)}, bf16[112,3584]{1,0:T(8,128)(2,1)}, bf16[112,3584]{1,0:T(8,128)(2,1)}) fusion(f32[112,3584]{1,0:T(8,128)S(1)} %fusion.1, bf16[112,128]{1,0:T(8,128)(2,1)S(1)} %copy-done.13, bf16[3584,128]{1,0:T(8,128)(2,1)S(1)} %bitcast.148, bf16[112,3584]{1,0:T(8,128)(2,1)S(1)} %copy-done.28), kind=kOutput, calls=%fused_computation.47 | convolution fusion | flops 107175936 | bytes 5763072 | tf_op jit(solution)/shard_map/dot_general | solution.py:103
  157.1 22.0 %all-to-all-done.4 = bf16[16,448,128]{2,1,0:T(8,128)(2,1)S(1)} async-done(((bf16[16,448,128]{2,1,0:T(8,128)(2,1)}), bf16[16,448,128]{2,1,0:T(8,128)(2,1)S(1)}, u32[]{:S(2)}, u32[]{:S(2)}) %all-to-all-start.4) | async-done | bytes 1835040 | tf_op jit(solution)/shard_map/all_to_all | solution.py:69
  181.1 2.2 %clamp_convert_fusion.1 = (bf16[112,3584]{1,0:T(8,128)(2,1)}, bf16[112,3584]{1,0:T(8,128)(2,1)}, bf16[112,3584]{1,0:T(8,128)(2,1)}) fusion(f32[112,3584]{1,0:T(8,128)S(1)} %fusion.3, bf16[3584,128]{1,0:T(8,128)(2,1)S(1)} %bitcast.156, f32[112]{0:T(128)S(1)} %copy-done.24, f32[128]{0:T(128)S(1)} %copy-done.26, f32[128]{0:T(128)S(1)} %copy-done.21, ...), kind=kOutput, calls=%fused_computation.48 | convolution fusion | flops 107247616 | bytes 5764544 | tf_op jit(solution)/shard_map/dot_general | solution.py:103
  (154 shorter events, 27.5 us)
Async XLA Ops:
  6.4 8.7 %copy-start.19 = (s32[2]{0:T(128)S(1)}, s32[2]{0:T(128)}, u32[]{:S(2)}) copy-start(s32[2]{0:T(128)} %param.19) | copy-start | bytes 28
  6.4 28.9 %all-to-all-start = ((bf16[16,112,384]{2,1,0:T(8,128)(2,1)}), bf16[16,112,384]{2,1,0:T(8,128)(2,1)S(1)}, u32[]{:S(2)}, u32[]{:S(2)}) async-start(bf16[16,112,384]{2,1,0:T(8,128)(2,1)} %copy.37), calls=%async_computation | async-start | bytes 2752512 | tf_op jit(solution)/shard_map/all_to_all | solution.py:69
  13.7 29.2 %copy-start.17 = (s32[1792]{0:T(1024)}, s32[1792]{0:T(1024)S(1)}, u32[]{:S(2)}) copy-start(s32[1792]{0:T(1024)S(1)} %mul.259) | copy-start | bytes 21508
  15.1 27.9 %copy-start.32 = (s32[224]{0:T(256)}, s32[224]{0:T(256)S(1)}, u32[]{:S(2)}) copy-start(s32[224]{0:T(256)S(1)} %iota_add_fusion.1) | copy-start | bytes 2692
  36.8 19.4 %all-to-all-start.1 = ((bf16[16,112,224]{1,2,0:T(8,128)(2,1)}), bf16[16,112,224]{1,2,0:T(8,128)(2,1)S(1)}, u32[]{:S(2)}, u32[]{:S(2)}) async-start(bf16[16,112,224]{1,2,0:T(8,128)(2,1)} %bitcast.151), calls=%async_computation.1 | async-start | bytes 1835008 | tf_op jit(solution)/shard_map/all_to_all | solution.py:69
  44.9 13.7 %collective-permute-start.2 = (bf16[464,128]{1,0:T(8,128)(2,1)S(1)}, bf16[464,128]{1,0:T(8,128)(2,1)S(1)}, u32[]{:S(2)}, u32[]{:S(2)}) collective-permute-start(bf16[464,128]{1,0:T(8,128)(2,1)S(1)} %fusion.57), channel_id=1, source_target_pairs={{0,12},{4,0},{8,4},{12,8},{1,13},{5,1},{9,5},{13,9},{2,14},{6,2},{... | collective-permute-start | bytes 356360 | tf_op jit(solution)/shard_map/ppermute | solution.py:80
  50.3 11.6 %collective-permute-start.1 = (bf16[464,128]{1,0:T(8,128)(2,1)S(1)}, bf16[464,128]{1,0:T(8,128)(2,1)S(1)}, u32[]{:S(2)}, u32[]{:S(2)}) collective-permute-start(bf16[464,128]{1,0:T(8,128)(2,1)S(1)} %fusion.57), channel_id=1, source_target_pairs={{0,8},{4,12},{8,0},{12,4},{1,9},{5,13},{9,1},{13,5},{2,10},{6,14},... | collective-permute-start | bytes 356360 | tf_op jit(solution)/shard_map/ppermute | solution.py:80
  51.8 11.1 %collective-permute-start = (bf16[464,128]{1,0:T(8,128)(2,1)S(1)}, bf16[464,128]{1,0:T(8,128)(2,1)S(1)}, u32[]{:S(2)}, u32[]{:S(2)}) collective-permute-start(bf16[464,128]{1,0:T(8,128)(2,1)S(1)} %fusion.57), channel_id=1, source_target_pairs={{0,4},{4,8},{8,12},{12,0},{1,5},{5,9},{9,13},{13,1},{2,6},{6,10},{... | collective-permute-start | bytes 356360 | tf_op jit(solution)/shard_map/ppermute | solution.py:80
  66.3 32.8 %all-to-all-start.2 = ((bf16[16,448,128]{2,1,0:T(8,128)(2,1)}), bf16[16,448,128]{2,1,0:T(8,128)(2,1)S(1)}, u32[]{:S(2)}, u32[]{:S(2)}) async-start(bf16[16,448,128]{2,1,0:T(8,128)(2,1)} %broadcast_in_dim.12), calls=%async_computation.2 | async-start | bytes 3670016 | tf_op jit(solution)/shard_map/all_to_all | solution.py:69
  107.9 19.4 %copy-start.4 = (f32[2,112,128]{2,1,0:T(8,128)}, f32[2,112,128]{2,1,0:T(8,128)S(1)}, u32[]{:S(2)}) copy-start(f32[2,112,128]{2,1,0:T(8,128)S(1)} %convert_reduce_fusion.2) | copy-start | bytes 344068
  107.9 19.4 %copy-start.12 = (bf16[112,128]{1,0:T(8,128)(2,1)}, bf16[112,128]{1,0:T(8,128)(2,1)S(1)}, u32[]{:S(2)}) copy-start(bf16[112,128]{1,0:T(8,128)(2,1)S(1)} %get-tuple-element.34) | copy-start | bytes 86020
  108.0 19.3 %copy-start.18 = (s32[1792]{0:T(1024)S(1)}, s32[1792]{0:T(1024)}, u32[]{:S(2)}) copy-start(s32[1792]{0:T(1024)} %copy-done.17) | copy-start | bytes 21508
  108.1 19.3 %copy-start.33 = (s32[224]{0:T(256)S(1)}, s32[224]{0:T(256)}, u32[]{:S(2)}) copy-start(s32[224]{0:T(256)} %copy-done.32) | copy-start | bytes 2692
  129.3 16.3 %copy-start.7 = (f32[224,128]{1,0:T(8,128)S(1)}, f32[224,128]{1,0:T(8,128)}, u32[]{:S(2)}) copy-start(f32[224,128]{1,0:T(8,128)} %copy-done.6) | copy-start | bytes 344068
  129.3 16.3 %copy-start.14 = (f32[224,128]{1,0:T(8,128)S(1)}, f32[224,128]{1,0:T(8,128)}, u32[]{:S(2)}) copy-start(f32[224,128]{1,0:T(8,128)} %get-tuple-element.51) | copy-start | bytes 344068
  130.1 10.3 %collective-permute-start.4 = (bf16[448,128]{1,0:T(8,128)(2,1)S(1)}, bf16[448,128]{1,0:T(8,128)(2,1)S(1)}, u32[]{:S(2)}, u32[]{:S(2)}) collective-permute-start(bf16[448,128]{1,0:T(8,128)(2,1)S(1)} %pad_maximum_fusion.2), channel_id=1, source_target_pairs={{0,8},{4,12},{8,0},{12,4},{1,9},{5,13},{9,1},{13,5},{2,10},{6,14},... | collective-permute-start | bytes 344072 | tf_op jit(solution)/shard_map/ppermute | solution.py:80
  135.9 9.7 %collective-permute-start.3 = (bf16[448,128]{1,0:T(8,128)(2,1)S(1)}, bf16[448,128]{1,0:T(8,128)(2,1)S(1)}, u32[]{:S(2)}, u32[]{:S(2)}) collective-permute-start(bf16[448,128]{1,0:T(8,128)(2,1)S(1)} %pad_maximum_fusion.2), channel_id=1, source_target_pairs={{0,4},{4,8},{8,12},{12,0},{1,5},{5,9},{9,13},{13,1},{2,6},{6,10},{... | collective-permute-start | bytes 344072 | tf_op jit(solution)/shard_map/ppermute | solution.py:80
  137.9 7.7 %collective-permute-start.5 = (bf16[448,128]{1,0:T(8,128)(2,1)S(1)}, bf16[448,128]{1,0:T(8,128)(2,1)S(1)}, u32[]{:S(2)}, u32[]{:S(2)}) collective-permute-start(bf16[448,128]{1,0:T(8,128)(2,1)S(1)} %pad_maximum_fusion.2), channel_id=1, source_target_pairs={{0,12},{4,0},{8,4},{12,8},{1,13},{5,1},{9,5},{13,9},{2,14},{6,2},{... | collective-permute-start | bytes 344072 | tf_op jit(solution)/shard_map/ppermute | solution.py:80
  147.4 31.7 %all-to-all-start.4 = ((bf16[16,448,128]{2,1,0:T(8,128)(2,1)}), bf16[16,448,128]{2,1,0:T(8,128)(2,1)S(1)}, u32[]{:S(2)}, u32[]{:S(2)}) async-start(bf16[16,448,128]{2,1,0:T(8,128)(2,1)} %broadcast_in_dim.14), calls=%async_computation.4 | async-start | bytes 3670016 | tf_op jit(solution)/shard_map/all_to_all | solution.py:69
  157.1 22.1 %copy-start.10 = (bf16[112,128]{1,0:T(8,128)(2,1)S(1)}, bf16[112,128]{1,0:T(8,128)(2,1)}, u32[]{:S(2)}) copy-start(bf16[112,128]{1,0:T(8,128)(2,1)} %param.10) | copy-start | bytes 86020
  157.1 22.1 %copy-start.21 = (f32[128]{0:T(128)S(1)}, f32[128]{0:T(128)}, u32[]{:S(2)}) copy-start(f32[128]{0:T(128)} %copy-done.20) | copy-start | bytes 1540
  157.1 22.1 %copy-start.24 = (f32[112]{0:T(128)S(1)}, f32[112]{0:T(128)}, u32[]{:S(2)}) copy-start(f32[112]{0:T(128)} %param.11) | copy-start | bytes 1348
  157.1 22.2 %copy-start.26 = (f32[128]{0:T(128)S(1)}, f32[128]{0:T(128)}, u32[]{:S(2)}) copy-start(f32[128]{0:T(128)} %copy-done.25) | copy-start | bytes 1540
  157.1 22.2 %copy-start.29 = (bf16[112,3584]{1,0:T(8,128)(2,1)S(1)}, bf16[112,3584]{1,0:T(8,128)(2,1)}, u32[]{:S(2)}) copy-start(bf16[112,3584]{1,0:T(8,128)(2,1)} %param.17) | copy-start | bytes 2408452
  (22 other events, 69.7 us)

commit v4 on v3

--- a/solution.py
+++ b/solution.py
@@ -1,6 +1,8 @@
 import jax
 import jax.numpy as jnp
 from jax import lax
+from jax.experimental import pallas as pl
+from jax.experimental.pallas import tpu as pltpu
 from jax.sharding import Mesh, PartitionSpec as P
 
 D = 7168
@@ -95,6 +97,46 @@
     return matrix.reshape(rows, count, cols // count).transpose(1, 0, 2)
 
 
+def pack_kernel(weight_ref, gain_ref, inputs_ref, sent_ref):
+    count, rows, _ = sent_ref.shape
+    units = weight_ref.shape[1] // count
+    length = inputs_ref.shape[1]
+    rest = units - length
+    on_row = lax.broadcasted_iota(jnp.int32, (rows, rows), 0)
+    on_col = lax.broadcasted_iota(jnp.int32, (rows, rows), 1)
+    gain = jnp.sum(jnp.where(on_row == on_col, gain_ref[...], 0.0), axis=1, keepdims=True)
+    lane = lax.broadcasted_iota(jnp.int32, (rows, length), 1)
+    tail = jnp.zeros((rows, length), jnp.float32)
+    for at, term in enumerate(three_terms(gain)):
+        tail = jnp.where(lane == rest + at, term.astype(jnp.float32), tail)
+    tail = tail[:, rest:].astype(jnp.bfloat16)
+    for at in range(count):
+        first = at * units
+        sent_ref[at, :, 0:length] = weight_ref[:, first : first + length]
+        sent_ref[at, :, length : 2 * length] = jnp.concatenate(
+            [weight_ref[:, first + length : first + units], tail], axis=1
+        )
+        sent_ref[at, :, 2 * length : 3 * length] = inputs_ref[...]
+
+
+def packed_blocks(weight, gain, inputs, count):
+    rows, cols = weight.shape
+    length = inputs.shape[1]
+    group = 4
+    return pl.pallas_call(
+        pack_kernel,
+        grid=(count // group,),
+        in_specs=[
+            pl.BlockSpec((rows, group * cols // count), lambda at: (0, at)),
+            pl.BlockSpec((1, rows), lambda at: (0, 0)),
+            pl.BlockSpec(inputs.shape, lambda at: (0, 0)),
+        ],
+        out_specs=pl.BlockSpec((group, rows, 3 * length), lambda at: (at, 0, 0)),
+        out_shape=jax.ShapeDtypeStruct((count, rows, 3 * length), weight.dtype),
+        cost_estimate=pl.CostEstimate(flops=0, bytes_accessed=5 * weight.size, transcendentals=0),
+    )(weight, gain[None], inputs)
+
+
 def dot_rows(left, right, **options):
     return lax.dot_general(left, right, contract_rows, preferred_element_type=jnp.float32, **options)
 
@@ -115,7 +157,6 @@
     units = hidden_width // planes
     plane_rows = planes * features
     padded = -(-units // length) * length
-    values = inputs.astype(jnp.float32)
 
     row_index = lax.axis_index(DP) * features + jnp.arange(features, dtype=jnp.int32)
     col_start = lax.axis_index(TENSOR) * hidden_width
@@ -125,23 +166,28 @@
     ).reshape(plane_rows)
     unit_start = col_start + lax.axis_index(PLANE) * units
 
-    gain_terms = jnp.stack(three_terms(ln_gain), axis=1)
-    side = jnp.concatenate(
-        [gain_terms, jnp.zeros((features, padded - units - 3), jnp.bfloat16), inputs], axis=1
-    )
-    sent = jnp.concatenate(
-        [column_blocks(w_in, planes), jnp.broadcast_to(side[None], (planes,) + side.shape)], axis=2
-    )
-    got = swap(sent, PLANE)
-    out_blocks, got = lax.optimization_barrier((column_blocks(w_out, planes), got))
-    plane_out = swap(out_blocks, PLANE).reshape(plane_rows, units)
+    sent = packed_blocks(w_in, ln_gain, inputs, planes)
+    sent, seeds, inputs, segment_ids = lax.optimization_barrier(
+        (sent, probe_seed, inputs, segment_ids)
+    )
+    values = inputs.astype(jnp.float32)
+    probes = (
+        probe_signs(seeds[0], plane_index, unit_start, units),
+        probe_signs(seeds[1], plane_index, unit_start, units),
+        probe_signs(seeds[0], row_index, col_start, hidden_width),
+        probe_signs(seeds[1], row_index, col_start, hidden_width),
+    )
+    target = jnp.concatenate([values[:, 1:], jnp.zeros((features, 1), jnp.float32)], axis=1)
+    weights = token_weights(segment_ids)
+    got, out_blocks, probes, target, weights = lax.optimization_barrier(
+        (swap(sent, PLANE), column_blocks(w_out, planes), probes, target, weights)
+    )
+    plane_probe_in, plane_probe_out, probe_in, probe_out = probes
     got = got.reshape(plane_rows, padded + length)
     plane_in = got[:, :units]
     gain_cols = got[:, units : units + 3]
     plane_gain = jnp.sum(gain_cols.astype(jnp.float32), axis=1, keepdims=True)
     plane_values = got[:, padded:].astype(jnp.float32)
-    plane_probe_in = probe_signs(probe_seed[0], plane_index, unit_start, units)
-    plane_probe_out = probe_signs(probe_seed[1], plane_index, unit_start, units)
 
     plane_mean = jnp.mean(plane_values, axis=0)
     plane_centered = plane_values - plane_mean
@@ -160,17 +206,17 @@
     )
     extra_rows = extras.shape[0]
     extras = jnp.pad(extras, ((0, -extra_rows % 16), (0, 0)))
-    every = turns(
-        jnp.concatenate(
-            [
-                dot_rows(plane_in, scaled).astype(jnp.bfloat16),
-                dot_rows(plane_probe_in, scaled).astype(jnp.bfloat16),
-                extras,
-            ],
-            axis=0,
-        )
-    )
-    every, plane_out = lax.optimization_barrier((every, plane_out))
+    own = jnp.concatenate(
+        [
+            dot_rows(plane_in, scaled).astype(jnp.bfloat16),
+            dot_rows(plane_probe_in, scaled).astype(jnp.bfloat16),
+            extras,
+        ],
+        axis=0,
+    )
+    own, out_blocks = lax.optimization_barrier((own, out_blocks))
+    every, plane_out = lax.optimization_barrier((turns(own), swap(out_blocks, PLANE)))
+    plane_out = plane_out.reshape(plane_rows, units)
     every = [part.astype(jnp.float32) for part in every]
     tails = jnp.stack([part[2 * units : 2 * units + extra_rows] for part in every])
     sums = tails[:, : 2 * padded // length].reshape(deep, 2, padded)[:, :, :units]
@@ -194,8 +240,6 @@
     hidden = both[:, :units].reshape(hidden_width, length)
     hidden_dot = both[:, units:].reshape(hidden_width, length)
 
-    probe_in = probe_signs(probe_seed[0], row_index, col_start, hidden_width)
-    probe_out = probe_signs(probe_seed[1], row_index, col_start, hidden_width)
     share = jnp.stack(
         [
             dot_plain(w_out, hidden),
@@ -203,23 +247,24 @@
         ]
     ).astype(jnp.bfloat16)
     output, output_dot = jnp.sum(lax.all_gather(share, TENSOR).astype(jnp.float32), axis=0)
-    target = jnp.concatenate([values[:, 1:], jnp.zeros((features, 1), jnp.float32)], axis=1)
-    weights = token_weights(segment_ids)
     cotangent = (weights * (output - target)).astype(jnp.bfloat16)
     cotangent_dot = (weights * output_dot).astype(jnp.bfloat16)
 
     plane_cot = spread(jnp.concatenate([cotangent, cotangent_dot], axis=0), PLANE)
     plane_cot_dot = plane_cot[:, features:].reshape(plane_rows, length)
     plane_cot = plane_cot[:, :features].reshape(plane_rows, length)
-    back_parts = turns(
-        jnp.concatenate(
-            [
-                dot_rows(plane_out, plane_cot),
-                dot_rows(plane_out, plane_cot_dot) + dot_rows(plane_probe_out, plane_cot),
-            ],
-            axis=0,
-        ).astype(jnp.bfloat16)
-    )
+    own = jnp.concatenate(
+        [
+            dot_rows(plane_out, plane_cot),
+            dot_rows(plane_out, plane_cot_dot) + dot_rows(plane_probe_out, plane_cot),
+        ],
+        axis=0,
+    ).astype(jnp.bfloat16)
+    own, cotangent, cotangent_dot = lax.optimization_barrier((own, cotangent, cotangent_dot))
+    grad_out = dot_cols(cotangent, hidden)
+    hvp_out = dot_cols(cotangent_dot, hidden) + dot_cols(cotangent, hidden_dot)
+    outs = sophia_update(mom_out, hess_out, grad_out, hvp_out, probe_out)
+    back_parts, outs = lax.optimization_barrier((turns(own), outs))
     back_total = sum(part.astype(jnp.float32) for part in back_parts)
     back, back_dot = back_total[:units], back_total[units:]
     grads = spread(
@@ -232,15 +277,10 @@
     pre_grad_dot = grads[:, units:].reshape(hidden_width, length)
 
     normed = ((values - mean_val) * scale * ln_gain[:, None]).astype(jnp.bfloat16)
-    grad_out = dot_cols(cotangent, hidden)
-    hvp_out = dot_cols(cotangent_dot, hidden) + dot_cols(cotangent, hidden_dot)
     grad_in = dot_cols(normed, pre_grad)
     hvp_in = dot_cols(normed, pre_grad_dot)
     new_mom_in, new_hess_in, step_in = sophia_update(mom_in, hess_in, grad_in, hvp_in, probe_in)
-    new_mom_out, new_hess_out, step_out = sophia_update(
-        mom_out, hess_out, grad_out, hvp_out, probe_out
-    )
-    return (new_mom_in, new_hess_in, step_in, new_mom_out, new_hess_out, step_out)
+    return (new_mom_in, new_hess_in, step_in) + tuple(outs)
 
 
 def solution(mesh):

time: 187 us -> 171 us (0.914); the launches traced: 183 us -> 170 us
  blocking collectives: 24.8 us -> 85.3 us
  waiting for transfers between devices: 76.5 us -> 25.2 us
  starting transfers between devices: 41.2 us -> 27.8 us
  local copies, waits for them, and re-layouts: 14.8 us -> 5.69 us
  matrix products: 20.7 us -> 12 us
  other arithmetic: 3.81 us -> 9.38 us
  Pallas kernels: 0 us -> 3.74 us
    all_to_all x1 -> x3, blocking collectives: 19.1 us -> 79.6 us  [swap(): return lax.all_to_all(blocks, axes, 0, 0, tiled=True)]
    all_to_all x4 -> x2, waiting for transfers between devices: 66.6 us -> 11.3 us  [swap(): return lax.all_to_all(blocks, axes, 0, 0, tiled=True)]
    all_to_all x4 -> x2, starting transfers between devices: 22 us -> 10.8 us  [swap(): return lax.all_to_all(blocks, axes, 0, 0, tiled=True)]
    convert_element_type x0 -> x2, other arithmetic: none -> 7.94 us  [probe_signs(): return (1 - 2 * (hashed & 1)).astype(jnp.bfloat16)]
    dot_general x9, matrix products: 8.95 us -> 4.65 us  [dot_rows(): lax.dot_general(left, right, contract_rows, preferred_element_type=jnp.fl...]
    ppermute x6, waiting for transfers between devices: 9.91 us -> 13.9 us  [turns(): lax.ppermute(block, DEPTH, [(at, (at + shift) % count) for at in range(co...]
    pallas_call x0 -> x1, Pallas kernels: none -> 3.74 us  [packed_blocks(): pl.pallas_call(pack_kernel, grid=(count // group,), in_specs=[pl.BlockSpe...]
    dot_general x5, matrix products: 8.55 us -> 5.93 us  [dot_cols(): lax.dot_general(left, right, contract_cols, preferred_element_type=jnp.fl...]
  transfers between devices with their start and end apart: 10 -> 8, of which waited for: 8 -> 6; matrix products, arithmetic and copies ran while one was open for 9% -> 8% of each run, Pallas kernels for 0% -> 0%
where the time goes in v4:
time: 171 us; the launch traced here: 170 us
  blocking collectives  85.3 us (50%)
  starting transfers between devices  27.8 us (16%)
  waiting for transfers between devices  25.2 us (15%)
  matrix products  12 us (7%)
  other arithmetic  9.38 us (5%)
  local copies, waits for them, and re-layouts  5.69 us (3%)
  Pallas kernels  3.74 us (2%)
    all_to_all x3, blocking collectives, swap(): return lax.all_to_all(blocks, axes, 0, 0, tiled=True)  79.6 us
    ppermute x6, starting transfers between devices, turns(): lax.ppermute(block, DEPTH, [(at, (at + shift) % count) for at in range(co...  17 us
    ppermute x6, waiting for transfers between devices, turns(): lax.ppermute(block, DEPTH, [(at, (at + shift) % count) for at in range(co...  13.9 us
    all_to_all x2, waiting for transfers between devices, swap(): return lax.all_to_all(blocks, axes, 0, 0, tiled=True)  11.3 us
    all_to_all x2, starting transfers between devices, swap(): return lax.all_to_all(blocks, axes, 0, 0, tiled=True)  10.8 us
    convert_element_type x2, other arithmetic, probe_signs(): return (1 - 2 * (hashed & 1)).astype(jnp.bfloat16)  7.94 us
    dot_general x5, matrix products, dot_cols(): lax.dot_general(left, right, contract_cols, preferred_element_type=jnp.fl...  5.93 us
    all_gather x1, blocking collectives, body(): lax.all_gather(share, TENSOR).astype(jnp.float32)  5.7 us
  transfers between devices with their start and end apart: 8, of which 6 were waited for; matrix products, arithmetic and copies ran while one was open for 8% of the time, Pallas kernels for 0%

profile of v4, /device:TPU:32, one launch (start us, length us, event | category | flops | bytes accessed | tf_op | source)
XLA Modules:
  0.0 170.1 jit_solution(2509304954952745732)
XLA Ops:
  0.6 3.7 %shard_map.145 = bf16[16,112,384]{2,1,0:T(8,128)(2,1)} custom-call(bf16[112,3584]{1,0:T(8,128)(2,1)} %weight_ref.1, f32[1,112]{1,0:T(1,128)} %bitcast.159, bf16[112,128]{1,0:T(8,128)(2,1)} %inputs_ref.1), custom_call_target="tpu_custom_call" | custom-call | bytes 2007040 | tf_op jit(solution)/shard_map/pallas_call | solution.py:126
  4.4 7.2 %all-to-all-start = ((bf16[16,112,384]{2,1,0:T(8,128)(2,1)}), bf16[16,112,384]{2,1,0:T(8,128)(2,1)S(1)}, u32[]{:S(2)}, u32[]{:S(2)}) async-start(bf16[16,112,384]{2,1,0:T(8,128)(2,1)} %shard_map.145), calls=%async_computation | async-start | bytes 2752512 | tf_op jit(solution)/shard_map/all_to_all | solution.py:71
  12.4 4.2 %subtract_convert_fusion = (bf16[1792,224]{1,0:T(8,128)(2,1)}, bf16[1792,224]{1,0:T(8,128)(2,1)}) fusion(s32[]{:T(128)} %bitcast.4, s32[224]{0:T(256)S(1)} %iota_add_fusion.1, s32[1792]{0:T(1024)S(1)} %mul.252, s32[]{:T(128)} %bitcast.3), kind=kLoop, calls=%fused_computation.33 | loop fusion | flops 13246464 | bytes 1613704 | tf_op jit(solution)/shard_map/convert_element_type | solution.py:35
  16.6 1.3 copy.23
  18.3 3.7 %subtract_convert_fusion.2 = (bf16[112,3584]{1,0:T(8,128)(2,1)S(1)}, bf16[112,3584]{1,0:T(8,128)(2,1)}) fusion(s32[]{:T(128)} %bitcast.4, s32[3584]{0:T(1024)S(1)} %iota_add_fusion, s32[112]{0:T(128)S(1)} %add_multiply_fusion.2, s32[]{:T(128)} %bitcast.3), kind=kLoop, calls=%fused_computation.49 | loop fusion | flops 13246464 | bytes 1620424 | tf_op jit(solution)/shard_map/convert_element_type | solution.py:35
  22.0 11.3 %all-to-all-done = bf16[16,112,384]{2,1,0:T(8,128)(2,1)S(1)} async-done(((bf16[16,112,384]{2,1,0:T(8,128)(2,1)}), bf16[16,112,384]{2,1,0:T(8,128)(2,1)S(1)}, u32[]{:S(2)}, u32[]{:S(2)}) %all-to-all-start) | async-done | bytes 1376288 | tf_op jit(solution)/shard_map/all_to_all | solution.py:71
  36.9 3.6 %all-to-all-start.1 = ((bf16[16,112,224]{1,2,0:T(8,128)(2,1)}), bf16[16,112,224]{1,2,0:T(8,128)(2,1)S(1)}, u32[]{:S(2)}, u32[]{:S(2)}) async-start(bf16[16,112,224]{1,2,0:T(8,128)(2,1)} %bitcast.154), calls=%async_computation.1 | async-start | bytes 1835008 | tf_op jit(solution)/shard_map/all_to_all | solution.py:71
  40.5 5.5 %collective-permute-start.2 = (bf16[464,128]{1,0:T(8,128)(2,1)S(1)}, bf16[464,128]{1,0:T(8,128)(2,1)S(1)}, u32[]{:S(2)}, u32[]{:S(2)}) collective-permute-start(bf16[464,128]{1,0:T(8,128)(2,1)S(1)} %fusion.58), channel_id=1, source_target_pairs={{0,12},{4,0},{8,4},{12,8},{1,13},{5,1},{9,5},{13,9},{2,14},{6,2},{... | collective-permute-start | bytes 356360 | tf_op jit(solution)/shard_map/ppermute | solution.py:82
  46.0 1.4 collective-permute-start.1
  47.4 2.4 %collective-permute-start = (bf16[464,128]{1,0:T(8,128)(2,1)S(1)}, bf16[464,128]{1,0:T(8,128)(2,1)S(1)}, u32[]{:S(2)}, u32[]{:S(2)}) collective-permute-start(bf16[464,128]{1,0:T(8,128)(2,1)S(1)} %fusion.58), channel_id=1, source_target_pairs={{0,4},{4,8},{8,12},{12,0},{1,5},{5,9},{9,13},{13,1},{2,6},{6,10},{... | collective-permute-start | bytes 356360 | tf_op jit(solution)/shard_map/ppermute | solution.py:82
  49.8 1.1 collective-permute-done.2
  50.9 6.6 %collective-permute-done.1 = bf16[464,128]{1,0:T(8,128)(2,1)S(1)} collective-permute-done((bf16[464,128]{1,0:T(8,128)(2,1)S(1)}, bf16[464,128]{1,0:T(8,128)(2,1)S(1)}, u32[]{:S(2)}, u32[]{:S(2)}) %collective-permute-start.1) | collective-permute-done | bytes 118816 | tf_op jit(solution)/shard_map/ppermute | solution.py:82
  60.1 31.6 %all_to_all.25 = bf16[16,448,128]{2,1,0:T(8,128)(2,1)S(1)} all-to-all(bf16[16,448,128]{2,1,0:T(8,128)(2,1)S(1)} %broadcast_in_dim.9), channel_id=1, replica_groups=mesh['y'=4,'x'=4,'h'=4,'l'=2,'c'=2] {'y','x'}, dimensions={0} | all-to-all | bytes 3670016 | tf_op jit(solution)/shard_map/all_to_all | solution.py:71
  93.0 5.7 %all_gather.4 = bf16[4,2,112,128]{3,2,1,0:T(8,128)(2,1)S(1)} all-gather(bf16[1,2,112,128]{3,2,1,0:T(8,128)(2,1)S(1)} %pad_maximum_fusion.3), channel_id=1, replica_groups=mesh['y'=4,'x'=4,'h'=4,'l'=2,'c'=2] {'l','c'}, dimensions={0}, use_global_device_ids=true | all-gather | bytes 286720 | tf_op jit(solution)/shard_map/all_gather | solution.py:249
  98.9 19.3 %all_to_all.26 = bf16[16,224,128]{2,1,0:T(8,128)(2,1)S(1)} all-to-all(bf16[16,224,128]{2,1,0:T(8,128)(2,1)S(1)} %broadcast_in_dim.10), channel_id=1, replica_groups=mesh['y'=4,'x'=4,'h'=4,'l'=2,'c'=2] {'y','x'}, dimensions={0} | all-to-all | bytes 1835008 | tf_op jit(solution)/shard_map/all_to_all | solution.py:71
  119.6 4.1 %collective-permute-start.5 = (bf16[448,128]{1,0:T(8,128)(2,1)S(1)}, bf16[448,128]{1,0:T(8,128)(2,1)S(1)}, u32[]{:S(2)}, u32[]{:S(2)}) collective-permute-start(bf16[448,128]{1,0:T(8,128)(2,1)S(1)} %pad_maximum_fusion.1), channel_id=1, source_target_pairs={{0,12},{4,0},{8,4},{12,8},{1,13},{5,1},{9,5},{13,9},{2,14},{6,2},{... | collective-permute-start | bytes 344072 | tf_op jit(solution)/shard_map/ppermute | solution.py:82
  123.7 1.5 collective-permute-start.4
  125.3 2.0 %collective-permute-start.3 = (bf16[448,128]{1,0:T(8,128)(2,1)S(1)}, bf16[448,128]{1,0:T(8,128)(2,1)S(1)}, u32[]{:S(2)}, u32[]{:S(2)}) collective-permute-start(bf16[448,128]{1,0:T(8,128)(2,1)S(1)} %pad_maximum_fusion.1), channel_id=1, source_target_pairs={{0,4},{4,8},{8,12},{12,0},{1,5},{5,9},{9,13},{13,1},{2,6},{6,10},{... | collective-permute-start | bytes 344072 | tf_op jit(solution)/shard_map/ppermute | solution.py:82
  128.8 2.2 %clamp_convert_fusion.1 = (bf16[112,3584]{1,0:T(8,128)(2,1)}, bf16[112,3584]{1,0:T(8,128)(2,1)}, bf16[112,3584]{1,0:T(8,128)(2,1)}) fusion(f32[112,3584]{1,0:T(8,128)S(1)} %fusion.3, bf16[112,128]{1,0:T(8,128)(2,1)S(1)} %get-tuple-element.54, bf16[3584,128]{1,0:T(8,128)(2,1)S(1)} %bitcast.151, bf16[112,3584]{1,0:T(8,128)(2,1)S(1)} %copy-done.9), kind=kOutput, calls=%fused_computation.48 | convolution fusion | flops 107175936 | bytes 5763072 | tf_op jit(solution)/shard_map/dot_general | solution.py:145
  131.0 3.6 %collective-permute-done.4 = bf16[448,128]{1,0:T(8,128)(2,1)S(1)} collective-permute-done((bf16[448,128]{1,0:T(8,128)(2,1)S(1)}, bf16[448,128]{1,0:T(8,128)(2,1)S(1)}, u32[]{:S(2)}, u32[]{:S(2)}) %collective-permute-start.4) | collective-permute-done | bytes 114720 | tf_op jit(solution)/shard_map/ppermute | solution.py:82
  134.6 1.6 collective-permute-done.3
  136.7 28.7 %all_to_all.27 = bf16[16,448,128]{2,1,0:T(8,128)(2,1)S(1)} all-to-all(bf16[16,448,128]{2,1,0:T(8,128)(2,1)S(1)} %broadcast_in_dim.11), channel_id=1, replica_groups=mesh['y'=4,'x'=4,'h'=4,'l'=2,'c'=2] {'y','x'}, dimensions={0} | all-to-all | bytes 3670016 | tf_op jit(solution)/shard_map/all_to_all | solution.py:71
  165.5 1.0 copy-done.3
  167.9 2.2 %clamp_convert_fusion = (bf16[112,3584]{1,0:T(8,128)(2,1)}, bf16[112,3584]{1,0:T(8,128)(2,1)}, bf16[112,3584]{1,0:T(8,128)(2,1)}) fusion(f32[112,3584]{1,0:T(8,128)S(1)} %fusion, bf16[3584,128]{1,0:T(8,128)(2,1)S(1)} %bitcast.157, f32[112]{0:T(128)S(1)} %copy-done.7, f32[128]{0:T(128)S(1)} %add_rsqrt_fusion, f32[128]{0:T(128)S(1)} %broadcast_multiply_fusion, ...), kind=kOutput, calls=%fused_computation.47 | convolution fusion | flops 107247616 | bytes 5764544 | tf_op jit(solution)/shard_map/dot_general | solution.py:145
  (96 shorter events, 13.3 us)
Async XLA Ops:
  4.4 7.4 %copy-start.8 = (s32[2]{0:T(128)S(1)}, s32[2]{0:T(128)}, u32[]{:S(2)}) copy-start(s32[2]{0:T(128)} %param.19) | copy-start | bytes 28
  4.4 28.9 %all-to-all-start = ((bf16[16,112,384]{2,1,0:T(8,128)(2,1)}), bf16[16,112,384]{2,1,0:T(8,128)(2,1)S(1)}, u32[]{:S(2)}, u32[]{:S(2)}) async-start(bf16[16,112,384]{2,1,0:T(8,128)(2,1)} %shard_map.145), calls=%async_computation | async-start | bytes 2752512 | tf_op jit(solution)/shard_map/all_to_all | solution.py:71
  11.5 5.0 %copy-start = (bf16[112,3584]{1,0:T(8,128)(2,1)S(1)}, bf16[112,3584]{1,0:T(8,128)(2,1)}, u32[]{:S(2)}) copy-start(bf16[112,3584]{1,0:T(8,128)(2,1)} %param.14) | copy-start | bytes 2408452
  12.4 5.5 %copy-start.11 = (s32[128]{0:T(128)S(1)}, s32[128]{0:T(128)}, u32[]{:S(2)}) copy-start(s32[128]{0:T(128)} %param.12) | copy-start | bytes 1540
  12.4 5.6 %copy-start.6 = (bf16[112,128]{1,0:T(8,128)(2,1)S(1)}, bf16[112,128]{1,0:T(8,128)(2,1)}, u32[]{:S(2)}) copy-start(bf16[112,128]{1,0:T(8,128)(2,1)} %inputs_ref.1) | copy-start | bytes 86020
  33.3 1.5 copy-start.1
  36.9 21.7 %all-to-all-start.1 = ((bf16[16,112,224]{1,2,0:T(8,128)(2,1)}), bf16[16,112,224]{1,2,0:T(8,128)(2,1)S(1)}, u32[]{:S(2)}, u32[]{:S(2)}) async-start(bf16[16,112,224]{1,2,0:T(8,128)(2,1)} %bitcast.154), calls=%async_computation.1 | async-start | bytes 1835008 | tf_op jit(solution)/shard_map/all_to_all | solution.py:71
  40.5 10.4 %collective-permute-start.2 = (bf16[464,128]{1,0:T(8,128)(2,1)S(1)}, bf16[464,128]{1,0:T(8,128)(2,1)S(1)}, u32[]{:S(2)}, u32[]{:S(2)}) collective-permute-start(bf16[464,128]{1,0:T(8,128)(2,1)S(1)} %fusion.58), channel_id=1, source_target_pairs={{0,12},{4,0},{8,4},{12,8},{1,13},{5,1},{9,5},{13,9},{2,14},{6,2},{... | collective-permute-start | bytes 356360 | tf_op jit(solution)/shard_map/ppermute | solution.py:82
  46.0 11.6 %collective-permute-start.1 = (bf16[464,128]{1,0:T(8,128)(2,1)S(1)}, bf16[464,128]{1,0:T(8,128)(2,1)S(1)}, u32[]{:S(2)}, u32[]{:S(2)}) collective-permute-start(bf16[464,128]{1,0:T(8,128)(2,1)S(1)} %fusion.58), channel_id=1, source_target_pairs={{0,8},{4,12},{8,0},{12,4},{1,9},{5,13},{9,1},{13,5},{2,10},{6,14},... | collective-permute-start | bytes 356360 | tf_op jit(solution)/shard_map/ppermute | solution.py:82
  47.4 11.1 %collective-permute-start = (bf16[464,128]{1,0:T(8,128)(2,1)S(1)}, bf16[464,128]{1,0:T(8,128)(2,1)S(1)}, u32[]{:S(2)}, u32[]{:S(2)}) collective-permute-start(bf16[464,128]{1,0:T(8,128)(2,1)S(1)} %fusion.58), channel_id=1, source_target_pairs={{0,4},{4,8},{8,12},{12,0},{1,5},{5,9},{9,13},{13,1},{2,6},{6,10},{... | collective-permute-start | bytes 356360 | tf_op jit(solution)/shard_map/ppermute | solution.py:82
  98.9 19.3 %copy-start.2 = (bf16[1792,224]{1,0:T(8,128)(2,1)S(1)}, bf16[1792,224]{1,0:T(8,128)(2,1)}, u32[]{:S(2)}) copy-start(bf16[1792,224]{1,0:T(8,128)(2,1)} %get-tuple-element.52) | copy-start | bytes 2408452
  119.6 8.1 %copy-start.4 = (bf16[112,3584]{1,0:T(8,128)(2,1)S(1)}, bf16[112,3584]{1,0:T(8,128)(2,1)}, u32[]{:S(2)}) copy-start(bf16[112,3584]{1,0:T(8,128)(2,1)} %param.18) | copy-start | bytes 2408452
  119.6 11.4 %collective-permute-start.5 = (bf16[448,128]{1,0:T(8,128)(2,1)S(1)}, bf16[448,128]{1,0:T(8,128)(2,1)S(1)}, u32[]{:S(2)}, u32[]{:S(2)}) collective-permute-start(bf16[448,128]{1,0:T(8,128)(2,1)S(1)} %pad_maximum_fusion.1), channel_id=1, source_target_pairs={{0,12},{4,0},{8,4},{12,8},{1,13},{5,1},{9,5},{13,9},{2,14},{6,2},{... | collective-permute-start | bytes 344072 | tf_op jit(solution)/shard_map/ppermute | solution.py:82
  123.7 10.8 %collective-permute-start.4 = (bf16[448,128]{1,0:T(8,128)(2,1)S(1)}, bf16[448,128]{1,0:T(8,128)(2,1)S(1)}, u32[]{:S(2)}, u32[]{:S(2)}) collective-permute-start(bf16[448,128]{1,0:T(8,128)(2,1)S(1)} %pad_maximum_fusion.1), channel_id=1, source_target_pairs={{0,8},{4,12},{8,0},{12,4},{1,9},{5,13},{9,1},{13,5},{2,10},{6,14},... | collective-permute-start | bytes 344072 | tf_op jit(solution)/shard_map/ppermute | solution.py:82
  125.3 10.9 %collective-permute-start.3 = (bf16[448,128]{1,0:T(8,128)(2,1)S(1)}, bf16[448,128]{1,0:T(8,128)(2,1)S(1)}, u32[]{:S(2)}, u32[]{:S(2)}) collective-permute-start(bf16[448,128]{1,0:T(8,128)(2,1)S(1)} %pad_maximum_fusion.1), channel_id=1, source_target_pairs={{0,4},{4,8},{8,12},{12,0},{1,5},{5,9},{9,13},{13,1},{2,6},{6,10},{... | collective-permute-start | bytes 344072 | tf_op jit(solution)/shard_map/ppermute | solution.py:82
  127.7 1.1 copy-start.9
  165.3 1.1 copy-start.3
  165.3 1.4 copy-start.5
  165.3 1.4 copy-start.7
  166.7 1.1 copy-start.10

commit v5 on v4

--- a/solution.py
+++ b/solution.py
@@ -21,6 +21,7 @@
 DEPTH = ("h",)
 DP = PLANE + DEPTH
 TENSOR = ("l", "c")
+CORE = "c"
 
 
 def mixing(words):
@@ -90,11 +91,6 @@
         terms.append(rest.astype(jnp.bfloat16))
         rest = rest - terms[-1].astype(jnp.float32)
     return terms
-
-
-def column_blocks(matrix, count):
-    rows, cols = matrix.shape
-    return matrix.reshape(rows, count, cols // count).transpose(1, 0, 2)
 
 
 def pack_kernel(weight_ref, gain_ref, inputs_ref, sent_ref):
@@ -137,6 +133,33 @@
     )(weight, gain[None], inputs)
 
 
+def column_kernel(weight_ref, blocks_ref):
+    count, rows, padded = blocks_ref.shape
+    units = weight_ref.shape[1] // count
+    for at in range(count):
+        blocks_ref[at] = jnp.concatenate(
+            [
+                weight_ref[:, at * units : (at + 1) * units],
+                jnp.zeros((rows, padded - units), weight_ref.dtype),
+            ],
+            axis=1,
+        )
+
+
+def column_blocks(weight, count, lanes):
+    rows, cols = weight.shape
+    padded = -(-cols // count // lanes) * lanes
+    group = 4
+    return pl.pallas_call(
+        column_kernel,
+        grid=(count // group,),
+        in_specs=[pl.BlockSpec((rows, group * cols // count), lambda at: (0, at))],
+        out_specs=pl.BlockSpec((group, rows, padded), lambda at: (at, 0, 0)),
+        out_shape=jax.ShapeDtypeStruct((count, rows, padded), weight.dtype),
+        cost_estimate=pl.CostEstimate(flops=0, bytes_accessed=5 * weight.size, transcendentals=0),
+    )(weight)
+
+
 def dot_rows(left, right, **options):
     return lax.dot_general(left, right, contract_rows, preferred_element_type=jnp.float32, **options)
 
@@ -167,8 +190,8 @@
     unit_start = col_start + lax.axis_index(PLANE) * units
 
     sent = packed_blocks(w_in, ln_gain, inputs, planes)
-    sent, seeds, inputs, segment_ids = lax.optimization_barrier(
-        (sent, probe_seed, inputs, segment_ids)
+    sent, seeds, inputs, segment_ids, later_out = lax.optimization_barrier(
+        (sent, probe_seed, inputs, segment_ids, w_out)
     )
     values = inputs.astype(jnp.float32)
     probes = (
@@ -179,8 +202,9 @@
     )
     target = jnp.concatenate([values[:, 1:], jnp.zeros((features, 1), jnp.float32)], axis=1)
     weights = token_weights(segment_ids)
-    got, out_blocks, probes, target, weights = lax.optimization_barrier(
-        (swap(sent, PLANE), column_blocks(w_out, planes), probes, target, weights)
+    first_core = lax.axis_index(CORE) == 0
+    got, out_blocks, probes, target, weights, first_core = lax.optimization_barrier(
+        (swap(sent, PLANE), column_blocks(later_out, planes, length), probes, target, weights, first_core)
     )
     plane_probe_in, plane_probe_out, probe_in, probe_out = probes
     got = got.reshape(plane_rows, padded + length)
@@ -216,7 +240,7 @@
     )
     own, out_blocks = lax.optimization_barrier((own, out_blocks))
     every, plane_out = lax.optimization_barrier((turns(own), swap(out_blocks, PLANE)))
-    plane_out = plane_out.reshape(plane_rows, units)
+    plane_out = plane_out.reshape(plane_rows, padded)[:, :units]
     every = [part.astype(jnp.float32) for part in every]
     tails = jnp.stack([part[2 * units : 2 * units + extra_rows] for part in every])
     sums = tails[:, : 2 * padded // length].reshape(deep, 2, padded)[:, :, :units]
@@ -250,9 +274,10 @@
     cotangent = (weights * (output - target)).astype(jnp.bfloat16)
     cotangent_dot = (weights * output_dot).astype(jnp.bfloat16)
 
-    plane_cot = spread(jnp.concatenate([cotangent, cotangent_dot], axis=0), PLANE)
-    plane_cot_dot = plane_cot[:, features:].reshape(plane_rows, length)
-    plane_cot = plane_cot[:, :features].reshape(plane_rows, length)
+    held = spread(jnp.where(first_core, cotangent, cotangent_dot), PLANE).reshape(plane_rows, length)
+    other = lax.ppermute(held, CORE, [(0, 1), (1, 0)])
+    plane_cot = jnp.where(first_core, held, other)
+    plane_cot_dot = jnp.where(first_core, other, held)
     own = jnp.concatenate(
         [
             dot_rows(plane_out, plane_cot),

time: 171 us -> 169 us (0.988)
  blocking collectives: 85.3 us -> 80.4 us
  Pallas kernels: 3.74 us -> 7.25 us
    all_to_all x3, blocking collectives: 79.6 us -> 74.5 us  [swap(): return lax.all_to_all(blocks, axes, 0, 0, tiled=True)]
    pallas_call x0 -> x1, Pallas kernels: none -> 3.52 us  [column_blocks(): pl.pallas_call(column_kernel, grid=(count // group,), in_specs=[pl.BlockS...]
    all_to_all x2, waiting for transfers between devices: 11.3 us -> 9.23 us  [swap(): return lax.all_to_all(blocks, axes, 0, 0, tiled=True)]
    ppermute x0 -> x1, waiting for transfers between devices: none -> 1.81 us  [body(): other = lax.ppermute(held, CORE, [(0, 1), (1, 0)])]
    unnamed x24 -> x22, local copies, waits for them, and re-layouts: 2.4 us -> 3.42 us
  transfers between devices with their start and end apart: 8 -> 9, of which waited for: 6 -> 7; matrix products, arithmetic and copies ran while one was open for 8% -> 7% of each run, Pallas kernels for 0% -> 2%
where the time goes in v5:
time: 169 us; the launch traced here: 168 us
  blocking collectives  80.4 us (48%)
  starting transfers between devices  27.8 us (16%)
  waiting for transfers between devices  25.5 us (15%)
  matrix products  11.9 us (7%)
  other arithmetic  9.22 us (5%)
  Pallas kernels  7.25 us (4%)
  local copies, waits for them, and re-layouts  5.35 us (3%)
    all_to_all x3, blocking collectives, swap(): return lax.all_to_all(blocks, axes, 0, 0, tiled=True)  74.5 us
    ppermute x6, starting transfers between devices, turns(): lax.ppermute(block, DEPTH, [(at, (at + shift) % count) for at in range(co...  17 us
    ppermute x6, waiting for transfers between devices, turns(): lax.ppermute(block, DEPTH, [(at, (at + shift) % count) for at in range(co...  14.5 us
    all_to_all x2, starting transfers between devices, swap(): return lax.all_to_all(blocks, axes, 0, 0, tiled=True)  10.8 us
    all_to_all x2, waiting for transfers between devices, swap(): return lax.all_to_all(blocks, axes, 0, 0, tiled=True)  9.23 us
    convert_element_type x2, other arithmetic, probe_signs(): return (1 - 2 * (hashed & 1)).astype(jnp.bfloat16)  7.78 us
    dot_general x5, matrix products, dot_cols(): lax.dot_general(left, right, contract_cols, preferred_element_type=jnp.fl...  5.91 us
    all_gather x1, blocking collectives, body(): lax.all_gather(share, TENSOR).astype(jnp.float32)  5.83 us
  transfers between devices with their start and end apart: 9, of which 7 were waited for; matrix products, arithmetic and copies ran while one was open for 7% of the time, Pallas kernels for 2%

profile of v5, /device:TPU:32, one launch (start us, length us, event | category | flops | bytes accessed | tf_op | source)
XLA Modules:
  0.0 168.4 jit_solution(12987262253189935194)
XLA Ops:
  0.6 3.7 %shard_map.145 = bf16[16,112,384]{2,1,0:T(8,128)(2,1)} custom-call(bf16[112,3584]{1,0:T(8,128)(2,1)} %weight_ref.1, f32[1,112]{1,0:T(1,128)} %bitcast.150, bf16[112,128]{1,0:T(8,128)(2,1)} %inputs_ref.1), custom_call_target="tpu_custom_call" | custom-call | bytes 2007040 | tf_op jit(solution)/shard_map/pallas_call | solution.py:122
  4.4 7.2 %all-to-all-start = ((bf16[16,112,384]{2,1,0:T(8,128)(2,1)}), bf16[16,112,384]{2,1,0:T(8,128)(2,1)S(1)}, u32[]{:S(2)}, u32[]{:S(2)}) async-start(bf16[16,112,384]{2,1,0:T(8,128)(2,1)} %shard_map.145), calls=%async_computation | async-start | bytes 2752512 | tf_op jit(solution)/shard_map/all_to_all | solution.py:72
  12.4 4.1 %subtract_convert_fusion = (bf16[1792,224]{1,0:T(8,128)(2,1)}, bf16[1792,224]{1,0:T(8,128)(2,1)S(1)}) fusion(s32[]{:T(128)} %bitcast.2, s32[224]{0:T(256)S(1)} %iota_add_fusion.1, s32[1792]{0:T(1024)S(1)} %mul.252, s32[]{:T(128)} %bitcast.1), kind=kLoop, calls=%fused_computation.33 | loop fusion | flops 13246464 | bytes 1613704 | tf_op jit(solution)/shard_map/convert_element_type | solution.py:36
  16.6 3.5 %shard_map.146 = bf16[16,112,256]{2,1,0:T(8,128)(2,1)} custom-call(bf16[112,3584]{1,0:T(8,128)(2,1)} %weight_ref.2), custom_call_target="tpu_custom_call" | custom-call | bytes 2007040 | tf_op jit(solution)/shard_map/pallas_call | solution.py:153
  20.3 3.7 %subtract_convert_fusion.2 = (bf16[112,3584]{1,0:T(8,128)(2,1)S(1)}, bf16[112,3584]{1,0:T(8,128)(2,1)}) fusion(s32[]{:T(128)} %bitcast.2, s32[3584]{0:T(1024)S(1)} %iota_add_fusion, s32[112]{0:T(128)S(1)} %add_multiply_fusion.2, s32[]{:T(128)} %bitcast.1), kind=kLoop, calls=%fused_computation.49 | loop fusion | flops 13246464 | bytes 1620424 | tf_op jit(solution)/shard_map/convert_element_type | solution.py:36
  24.1 9.2 %all-to-all-done = bf16[16,112,384]{2,1,0:T(8,128)(2,1)S(1)} async-done(((bf16[16,112,384]{2,1,0:T(8,128)(2,1)}), bf16[16,112,384]{2,1,0:T(8,128)(2,1)S(1)}, u32[]{:S(2)}, u32[]{:S(2)}) %all-to-all-start) | async-done | bytes 1376288 | tf_op jit(solution)/shard_map/all_to_all | solution.py:72
  36.9 3.6 %all-to-all-start.1 = ((bf16[16,112,256]{2,1,0:T(8,128)(2,1)}), bf16[16,112,256]{2,1,0:T(8,128)(2,1)S(1)}, u32[]{:S(2)}, u32[]{:S(2)}) async-start(bf16[16,112,256]{2,1,0:T(8,128)(2,1)} %shard_map.146), calls=%async_computation.1 | async-start | bytes 1835008 | tf_op jit(solution)/shard_map/all_to_all | solution.py:72
  40.5 5.5 %collective-permute-start.2 = (bf16[464,128]{1,0:T(8,128)(2,1)S(1)}, bf16[464,128]{1,0:T(8,128)(2,1)S(1)}, u32[]{:S(2)}, u32[]{:S(2)}) collective-permute-start(bf16[464,128]{1,0:T(8,128)(2,1)S(1)} %fusion.60), channel_id=1, source_target_pairs={{0,12},{4,0},{8,4},{12,8},{1,13},{5,1},{9,5},{13,9},{2,14},{6,2},{... | collective-permute-start | bytes 356360 | tf_op jit(solution)/shard_map/ppermute | solution.py:83
  46.0 1.4 collective-permute-start.1
  47.4 2.4 %collective-permute-start = (bf16[464,128]{1,0:T(8,128)(2,1)S(1)}, bf16[464,128]{1,0:T(8,128)(2,1)S(1)}, u32[]{:S(2)}, u32[]{:S(2)}) collective-permute-start(bf16[464,128]{1,0:T(8,128)(2,1)S(1)} %fusion.60), channel_id=1, source_target_pairs={{0,4},{4,8},{8,12},{12,0},{1,5},{5,9},{9,13},{13,1},{2,6},{6,10},{... | collective-permute-start | bytes 356360 | tf_op jit(solution)/shard_map/ppermute | solution.py:83
  49.8 1.1 collective-permute-done.2
  50.9 6.7 %collective-permute-done.1 = bf16[464,128]{1,0:T(8,128)(2,1)S(1)} collective-permute-done((bf16[464,128]{1,0:T(8,128)(2,1)S(1)}, bf16[464,128]{1,0:T(8,128)(2,1)S(1)}, u32[]{:S(2)}, u32[]{:S(2)}) %collective-permute-start.1) | collective-permute-done | bytes 118816 | tf_op jit(solution)/shard_map/ppermute | solution.py:83
  60.0 31.6 %all_to_all.25 = bf16[16,448,128]{2,1,0:T(8,128)(2,1)S(1)} all-to-all(bf16[16,448,128]{2,1,0:T(8,128)(2,1)S(1)} %broadcast_in_dim.9), channel_id=1, replica_groups=mesh['y'=4,'x'=4,'h'=4,'l'=2,'c'=2] {'y','x'}, dimensions={0} | all-to-all | bytes 3670016 | tf_op jit(solution)/shard_map/all_to_all | solution.py:72
  91.8 1.0 copy-done
  94.0 5.8 %all_gather.4 = bf16[4,2,112,128]{3,2,1,0:T(8,128)(2,1)S(1)} all-gather(bf16[1,2,112,128]{3,2,1,0:T(8,128)(2,1)S(1)} %pad_maximum_fusion.3), channel_id=1, replica_groups=mesh['y'=4,'x'=4,'h'=4,'l'=2,'c'=2] {'l','c'}, dimensions={0}, use_global_device_ids=true | all-gather | bytes 286720 | tf_op jit(solution)/shard_map/all_gather | solution.py:273
  100.0 14.2 %all_to_all.26 = bf16[16,112,128]{2,1,0:T(8,128)(2,1)S(1)} all-to-all(bf16[16,112,128]{2,1,0:T(8,128)(2,1)S(1)} %broadcast_in_dim.10), channel_id=1, replica_groups=mesh['y'=4,'x'=4,'h'=4,'l'=2,'c'=2] {'y','x'}, dimensions={0} | all-to-all | bytes 917504 | tf_op jit(solution)/shard_map/all_to_all | solution.py:72
  114.2 1.8 %collective-permute-done.3 = bf16[1792,128]{1,0:T(8,128)(2,1)S(1)} collective-permute-done((bf16[1792,128]{1,0:T(8,128)(2,1)S(1)}, bf16[1792,128]{1,0:T(8,128)(2,1)S(1)}, u32[]{:S(2)}, u32[]{:S(2)}) %collective-permute-start.3) | collective-permute-done | bytes 458784 | tf_op jit(solution)/shard_map/ppermute | solution.py:278
  117.3 4.1 %collective-permute-start.6 = (bf16[448,128]{1,0:T(8,128)(2,1)S(1)}, bf16[448,128]{1,0:T(8,128)(2,1)S(1)}, u32[]{:S(2)}, u32[]{:S(2)}) collective-permute-start(bf16[448,128]{1,0:T(8,128)(2,1)S(1)} %pad_maximum_fusion.1), channel_id=1, source_target_pairs={{0,12},{4,0},{8,4},{12,8},{1,13},{5,1},{9,5},{13,9},{2,14},{6,2},{... | collective-permute-start | bytes 344072 | tf_op jit(solution)/shard_map/ppermute | solution.py:83
  121.5 1.5 collective-permute-start.5
  123.0 2.0 %collective-permute-start.4 = (bf16[448,128]{1,0:T(8,128)(2,1)S(1)}, bf16[448,128]{1,0:T(8,128)(2,1)S(1)}, u32[]{:S(2)}, u32[]{:S(2)}) collective-permute-start(bf16[448,128]{1,0:T(8,128)(2,1)S(1)} %pad_maximum_fusion.1), channel_id=1, source_target_pairs={{0,4},{4,8},{8,12},{12,0},{1,5},{5,9},{9,13},{13,1},{2,6},{6,10},{... | collective-permute-start | bytes 344072 | tf_op jit(solution)/shard_map/ppermute | solution.py:83
  126.6 2.2 %clamp_convert_fusion.1 = (bf16[112,3584]{1,0:T(8,128)(2,1)}, bf16[112,3584]{1,0:T(8,128)(2,1)}, bf16[112,3584]{1,0:T(8,128)(2,1)}) fusion(f32[112,3584]{1,0:T(8,128)S(1)} %fusion.3, bf16[112,128]{1,0:T(8,128)(2,1)S(1)} %get-tuple-element.58, bf16[3584,128]{1,0:T(8,128)(2,1)S(1)} %bitcast.138, bf16[112,3584]{1,0:T(8,128)(2,1)S(1)} %copy-done.8), kind=kOutput, calls=%fused_computation.48 | convolution fusion | flops 107175936 | bytes 5763072 | tf_op jit(solution)/shard_map/dot_general | solution.py:168
  128.7 4.8 %collective-permute-done.5 = bf16[448,128]{1,0:T(8,128)(2,1)S(1)} collective-permute-done((bf16[448,128]{1,0:T(8,128)(2,1)S(1)}, bf16[448,128]{1,0:T(8,128)(2,1)S(1)}, u32[]{:S(2)}, u32[]{:S(2)}) %collective-permute-start.5) | collective-permute-done | bytes 114720 | tf_op jit(solution)/shard_map/ppermute | solution.py:83
  135.0 28.7 %all_to_all.27 = bf16[16,448,128]{2,1,0:T(8,128)(2,1)S(1)} all-to-all(bf16[16,448,128]{2,1,0:T(8,128)(2,1)S(1)} %broadcast_in_dim.11), channel_id=1, replica_groups=mesh['y'=4,'x'=4,'h'=4,'l'=2,'c'=2] {'y','x'}, dimensions={0} | all-to-all | bytes 3670016 | tf_op jit(solution)/shard_map/all_to_all | solution.py:72
  166.2 2.2 %clamp_convert_fusion = (bf16[112,3584]{1,0:T(8,128)(2,1)}, bf16[112,3584]{1,0:T(8,128)(2,1)}, bf16[112,3584]{1,0:T(8,128)(2,1)}) fusion(f32[112,3584]{1,0:T(8,128)S(1)} %fusion, bf16[3584,128]{1,0:T(8,128)(2,1)S(1)} %bitcast.146, f32[112]{0:T(128)S(1)} %copy-done.6, f32[128]{0:T(128)S(1)} %add_rsqrt_fusion, f32[128]{0:T(128)S(1)} %broadcast_multiply_fusion, ...), kind=kOutput, calls=%fused_computation.47 | convolution fusion | flops 107247616 | bytes 5764544 | tf_op jit(solution)/shard_map/dot_general | solution.py:168
  (94 shorter events, 15.2 us)
Async XLA Ops:
  4.4 7.4 %copy-start.7 = (s32[2]{0:T(128)S(1)}, s32[2]{0:T(128)}, u32[]{:S(2)}) copy-start(s32[2]{0:T(128)} %param.19) | copy-start | bytes 28
  4.4 28.9 %all-to-all-start = ((bf16[16,112,384]{2,1,0:T(8,128)(2,1)}), bf16[16,112,384]{2,1,0:T(8,128)(2,1)S(1)}, u32[]{:S(2)}, u32[]{:S(2)}) async-start(bf16[16,112,384]{2,1,0:T(8,128)(2,1)} %shard_map.145), calls=%async_computation | async-start | bytes 2752512 | tf_op jit(solution)/shard_map/all_to_all | solution.py:72
  11.5 4.9 %copy-start.10 = (s32[128]{0:T(128)S(1)}, s32[128]{0:T(128)}, u32[]{:S(2)}) copy-start(s32[128]{0:T(128)} %param.12) | copy-start | bytes 1540
  11.6 5.0 %copy-start.5 = (bf16[112,128]{1,0:T(8,128)(2,1)S(1)}, bf16[112,128]{1,0:T(8,128)(2,1)}, u32[]{:S(2)}) copy-start(bf16[112,128]{1,0:T(8,128)(2,1)} %inputs_ref.1) | copy-start | bytes 86020
  36.9 21.7 %all-to-all-start.1 = ((bf16[16,112,256]{2,1,0:T(8,128)(2,1)}), bf16[16,112,256]{2,1,0:T(8,128)(2,1)S(1)}, u32[]{:S(2)}, u32[]{:S(2)}) async-start(bf16[16,112,256]{2,1,0:T(8,128)(2,1)} %shard_map.146), calls=%async_computation.1 | async-start | bytes 1835008 | tf_op jit(solution)/shard_map/all_to_all | solution.py:72
  40.5 10.4 %collective-permute-start.2 = (bf16[464,128]{1,0:T(8,128)(2,1)S(1)}, bf16[464,128]{1,0:T(8,128)(2,1)S(1)}, u32[]{:S(2)}, u32[]{:S(2)}) collective-permute-start(bf16[464,128]{1,0:T(8,128)(2,1)S(1)} %fusion.60), channel_id=1, source_target_pairs={{0,12},{4,0},{8,4},{12,8},{1,13},{5,1},{9,5},{13,9},{2,14},{6,2},{... | collective-permute-start | bytes 356360 | tf_op jit(solution)/shard_map/ppermute | solution.py:83
  46.0 11.6 %collective-permute-start.1 = (bf16[464,128]{1,0:T(8,128)(2,1)S(1)}, bf16[464,128]{1,0:T(8,128)(2,1)S(1)}, u32[]{:S(2)}, u32[]{:S(2)}) collective-permute-start(bf16[464,128]{1,0:T(8,128)(2,1)S(1)} %fusion.60), channel_id=1, source_target_pairs={{0,8},{4,12},{8,0},{12,4},{1,9},{5,13},{9,1},{13,5},{2,10},{6,14},... | collective-permute-start | bytes 356360 | tf_op jit(solution)/shard_map/ppermute | solution.py:83
  47.4 11.1 %collective-permute-start = (bf16[464,128]{1,0:T(8,128)(2,1)S(1)}, bf16[464,128]{1,0:T(8,128)(2,1)S(1)}, u32[]{:S(2)}, u32[]{:S(2)}) collective-permute-start(bf16[464,128]{1,0:T(8,128)(2,1)S(1)} %fusion.60), channel_id=1, source_target_pairs={{0,4},{4,8},{8,12},{12,0},{1,5},{5,9},{9,13},{13,1},{2,6},{6,10},{... | collective-permute-start | bytes 356360 | tf_op jit(solution)/shard_map/ppermute | solution.py:83
  91.7 1.1 copy-start
  94.0 22.0 %copy-start.1 = (bf16[1792,224]{1,0:T(8,128)(2,1)S(1)}, bf16[1792,224]{1,0:T(8,128)(2,1)}, u32[]{:S(2)}) copy-start(bf16[1792,224]{1,0:T(8,128)(2,1)} %get-tuple-element.56) | copy-start | bytes 2408452
  114.2 1.8 %collective-permute-start.3 = (bf16[1792,128]{1,0:T(8,128)(2,1)S(1)}, bf16[1792,128]{1,0:T(8,128)(2,1)S(1)}, u32[]{:S(2)}, u32[]{:S(2)}) collective-permute-start(bf16[1792,128]{1,0:T(8,128)(2,1)S(1)} %bitcast.142), channel_id=1, source_target_pairs={{0,1},{1,0},{2,3},{3,2},{4,5},{5,4},{6,7},{7,6},{8,9},{9,8},{10,11... | collective-permute-start | bytes 1376264 | tf_op jit(solution)/shard_map/ppermute | solution.py:278
  117.3 8.1 %copy-start.3 = (bf16[112,3584]{1,0:T(8,128)(2,1)S(1)}, bf16[112,3584]{1,0:T(8,128)(2,1)}, u32[]{:S(2)}) copy-start(bf16[112,3584]{1,0:T(8,128)(2,1)} %param.18) | copy-start | bytes 2408452
  117.3 11.4 %collective-permute-start.6 = (bf16[448,128]{1,0:T(8,128)(2,1)S(1)}, bf16[448,128]{1,0:T(8,128)(2,1)S(1)}, u32[]{:S(2)}, u32[]{:S(2)}) collective-permute-start(bf16[448,128]{1,0:T(8,128)(2,1)S(1)} %pad_maximum_fusion.1), channel_id=1, source_target_pairs={{0,12},{4,0},{8,4},{12,8},{1,13},{5,1},{9,5},{13,9},{2,14},{6,2},{... | collective-permute-start | bytes 344072 | tf_op jit(solution)/shard_map/ppermute | solution.py:83
  121.5 12.1 %collective-permute-start.5 = (bf16[448,128]{1,0:T(8,128)(2,1)S(1)}, bf16[448,128]{1,0:T(8,128)(2,1)S(1)}, u32[]{:S(2)}, u32[]{:S(2)}) collective-permute-start(bf16[448,128]{1,0:T(8,128)(2,1)S(1)} %pad_maximum_fusion.1), channel_id=1, source_target_pairs={{0,8},{4,12},{8,0},{12,4},{1,9},{5,13},{9,1},{13,5},{2,10},{6,14},... | collective-permute-start | bytes 344072 | tf_op jit(solution)/shard_map/ppermute | solution.py:83
  123.0 11.5 %collective-permute-start.4 = (bf16[448,128]{1,0:T(8,128)(2,1)S(1)}, bf16[448,128]{1,0:T(8,128)(2,1)S(1)}, u32[]{:S(2)}, u32[]{:S(2)}) collective-permute-start(bf16[448,128]{1,0:T(8,128)(2,1)S(1)} %pad_maximum_fusion.1), channel_id=1, source_target_pairs={{0,4},{4,8},{8,12},{12,0},{1,5},{5,9},{9,13},{13,1},{2,6},{6,10},{... | collective-permute-start | bytes 344072 | tf_op jit(solution)/shard_map/ppermute | solution.py:83
  125.4 1.1 copy-start.8
  163.7 1.1 copy-start.2
  163.7 1.4 copy-start.4
  163.7 1.4 copy-start.6
  165.1 1.1 copy-start.9

commit v6 on v5

--- a/solution.py
+++ b/solution.py
@@ -66,6 +66,45 @@
         curvature.astype(jnp.bfloat16),
         stepped.astype(jnp.bfloat16),
     )
+
+
+def update_kernel(normed_ref, grads_ref, probe_ref, mom_ref, hess_ref, new_mom, new_hess, step):
+    count, both, _ = grads_ref.shape
+    units = both // 2
+    normed = normed_ref[...]
+    pre_grad = jnp.concatenate([grads_ref[at, 0:units] for at in range(count)], axis=0)
+    pre_grad_dot = jnp.concatenate([grads_ref[at, units:both] for at in range(count)], axis=0)
+    new_mom[...], new_hess[...], step[...] = sophia_update(
+        mom_ref[...],
+        hess_ref[...],
+        dot_cols(normed, pre_grad),
+        dot_cols(normed, pre_grad_dot),
+        probe_ref[...],
+    )
+
+
+def updated(normed, grads, probe, mom, hess):
+    count, both, length = grads.shape
+    rows, cols = mom.shape
+    group = 4
+    wide = pl.BlockSpec((rows, group * cols // count), lambda at: (0, at))
+    return pl.pallas_call(
+        update_kernel,
+        grid=(count // group,),
+        in_specs=[
+            pl.BlockSpec(normed.shape, lambda at: (0, 0)),
+            pl.BlockSpec((group, both, length), lambda at: (at, 0, 0)),
+            wide,
+            wide,
+            wide,
+        ],
+        out_specs=[wide] * 3,
+        out_shape=[jax.ShapeDtypeStruct(mom.shape, mom.dtype)] * 3,
+        cost_estimate=pl.CostEstimate(
+            flops=4 * rows * cols * length, bytes_accessed=16 * mom.size, transcendentals=0
+        ),
+        compiler_params=pltpu.CompilerParams(vmem_limit_bytes=32 * 1024 * 1024),
+    )(normed, grads, probe, mom, hess)
 
 
 def swap(blocks, axes):
@@ -289,7 +328,8 @@
     grad_out = dot_cols(cotangent, hidden)
     hvp_out = dot_cols(cotangent_dot, hidden) + dot_cols(cotangent, hidden_dot)
     outs = sophia_update(mom_out, hess_out, grad_out, hvp_out, probe_out)
-    back_parts, outs = lax.optimization_barrier((turns(own), outs))
+    normed = ((values - mean_val) * scale * ln_gain[:, None]).astype(jnp.bfloat16)
+    back_parts, outs, normed = lax.optimization_barrier((turns(own), outs, normed))
     back_total = sum(part.astype(jnp.float32) for part in back_parts)
     back, back_dot = back_total[:units], back_total[units:]
     grads = spread(
@@ -298,13 +338,8 @@
         ).astype(jnp.bfloat16),
         PLANE,
     )
-    pre_grad = grads[:, :units].reshape(hidden_width, length)
-    pre_grad_dot = grads[:, units:].reshape(hidden_width, length)
-
-    normed = ((values - mean_val) * scale * ln_gain[:, None]).astype(jnp.bfloat16)
-    grad_in = dot_cols(normed, pre_grad)
-    hvp_in = dot_cols(normed, pre_grad_dot)
-    new_mom_in, new_hess_in, step_in = sophia_update(mom_in, hess_in, grad_in, hvp_in, probe_in)
+
+    new_mom_in, new_hess_in, step_in = updated(normed, grads, probe_in, mom_in, hess_in)
     return (new_mom_in, new_hess_in, step_in) + tuple(outs)
 
 

time: 169 us -> 167 us (0.988)
  Pallas kernels: 7.25 us -> 10.1 us
  matrix products: 11.9 us -> 9.09 us
  local copies, waits for them, and re-layouts: 5.35 us -> 3.44 us
    pallas_call x0 -> x1, Pallas kernels: none -> 2.84 us  [updated(): pl.pallas_call(update_kernel, grid=(count // group,), in_specs=[pl.BlockS...]
    dot_general x5 -> x3, matrix products: 5.91 us -> 3.12 us  [dot_cols(): lax.dot_general(left, right, contract_cols, preferred_element_type=jnp.fl...]
    unnamed x22, local copies, waits for them, and re-layouts: 3.42 us -> 1.64 us
where the time goes in v6:
time: 167 us
  blocking collectives  80.5 us (48%)
  starting transfers between devices  27.7 us (17%)
  waiting for transfers between devices  26.2 us (16%)
  Pallas kernels  10.1 us (6%)
  matrix products  9.09 us (5%)
  other arithmetic  8.54 us (5%)
  local copies, waits for them, and re-layouts  3.44 us (2%)
    all_to_all x3, blocking collectives, swap(): return lax.all_to_all(blocks, axes, 0, 0, tiled=True)  74.7 us
    ppermute x6, starting transfers between devices, turns(): lax.ppermute(block, DEPTH, [(at, (at + shift) % count) for at in range(co...  16.9 us
    ppermute x6, waiting for transfers between devices, turns(): lax.ppermute(block, DEPTH, [(at, (at + shift) % count) for at in range(co...  14.5 us
    all_to_all x2, starting transfers between devices, swap(): return lax.all_to_all(blocks, axes, 0, 0, tiled=True)  10.8 us
    all_to_all x2, waiting for transfers between devices, swap(): return lax.all_to_all(blocks, axes, 0, 0, tiled=True)  9.99 us
    convert_element_type x2, other arithmetic, probe_signs(): return (1 - 2 * (hashed & 1)).astype(jnp.bfloat16)  7.03 us
    all_gather x1, blocking collectives, body(): lax.all_gather(share, TENSOR).astype(jnp.float32)  5.83 us
    dot_general x9, matrix products, dot_rows(): lax.dot_general(left, right, contract_rows, preferred_element_type=jnp.fl...  4.64 us
  transfers between devices with their start and end apart: 9, of which 7 were waited for; matrix products, arithmetic and copies ran while one was open for 7% of the time, Pallas kernels for 2%

profile of v6, /device:TPU:32, one launch (start us, length us, event | category | flops | bytes accessed | tf_op | source)
XLA Modules:
  0.0 166.7 jit_solution(3559255769736455318)
XLA Ops:
  0.6 3.7 %shard_map.145 = bf16[16,112,384]{2,1,0:T(8,128)(2,1)} custom-call(bf16[112,3584]{1,0:T(8,128)(2,1)} %weight_ref.1, f32[1,112]{1,0:T(1,128)} %bitcast.144, bf16[112,128]{1,0:T(8,128)(2,1)} %inputs_ref.1), custom_call_target="tpu_custom_call" | custom-call | bytes 2007040 | tf_op jit(solution)/shard_map/pallas_call | solution.py:161
  4.4 7.2 %all-to-all-start = ((bf16[16,112,384]{2,1,0:T(8,128)(2,1)}), bf16[16,112,384]{2,1,0:T(8,128)(2,1)S(1)}, u32[]{:S(2)}, u32[]{:S(2)}) async-start(bf16[16,112,384]{2,1,0:T(8,128)(2,1)} %shard_map.145), calls=%async_computation | async-start | bytes 2752512 | tf_op jit(solution)/shard_map/all_to_all | solution.py:111
  12.4 4.2 %subtract_convert_fusion = (bf16[1792,224]{1,0:T(8,128)(2,1)}, bf16[1792,224]{1,0:T(8,128)(2,1)}) fusion(s32[]{:T(128)} %bitcast.2, s32[224]{0:T(256)S(1)} %iota_add_fusion.1, s32[1792]{0:T(1024)S(1)} %mul.248, s32[]{:T(128)} %bitcast.1), kind=kLoop, calls=%fused_computation.29 | loop fusion | flops 13246464 | bytes 1613704 | tf_op jit(solution)/shard_map/convert_element_type | solution.py:36
  16.7 3.5 %shard_map.146 = bf16[16,112,256]{2,1,0:T(8,128)(2,1)} custom-call(bf16[112,3584]{1,0:T(8,128)(2,1)} %weight_ref.2), custom_call_target="tpu_custom_call" | custom-call | bytes 2007040 | tf_op jit(solution)/shard_map/pallas_call | solution.py:192
  20.4 2.8 %subtract_convert_fusion.2 = (bf16[112,3584]{1,0:T(8,128)(2,1)S(1)}, bf16[112,3584]{1,0:T(8,128)(2,1)S(1)}) fusion(s32[]{:T(128)} %bitcast.2, s32[3584]{0:T(1024)S(1)} %iota_add_fusion, s32[112]{0:T(128)S(1)} %add_multiply_fusion.2, s32[]{:T(128)} %bitcast.1), kind=kLoop, calls=%fused_computation.44 | loop fusion | flops 13246464 | bytes 1620424 | tf_op jit(solution)/shard_map/convert_element_type | solution.py:36
  23.3 10.0 %all-to-all-done = bf16[16,112,384]{2,1,0:T(8,128)(2,1)S(1)} async-done(((bf16[16,112,384]{2,1,0:T(8,128)(2,1)}), bf16[16,112,384]{2,1,0:T(8,128)(2,1)S(1)}, u32[]{:S(2)}, u32[]{:S(2)}) %all-to-all-start) | async-done | bytes 1376288 | tf_op jit(solution)/shard_map/all_to_all | solution.py:111
  36.9 3.6 %all-to-all-start.1 = ((bf16[16,112,256]{2,1,0:T(8,128)(2,1)}), bf16[16,112,256]{2,1,0:T(8,128)(2,1)S(1)}, u32[]{:S(2)}, u32[]{:S(2)}) async-start(bf16[16,112,256]{2,1,0:T(8,128)(2,1)} %shard_map.146), calls=%async_computation.1 | async-start | bytes 1835008 | tf_op jit(solution)/shard_map/all_to_all | solution.py:111
  40.5 5.5 %collective-permute-start.2 = (bf16[464,128]{1,0:T(8,128)(2,1)S(1)}, bf16[464,128]{1,0:T(8,128)(2,1)S(1)}, u32[]{:S(2)}, u32[]{:S(2)}) collective-permute-start(bf16[464,128]{1,0:T(8,128)(2,1)S(1)} %fusion.58), channel_id=1, source_target_pairs={{0,12},{4,0},{8,4},{12,8},{1,13},{5,1},{9,5},{13,9},{2,14},{6,2},{... | collective-permute-start | bytes 356360 | tf_op jit(solution)/shard_map/ppermute | solution.py:122
  46.0 1.4 collective-permute-start.1
  47.4 2.4 %collective-permute-start = (bf16[464,128]{1,0:T(8,128)(2,1)S(1)}, bf16[464,128]{1,0:T(8,128)(2,1)S(1)}, u32[]{:S(2)}, u32[]{:S(2)}) collective-permute-start(bf16[464,128]{1,0:T(8,128)(2,1)S(1)} %fusion.58), channel_id=1, source_target_pairs={{0,4},{4,8},{8,12},{12,0},{1,5},{5,9},{9,13},{13,1},{2,6},{6,10},{... | collective-permute-start | bytes 356360 | tf_op jit(solution)/shard_map/ppermute | solution.py:122
  49.8 1.1 collective-permute-done.2
  50.9 6.6 %collective-permute-done.1 = bf16[464,128]{1,0:T(8,128)(2,1)S(1)} collective-permute-done((bf16[464,128]{1,0:T(8,128)(2,1)S(1)}, bf16[464,128]{1,0:T(8,128)(2,1)S(1)}, u32[]{:S(2)}, u32[]{:S(2)}) %collective-permute-start.1) | collective-permute-done | bytes 118816 | tf_op jit(solution)/shard_map/ppermute | solution.py:122
  60.0 31.7 %all_to_all.25 = bf16[16,448,128]{2,1,0:T(8,128)(2,1)S(1)} all-to-all(bf16[16,448,128]{2,1,0:T(8,128)(2,1)S(1)} %broadcast_in_dim.9), channel_id=1, replica_groups=mesh['y'=4,'x'=4,'h'=4,'l'=2,'c'=2] {'y','x'}, dimensions={0} | all-to-all | bytes 3670016 | tf_op jit(solution)/shard_map/all_to_all | solution.py:111
  91.8 1.0 copy-done.2
  94.0 5.8 %all_gather.4 = bf16[4,2,112,128]{3,2,1,0:T(8,128)(2,1)S(1)} all-gather(bf16[1,2,112,128]{3,2,1,0:T(8,128)(2,1)S(1)} %pad_maximum_fusion.3), channel_id=1, replica_groups=mesh['y'=4,'x'=4,'h'=4,'l'=2,'c'=2] {'l','c'}, dimensions={0}, use_global_device_ids=true | all-gather | bytes 286720 | tf_op jit(solution)/shard_map/all_gather | solution.py:312
  100.0 14.2 %all_to_all.26 = bf16[16,112,128]{2,1,0:T(8,128)(2,1)S(1)} all-to-all(bf16[16,112,128]{2,1,0:T(8,128)(2,1)S(1)} %broadcast_in_dim.10), channel_id=1, replica_groups=mesh['y'=4,'x'=4,'h'=4,'l'=2,'c'=2] {'y','x'}, dimensions={0} | all-to-all | bytes 917504 | tf_op jit(solution)/shard_map/all_to_all | solution.py:111
  114.3 1.7 %collective-permute-done.3 = bf16[1792,128]{1,0:T(8,128)(2,1)S(1)} collective-permute-done((bf16[1792,128]{1,0:T(8,128)(2,1)S(1)}, bf16[1792,128]{1,0:T(8,128)(2,1)S(1)}, u32[]{:S(2)}, u32[]{:S(2)}) %collective-permute-start.3) | collective-permute-done | bytes 458784 | tf_op jit(solution)/shard_map/ppermute | solution.py:317
  117.4 4.1 %collective-permute-start.6 = (bf16[448,128]{1,0:T(8,128)(2,1)S(1)}, bf16[448,128]{1,0:T(8,128)(2,1)S(1)}, u32[]{:S(2)}, u32[]{:S(2)}) collective-permute-start(bf16[448,128]{1,0:T(8,128)(2,1)S(1)} %pad_maximum_fusion.1), channel_id=1, source_target_pairs={{0,12},{4,0},{8,4},{12,8},{1,13},{5,1},{9,5},{13,9},{2,14},{6,2},{... | collective-permute-start | bytes 344072 | tf_op jit(solution)/shard_map/ppermute | solution.py:122
  121.5 1.5 collective-permute-start.5
  123.0 2.0 %collective-permute-start.4 = (bf16[448,128]{1,0:T(8,128)(2,1)S(1)}, bf16[448,128]{1,0:T(8,128)(2,1)S(1)}, u32[]{:S(2)}, u32[]{:S(2)}) collective-permute-start(bf16[448,128]{1,0:T(8,128)(2,1)S(1)} %pad_maximum_fusion.1), channel_id=1, source_target_pairs={{0,4},{4,8},{8,12},{12,0},{1,5},{5,9},{9,13},{13,1},{2,6},{6,10},{... | collective-permute-start | bytes 344072 | tf_op jit(solution)/shard_map/ppermute | solution.py:122
  126.5 2.2 %clamp_convert_fusion = (bf16[112,3584]{1,0:T(8,128)(2,1)}, bf16[112,3584]{1,0:T(8,128)(2,1)}, bf16[112,3584]{1,0:T(8,128)(2,1)}) fusion(f32[112,3584]{1,0:T(8,128)S(1)} %fusion.1, bf16[112,128]{1,0:T(8,128)(2,1)S(1)} %get-tuple-element.62, bf16[3584,128]{1,0:T(8,128)(2,1)S(1)} %bitcast.134, bf16[112,3584]{1,0:T(8,128)(2,1)S(1)} %copy-done.9), kind=kOutput, calls=%fused_computation.43 | convolution fusion | flops 107175936 | bytes 5763072 | tf_op jit(solution)/shard_map/dot_general | solution.py:207
  128.7 4.8 %collective-permute-done.5 = bf16[448,128]{1,0:T(8,128)(2,1)S(1)} collective-permute-done((bf16[448,128]{1,0:T(8,128)(2,1)S(1)}, bf16[448,128]{1,0:T(8,128)(2,1)S(1)}, u32[]{:S(2)}, u32[]{:S(2)}) %collective-permute-start.5) | collective-permute-done | bytes 114720 | tf_op jit(solution)/shard_map/ppermute | solution.py:122
  135.0 28.8 %all_to_all.27.grads_ref = bf16[16,448,128]{2,1,0:T(8,128)(2,1)S(1)} all-to-all(bf16[16,448,128]{2,1,0:T(8,128)(2,1)S(1)} %broadcast_in_dim.11), channel_id=1, replica_groups=mesh['y'=4,'x'=4,'h'=4,'l'=2,'c'=2] {'y','x'}, dimensions={0} | all-to-all | bytes 3670016 | tf_op jit(solution)/shard_map/all_to_all | solution.py:111
  163.8 2.8 %shard_map.147 = (bf16[112,3584]{1,0:T(8,128)(2,1)}, bf16[112,3584]{1,0:T(8,128)(2,1)}, bf16[112,3584]{1,0:T(8,128)(2,1)}) custom-call(bf16[112,128]{1,0:T(8,128)(2,1)S(1)} %multiply_convert_fusion.3.normed_ref, bf16[16,448,128]{2,1,0:T(8,128)(2,1)S(1)} %all_to_all.27.grads_ref, bf16[112,3584]{1,0:T(8,128)(2,1)S(1)} %get-tuple-element.69.probe_ref, ...), custom_call_target="tpu_custom_call" | custom-call | flops 205520896 | bytes 6422528 | tf_op jit(solution)/shard_map/pallas_call | solution.py:91
  (93 shorter events, 12.7 us)
Async XLA Ops:
  4.4 7.4 %copy-start.8 = (s32[2]{0:T(128)S(1)}, s32[2]{0:T(128)}, u32[]{:S(2)}) copy-start(s32[2]{0:T(128)} %param.19) | copy-start | bytes 28
  4.4 28.9 %all-to-all-start = ((bf16[16,112,384]{2,1,0:T(8,128)(2,1)}), bf16[16,112,384]{2,1,0:T(8,128)(2,1)S(1)}, u32[]{:S(2)}, u32[]{:S(2)}) async-start(bf16[16,112,384]{2,1,0:T(8,128)(2,1)} %shard_map.145), calls=%async_computation | async-start | bytes 2752512 | tf_op jit(solution)/shard_map/all_to_all | solution.py:111
  11.5 5.0 %copy-start.10 = (s32[128]{0:T(128)S(1)}, s32[128]{0:T(128)}, u32[]{:S(2)}) copy-start(s32[128]{0:T(128)} %param.12) | copy-start | bytes 1540
  11.5 5.1 %copy-start.6 = (bf16[112,128]{1,0:T(8,128)(2,1)S(1)}, bf16[112,128]{1,0:T(8,128)(2,1)}, u32[]{:S(2)}) copy-start(bf16[112,128]{1,0:T(8,128)(2,1)} %inputs_ref.1) | copy-start | bytes 86020
  33.3 1.5 copy-start.3
  36.9 21.7 %all-to-all-start.1 = ((bf16[16,112,256]{2,1,0:T(8,128)(2,1)}), bf16[16,112,256]{2,1,0:T(8,128)(2,1)S(1)}, u32[]{:S(2)}, u32[]{:S(2)}) async-start(bf16[16,112,256]{2,1,0:T(8,128)(2,1)} %shard_map.146), calls=%async_computation.1 | async-start | bytes 1835008 | tf_op jit(solution)/shard_map/all_to_all | solution.py:111
  40.5 10.4 %collective-permute-start.2 = (bf16[464,128]{1,0:T(8,128)(2,1)S(1)}, bf16[464,128]{1,0:T(8,128)(2,1)S(1)}, u32[]{:S(2)}, u32[]{:S(2)}) collective-permute-start(bf16[464,128]{1,0:T(8,128)(2,1)S(1)} %fusion.58), channel_id=1, source_target_pairs={{0,12},{4,0},{8,4},{12,8},{1,13},{5,1},{9,5},{13,9},{2,14},{6,2},{... | collective-permute-start | bytes 356360 | tf_op jit(solution)/shard_map/ppermute | solution.py:122
  46.0 11.6 %collective-permute-start.1 = (bf16[464,128]{1,0:T(8,128)(2,1)S(1)}, bf16[464,128]{1,0:T(8,128)(2,1)S(1)}, u32[]{:S(2)}, u32[]{:S(2)}) collective-permute-start(bf16[464,128]{1,0:T(8,128)(2,1)S(1)} %fusion.58), channel_id=1, source_target_pairs={{0,8},{4,12},{8,0},{12,4},{1,9},{5,13},{9,1},{13,5},{2,10},{6,14},... | collective-permute-start | bytes 356360 | tf_op jit(solution)/shard_map/ppermute | solution.py:122
  47.4 11.1 %collective-permute-start = (bf16[464,128]{1,0:T(8,128)(2,1)S(1)}, bf16[464,128]{1,0:T(8,128)(2,1)S(1)}, u32[]{:S(2)}, u32[]{:S(2)}) collective-permute-start(bf16[464,128]{1,0:T(8,128)(2,1)S(1)} %fusion.58), channel_id=1, source_target_pairs={{0,4},{4,8},{8,12},{12,0},{1,5},{5,9},{9,13},{13,1},{2,6},{6,10},{... | collective-permute-start | bytes 356360 | tf_op jit(solution)/shard_map/ppermute | solution.py:122
  91.7 1.1 copy-start.2
  94.0 20.2 %copy-start.7 = (f32[112]{0:T(128)S(1)}, f32[112]{0:T(128)}, u32[]{:S(2)}) copy-start(f32[112]{0:T(128)} %param.11) | copy-start | bytes 1348
  94.0 22.0 %copy-start.4 = (bf16[1792,224]{1,0:T(8,128)(2,1)S(1)}, bf16[1792,224]{1,0:T(8,128)(2,1)}, u32[]{:S(2)}) copy-start(bf16[1792,224]{1,0:T(8,128)(2,1)} %get-tuple-element.60) | copy-start | bytes 2408452
  114.2 1.8 %collective-permute-start.3 = (bf16[1792,128]{1,0:T(8,128)(2,1)S(1)}, bf16[1792,128]{1,0:T(8,128)(2,1)S(1)}, u32[]{:S(2)}, u32[]{:S(2)}) collective-permute-start(bf16[1792,128]{1,0:T(8,128)(2,1)S(1)} %bitcast.137), channel_id=1, source_target_pairs={{0,1},{1,0},{2,3},{3,2},{4,5},{5,4},{6,7},{7,6},{8,9},{9,8},{10,11... | collective-permute-start | bytes 1376264 | tf_op jit(solution)/shard_map/ppermute | solution.py:317
  117.3 8.1 %copy-start.5 = (bf16[112,3584]{1,0:T(8,128)(2,1)S(1)}, bf16[112,3584]{1,0:T(8,128)(2,1)}, u32[]{:S(2)}) copy-start(bf16[112,3584]{1,0:T(8,128)(2,1)} %param.18) | copy-start | bytes 2408452
  117.4 11.4 %collective-permute-start.6 = (bf16[448,128]{1,0:T(8,128)(2,1)S(1)}, bf16[448,128]{1,0:T(8,128)(2,1)S(1)}, u32[]{:S(2)}, u32[]{:S(2)}) collective-permute-start(bf16[448,128]{1,0:T(8,128)(2,1)S(1)} %pad_maximum_fusion.1), channel_id=1, source_target_pairs={{0,12},{4,0},{8,4},{12,8},{1,13},{5,1},{9,5},{13,9},{2,14},{6,2},{... | collective-permute-start | bytes 344072 | tf_op jit(solution)/shard_map/ppermute | solution.py:122
  121.5 12.1 %collective-permute-start.5 = (bf16[448,128]{1,0:T(8,128)(2,1)S(1)}, bf16[448,128]{1,0:T(8,128)(2,1)S(1)}, u32[]{:S(2)}, u32[]{:S(2)}) collective-permute-start(bf16[448,128]{1,0:T(8,128)(2,1)S(1)} %pad_maximum_fusion.1), channel_id=1, source_target_pairs={{0,8},{4,12},{8,0},{12,4},{1,9},{5,13},{9,1},{13,5},{2,10},{6,14},... | collective-permute-start | bytes 344072 | tf_op jit(solution)/shard_map/ppermute | solution.py:122
  123.0 11.5 %collective-permute-start.4 = (bf16[448,128]{1,0:T(8,128)(2,1)S(1)}, bf16[448,128]{1,0:T(8,128)(2,1)S(1)}, u32[]{:S(2)}, u32[]{:S(2)}) collective-permute-start(bf16[448,128]{1,0:T(8,128)(2,1)S(1)} %pad_maximum_fusion.1), channel_id=1, source_target_pairs={{0,4},{4,8},{8,12},{12,0},{1,5},{5,9},{9,13},{13,1},{2,6},{6,10},{... | collective-permute-start | bytes 344072 | tf_op jit(solution)/shard_map/ppermute | solution.py:122
  125.4 1.1 copy-start.9
  135.0 28.8 %copy-start = (bf16[112,3584]{1,0:T(8,128)(2,1)S(1)}, bf16[112,3584]{1,0:T(8,128)(2,1)}, u32[]{:S(2)}) copy-start(bf16[112,3584]{1,0:T(8,128)(2,1)} %mom_ref.1) | copy-start | bytes 2408452
  135.0 28.8 %copy-start.1 = (bf16[112,3584]{1,0:T(8,128)(2,1)S(1)}, bf16[112,3584]{1,0:T(8,128)(2,1)}, u32[]{:S(2)}) copy-start(bf16[112,3584]{1,0:T(8,128)(2,1)} %hess_ref.1) | copy-start | bytes 2408452

commit v7 on v6

--- a/solution.py
+++ b/solution.py
@@ -86,7 +86,7 @@
 def updated(normed, grads, probe, mom, hess):
     count, both, length = grads.shape
     rows, cols = mom.shape
-    group = 4
+    group = 8
     wide = pl.BlockSpec((rows, group * cols // count), lambda at: (0, at))
     return pl.pallas_call(
         update_kernel,
@@ -157,7 +157,7 @@
 def packed_blocks(weight, gain, inputs, count):
     rows, cols = weight.shape
     length = inputs.shape[1]
-    group = 4
+    group = 8
     return pl.pallas_call(
         pack_kernel,
         grid=(count // group,),
@@ -188,7 +188,7 @@
 def column_blocks(weight, count, lanes):
     rows, cols = weight.shape
     padded = -(-cols // count // lanes) * lanes
-    group = 4
+    group = 16
     return pl.pallas_call(
         column_kernel,
         grid=(count // group,),

time: 167 us -> 165 us (0.988)
  Pallas kernels: 10.1 us -> 7.18 us
  transfers between devices with their start and end apart: 9 -> 9, of which waited for: 7 -> 7; matrix products, arithmetic and copies ran while one was open for 7% -> 7% of each run, Pallas kernels for 2% -> 1%
where the time goes in v7:
time: 165 us
  blocking collectives  80.5 us (49%)
  starting transfers between devices  27.7 us (17%)
  waiting for transfers between devices  27.3 us (17%)
  matrix products  9.09 us (6%)
  other arithmetic  8.54 us (5%)
  Pallas kernels  7.18 us (4%)
  local copies, waits for them, and re-layouts  3.44 us (2%)
    all_to_all x3, blocking collectives, swap(): return lax.all_to_all(blocks, axes, 0, 0, tiled=True)  74.7 us
    ppermute x6, starting transfers between devices, turns(): lax.ppermute(block, DEPTH, [(at, (at + shift) % count) for at in range(co...  16.9 us
    ppermute x6, waiting for transfers between devices, turns(): lax.ppermute(block, DEPTH, [(at, (at + shift) % count) for at in range(co...  14.5 us
    all_to_all x2, waiting for transfers between devices, swap(): return lax.all_to_all(blocks, axes, 0, 0, tiled=True)  11.1 us
    all_to_all x2, starting transfers between devices, swap(): return lax.all_to_all(blocks, axes, 0, 0, tiled=True)  10.8 us
    convert_element_type x2, other arithmetic, probe_signs(): return (1 - 2 * (hashed & 1)).astype(jnp.bfloat16)  7.03 us
    all_gather x1, blocking collectives, body(): lax.all_gather(share, TENSOR).astype(jnp.float32)  5.83 us
    dot_general x9, matrix products, dot_rows(): lax.dot_general(left, right, contract_rows, preferred_element_type=jnp.fl...  4.64 us
  transfers between devices with their start and end apart: 9, of which 7 were waited for; matrix products, arithmetic and copies ran while one was open for 7% of the time, Pallas kernels for 1%

profile of v7, /device:TPU:32, one launch (start us, length us, event | category | flops | bytes accessed | tf_op | source)
XLA Modules:
  0.0 164.9 jit_solution(14387515179292375661)
XLA Ops:
  0.6 2.4 %shard_map.145 = bf16[16,112,384]{2,1,0:T(8,128)(2,1)} custom-call(bf16[112,3584]{1,0:T(8,128)(2,1)} %weight_ref.1, f32[1,112]{1,0:T(1,128)} %bitcast.144, bf16[112,128]{1,0:T(8,128)(2,1)} %inputs_ref.1), custom_call_target="tpu_custom_call" | custom-call | bytes 2007040 | tf_op jit(solution)/shard_map/pallas_call | solution.py:161
  3.1 7.2 %all-to-all-start = ((bf16[16,112,384]{2,1,0:T(8,128)(2,1)}), bf16[16,112,384]{2,1,0:T(8,128)(2,1)S(1)}, u32[]{:S(2)}, u32[]{:S(2)}) async-start(bf16[16,112,384]{2,1,0:T(8,128)(2,1)} %shard_map.145), calls=%async_computation | async-start | bytes 2752512 | tf_op jit(solution)/shard_map/all_to_all | solution.py:111
  11.1 4.2 %subtract_convert_fusion = (bf16[1792,224]{1,0:T(8,128)(2,1)}, bf16[1792,224]{1,0:T(8,128)(2,1)}) fusion(s32[]{:T(128)} %bitcast.2, s32[224]{0:T(256)S(1)} %iota_add_fusion.1, s32[1792]{0:T(1024)S(1)} %mul.248, s32[]{:T(128)} %bitcast.1), kind=kLoop, calls=%fused_computation.29 | loop fusion | flops 13246464 | bytes 1613704 | tf_op jit(solution)/shard_map/convert_element_type | solution.py:36
  15.4 2.4 %shard_map.146 = bf16[16,112,256]{2,1,0:T(8,128)(2,1)} custom-call(bf16[112,3584]{1,0:T(8,128)(2,1)} %weight_ref.2), custom_call_target="tpu_custom_call" | custom-call | bytes 2007040 | tf_op jit(solution)/shard_map/pallas_call | solution.py:192
  18.0 2.8 %subtract_convert_fusion.2 = (bf16[112,3584]{1,0:T(8,128)(2,1)S(1)}, bf16[112,3584]{1,0:T(8,128)(2,1)S(1)}) fusion(s32[]{:T(128)} %bitcast.2, s32[3584]{0:T(1024)S(1)} %iota_add_fusion, s32[112]{0:T(128)S(1)} %add_multiply_fusion.2, s32[]{:T(128)} %bitcast.1), kind=kLoop, calls=%fused_computation.44 | loop fusion | flops 13246464 | bytes 1620424 | tf_op jit(solution)/shard_map/convert_element_type | solution.py:36
  20.9 11.1 %all-to-all-done = bf16[16,112,384]{2,1,0:T(8,128)(2,1)S(1)} async-done(((bf16[16,112,384]{2,1,0:T(8,128)(2,1)}), bf16[16,112,384]{2,1,0:T(8,128)(2,1)S(1)}, u32[]{:S(2)}, u32[]{:S(2)}) %all-to-all-start) | async-done | bytes 1376288 | tf_op jit(solution)/shard_map/all_to_all | solution.py:111
  35.6 3.6 %all-to-all-start.1 = ((bf16[16,112,256]{2,1,0:T(8,128)(2,1)}), bf16[16,112,256]{2,1,0:T(8,128)(2,1)S(1)}, u32[]{:S(2)}, u32[]{:S(2)}) async-start(bf16[16,112,256]{2,1,0:T(8,128)(2,1)} %shard_map.146), calls=%async_computation.1 | async-start | bytes 1835008 | tf_op jit(solution)/shard_map/all_to_all | solution.py:111
  39.2 5.5 %collective-permute-start.2 = (bf16[464,128]{1,0:T(8,128)(2,1)S(1)}, bf16[464,128]{1,0:T(8,128)(2,1)S(1)}, u32[]{:S(2)}, u32[]{:S(2)}) collective-permute-start(bf16[464,128]{1,0:T(8,128)(2,1)S(1)} %fusion.58), channel_id=1, source_target_pairs={{0,12},{4,0},{8,4},{12,8},{1,13},{5,1},{9,5},{13,9},{2,14},{6,2},{... | collective-permute-start | bytes 356360 | tf_op jit(solution)/shard_map/ppermute | solution.py:122
  44.7 1.4 collective-permute-start.1
  46.1 2.4 %collective-permute-start = (bf16[464,128]{1,0:T(8,128)(2,1)S(1)}, bf16[464,128]{1,0:T(8,128)(2,1)S(1)}, u32[]{:S(2)}, u32[]{:S(2)}) collective-permute-start(bf16[464,128]{1,0:T(8,128)(2,1)S(1)} %fusion.58), channel_id=1, source_target_pairs={{0,4},{4,8},{8,12},{12,0},{1,5},{5,9},{9,13},{13,1},{2,6},{6,10},{... | collective-permute-start | bytes 356360 | tf_op jit(solution)/shard_map/ppermute | solution.py:122
  48.5 1.1 collective-permute-done.2
  49.6 6.6 %collective-permute-done.1 = bf16[464,128]{1,0:T(8,128)(2,1)S(1)} collective-permute-done((bf16[464,128]{1,0:T(8,128)(2,1)S(1)}, bf16[464,128]{1,0:T(8,128)(2,1)S(1)}, u32[]{:S(2)}, u32[]{:S(2)}) %collective-permute-start.1) | collective-permute-done | bytes 118816 | tf_op jit(solution)/shard_map/ppermute | solution.py:122
  58.8 31.7 %all_to_all.25 = bf16[16,448,128]{2,1,0:T(8,128)(2,1)S(1)} all-to-all(bf16[16,448,128]{2,1,0:T(8,128)(2,1)S(1)} %broadcast_in_dim.9), channel_id=1, replica_groups=mesh['y'=4,'x'=4,'h'=4,'l'=2,'c'=2] {'y','x'}, dimensions={0} | all-to-all | bytes 3670016 | tf_op jit(solution)/shard_map/all_to_all | solution.py:111
  90.5 1.0 copy-done.2
  92.7 5.8 %all_gather.4 = bf16[4,2,112,128]{3,2,1,0:T(8,128)(2,1)S(1)} all-gather(bf16[1,2,112,128]{3,2,1,0:T(8,128)(2,1)S(1)} %pad_maximum_fusion.3), channel_id=1, replica_groups=mesh['y'=4,'x'=4,'h'=4,'l'=2,'c'=2] {'l','c'}, dimensions={0}, use_global_device_ids=true | all-gather | bytes 286720 | tf_op jit(solution)/shard_map/all_gather | solution.py:312
  98.7 14.2 %all_to_all.26 = bf16[16,112,128]{2,1,0:T(8,128)(2,1)S(1)} all-to-all(bf16[16,112,128]{2,1,0:T(8,128)(2,1)S(1)} %broadcast_in_dim.10), channel_id=1, replica_groups=mesh['y'=4,'x'=4,'h'=4,'l'=2,'c'=2] {'y','x'}, dimensions={0} | all-to-all | bytes 917504 | tf_op jit(solution)/shard_map/all_to_all | solution.py:111
  113.0 1.7 %collective-permute-done.3 = bf16[1792,128]{1,0:T(8,128)(2,1)S(1)} collective-permute-done((bf16[1792,128]{1,0:T(8,128)(2,1)S(1)}, bf16[1792,128]{1,0:T(8,128)(2,1)S(1)}, u32[]{:S(2)}, u32[]{:S(2)}) %collective-permute-start.3) | collective-permute-done | bytes 458784 | tf_op jit(solution)/shard_map/ppermute | solution.py:317
  116.1 4.1 %collective-permute-start.6 = (bf16[448,128]{1,0:T(8,128)(2,1)S(1)}, bf16[448,128]{1,0:T(8,128)(2,1)S(1)}, u32[]{:S(2)}, u32[]{:S(2)}) collective-permute-start(bf16[448,128]{1,0:T(8,128)(2,1)S(1)} %pad_maximum_fusion.1), channel_id=1, source_target_pairs={{0,12},{4,0},{8,4},{12,8},{1,13},{5,1},{9,5},{13,9},{2,14},{6,2},{... | collective-permute-start | bytes 344072 | tf_op jit(solution)/shard_map/ppermute | solution.py:122
  120.2 1.5 collective-permute-start.5
  121.7 2.0 %collective-permute-start.4 = (bf16[448,128]{1,0:T(8,128)(2,1)S(1)}, bf16[448,128]{1,0:T(8,128)(2,1)S(1)}, u32[]{:S(2)}, u32[]{:S(2)}) collective-permute-start(bf16[448,128]{1,0:T(8,128)(2,1)S(1)} %pad_maximum_fusion.1), channel_id=1, source_target_pairs={{0,4},{4,8},{8,12},{12,0},{1,5},{5,9},{9,13},{13,1},{2,6},{6,10},{... | collective-permute-start | bytes 344072 | tf_op jit(solution)/shard_map/ppermute | solution.py:122
  125.3 2.2 %clamp_convert_fusion = (bf16[112,3584]{1,0:T(8,128)(2,1)}, bf16[112,3584]{1,0:T(8,128)(2,1)}, bf16[112,3584]{1,0:T(8,128)(2,1)}) fusion(f32[112,3584]{1,0:T(8,128)S(1)} %fusion.1, bf16[112,128]{1,0:T(8,128)(2,1)S(1)} %get-tuple-element.62, bf16[3584,128]{1,0:T(8,128)(2,1)S(1)} %bitcast.134, bf16[112,3584]{1,0:T(8,128)(2,1)S(1)} %copy-done.9), kind=kOutput, calls=%fused_computation.43 | convolution fusion | flops 107175936 | bytes 5763072 | tf_op jit(solution)/shard_map/dot_general | solution.py:207
  127.4 4.8 %collective-permute-done.5 = bf16[448,128]{1,0:T(8,128)(2,1)S(1)} collective-permute-done((bf16[448,128]{1,0:T(8,128)(2,1)S(1)}, bf16[448,128]{1,0:T(8,128)(2,1)S(1)}, u32[]{:S(2)}, u32[]{:S(2)}) %collective-permute-start.5) | collective-permute-done | bytes 114720 | tf_op jit(solution)/shard_map/ppermute | solution.py:122
  133.8 28.8 %all_to_all.27.grads_ref = bf16[16,448,128]{2,1,0:T(8,128)(2,1)S(1)} all-to-all(bf16[16,448,128]{2,1,0:T(8,128)(2,1)S(1)} %broadcast_in_dim.11), channel_id=1, replica_groups=mesh['y'=4,'x'=4,'h'=4,'l'=2,'c'=2] {'y','x'}, dimensions={0} | all-to-all | bytes 3670016 | tf_op jit(solution)/shard_map/all_to_all | solution.py:111
  162.6 2.3 %shard_map.147 = (bf16[112,3584]{1,0:T(8,128)(2,1)}, bf16[112,3584]{1,0:T(8,128)(2,1)}, bf16[112,3584]{1,0:T(8,128)(2,1)}) custom-call(bf16[112,128]{1,0:T(8,128)(2,1)S(1)} %multiply_convert_fusion.3.normed_ref, bf16[16,448,128]{2,1,0:T(8,128)(2,1)S(1)} %all_to_all.27.grads_ref, bf16[112,3584]{1,0:T(8,128)(2,1)S(1)} %get-tuple-element.69.probe_ref, ...), custom_call_target="tpu_custom_call" | custom-call | flops 205520896 | bytes 6422528 | tf_op jit(solution)/shard_map/pallas_call | solution.py:91
  (93 shorter events, 12.8 us)
Async XLA Ops:
  3.1 7.4 %copy-start.8 = (s32[2]{0:T(128)S(1)}, s32[2]{0:T(128)}, u32[]{:S(2)}) copy-start(s32[2]{0:T(128)} %param.19) | copy-start | bytes 28
  3.1 28.9 %all-to-all-start = ((bf16[16,112,384]{2,1,0:T(8,128)(2,1)}), bf16[16,112,384]{2,1,0:T(8,128)(2,1)S(1)}, u32[]{:S(2)}, u32[]{:S(2)}) async-start(bf16[16,112,384]{2,1,0:T(8,128)(2,1)} %shard_map.145), calls=%async_computation | async-start | bytes 2752512 | tf_op jit(solution)/shard_map/all_to_all | solution.py:111
  10.2 5.0 %copy-start.10 = (s32[128]{0:T(128)S(1)}, s32[128]{0:T(128)}, u32[]{:S(2)}) copy-start(s32[128]{0:T(128)} %param.12) | copy-start | bytes 1540
  10.3 5.1 %copy-start.6 = (bf16[112,128]{1,0:T(8,128)(2,1)S(1)}, bf16[112,128]{1,0:T(8,128)(2,1)}, u32[]{:S(2)}) copy-start(bf16[112,128]{1,0:T(8,128)(2,1)} %inputs_ref.1) | copy-start | bytes 86020
  32.0 1.5 copy-start.3
  35.6 21.7 %all-to-all-start.1 = ((bf16[16,112,256]{2,1,0:T(8,128)(2,1)}), bf16[16,112,256]{2,1,0:T(8,128)(2,1)S(1)}, u32[]{:S(2)}, u32[]{:S(2)}) async-start(bf16[16,112,256]{2,1,0:T(8,128)(2,1)} %shard_map.146), calls=%async_computation.1 | async-start | bytes 1835008 | tf_op jit(solution)/shard_map/all_to_all | solution.py:111
  39.2 10.4 %collective-permute-start.2 = (bf16[464,128]{1,0:T(8,128)(2,1)S(1)}, bf16[464,128]{1,0:T(8,128)(2,1)S(1)}, u32[]{:S(2)}, u32[]{:S(2)}) collective-permute-start(bf16[464,128]{1,0:T(8,128)(2,1)S(1)} %fusion.58), channel_id=1, source_target_pairs={{0,12},{4,0},{8,4},{12,8},{1,13},{5,1},{9,5},{13,9},{2,14},{6,2},{... | collective-permute-start | bytes 356360 | tf_op jit(solution)/shard_map/ppermute | solution.py:122
  44.7 11.6 %collective-permute-start.1 = (bf16[464,128]{1,0:T(8,128)(2,1)S(1)}, bf16[464,128]{1,0:T(8,128)(2,1)S(1)}, u32[]{:S(2)}, u32[]{:S(2)}) collective-permute-start(bf16[464,128]{1,0:T(8,128)(2,1)S(1)} %fusion.58), channel_id=1, source_target_pairs={{0,8},{4,12},{8,0},{12,4},{1,9},{5,13},{9,1},{13,5},{2,10},{6,14},... | collective-permute-start | bytes 356360 | tf_op jit(solution)/shard_map/ppermute | solution.py:122
  46.1 11.1 %collective-permute-start = (bf16[464,128]{1,0:T(8,128)(2,1)S(1)}, bf16[464,128]{1,0:T(8,128)(2,1)S(1)}, u32[]{:S(2)}, u32[]{:S(2)}) collective-permute-start(bf16[464,128]{1,0:T(8,128)(2,1)S(1)} %fusion.58), channel_id=1, source_target_pairs={{0,4},{4,8},{8,12},{12,0},{1,5},{5,9},{9,13},{13,1},{2,6},{6,10},{... | collective-permute-start | bytes 356360 | tf_op jit(solution)/shard_map/ppermute | solution.py:122
  90.4 1.1 copy-start.2
  92.7 20.2 %copy-start.7 = (f32[112]{0:T(128)S(1)}, f32[112]{0:T(128)}, u32[]{:S(2)}) copy-start(f32[112]{0:T(128)} %param.11) | copy-start | bytes 1348
  92.7 22.0 %copy-start.4 = (bf16[1792,224]{1,0:T(8,128)(2,1)S(1)}, bf16[1792,224]{1,0:T(8,128)(2,1)}, u32[]{:S(2)}) copy-start(bf16[1792,224]{1,0:T(8,128)(2,1)} %get-tuple-element.60) | copy-start | bytes 2408452
  112.9 1.8 %collective-permute-start.3 = (bf16[1792,128]{1,0:T(8,128)(2,1)S(1)}, bf16[1792,128]{1,0:T(8,128)(2,1)S(1)}, u32[]{:S(2)}, u32[]{:S(2)}) collective-permute-start(bf16[1792,128]{1,0:T(8,128)(2,1)S(1)} %bitcast.137), channel_id=1, source_target_pairs={{0,1},{1,0},{2,3},{3,2},{4,5},{5,4},{6,7},{7,6},{8,9},{9,8},{10,11... | collective-permute-start | bytes 1376264 | tf_op jit(solution)/shard_map/ppermute | solution.py:317
  116.1 8.1 %copy-start.5 = (bf16[112,3584]{1,0:T(8,128)(2,1)S(1)}, bf16[112,3584]{1,0:T(8,128)(2,1)}, u32[]{:S(2)}) copy-start(bf16[112,3584]{1,0:T(8,128)(2,1)} %param.18) | copy-start | bytes 2408452
  116.1 11.4 %collective-permute-start.6 = (bf16[448,128]{1,0:T(8,128)(2,1)S(1)}, bf16[448,128]{1,0:T(8,128)(2,1)S(1)}, u32[]{:S(2)}, u32[]{:S(2)}) collective-permute-start(bf16[448,128]{1,0:T(8,128)(2,1)S(1)} %pad_maximum_fusion.1), channel_id=1, source_target_pairs={{0,12},{4,0},{8,4},{12,8},{1,13},{5,1},{9,5},{13,9},{2,14},{6,2},{... | collective-permute-start | bytes 344072 | tf_op jit(solution)/shard_map/ppermute | solution.py:122
  120.2 12.1 %collective-permute-start.5 = (bf16[448,128]{1,0:T(8,128)(2,1)S(1)}, bf16[448,128]{1,0:T(8,128)(2,1)S(1)}, u32[]{:S(2)}, u32[]{:S(2)}) collective-permute-start(bf16[448,128]{1,0:T(8,128)(2,1)S(1)} %pad_maximum_fusion.1), channel_id=1, source_target_pairs={{0,8},{4,12},{8,0},{12,4},{1,9},{5,13},{9,1},{13,5},{2,10},{6,14},... | collective-permute-start | bytes 344072 | tf_op jit(solution)/shard_map/ppermute | solution.py:122
  121.7 11.5 %collective-permute-start.4 = (bf16[448,128]{1,0:T(8,128)(2,1)S(1)}, bf16[448,128]{1,0:T(8,128)(2,1)S(1)}, u32[]{:S(2)}, u32[]{:S(2)}) collective-permute-start(bf16[448,128]{1,0:T(8,128)(2,1)S(1)} %pad_maximum_fusion.1), channel_id=1, source_target_pairs={{0,4},{4,8},{8,12},{12,0},{1,5},{5,9},{9,13},{13,1},{2,6},{6,10},{... | collective-permute-start | bytes 344072 | tf_op jit(solution)/shard_map/ppermute | solution.py:122
  124.1 1.1 copy-start.9
  133.7 28.8 %copy-start = (bf16[112,3584]{1,0:T(8,128)(2,1)S(1)}, bf16[112,3584]{1,0:T(8,128)(2,1)}, u32[]{:S(2)}) copy-start(bf16[112,3584]{1,0:T(8,128)(2,1)} %mom_ref.1) | copy-start | bytes 2408452
  133.7 28.8 %copy-start.1 = (bf16[112,3584]{1,0:T(8,128)(2,1)S(1)}, bf16[112,3584]{1,0:T(8,128)(2,1)}, u32[]{:S(2)}) copy-start(bf16[112,3584]{1,0:T(8,128)(2,1)} %hess_ref.1) | copy-start | bytes 2408452

commit v8 on v7

--- a/solution.py
+++ b/solution.py
@@ -120,7 +120,7 @@
     count = lax.axis_size(DEPTH)
     return [block] + [
         lax.ppermute(block, DEPTH, [(at, (at + shift) % count) for at in range(count)])
-        for shift in range(1, count)
+        for shift in sorted(range(1, count), key=lambda turn: -min(turn, count - turn))
     ]
 
 

time: 165 us -> 165 us (level); the launches traced: 165 us -> 161 us
  blocking collectives: 80.5 us -> 72.9 us
  waiting for transfers between devices: 27.3 us -> 30.4 us
    all_to_all x3, blocking collectives: 74.7 us -> 67.1 us  [swap(): return lax.all_to_all(blocks, axes, 0, 0, tiled=True)]
    ppermute x6, waiting for transfers between devices: 14.5 us -> 17.6 us  [turns(): lax.ppermute(block, DEPTH, [(at, (at + shift) % count) for at in range(co...]
  transfers between devices with their start and end apart: 9 -> 9, of which waited for: 7 -> 4; matrix products, arithmetic and copies ran while one was open for 7% -> 7% of each run, Pallas kernels for 1% -> 1%
where the time goes in v8:
time: 165 us; the launch traced here: 161 us
  blocking collectives  72.9 us (44%)
  waiting for transfers between devices  30.4 us (18%)
  starting transfers between devices  28.7 us (17%)
  matrix products  9.1 us (6%)
  other arithmetic  8.54 us (5%)
  Pallas kernels  7.18 us (4%)
  local copies, waits for them, and re-layouts  3.44 us (2%)
    all_to_all x3, blocking collectives, swap(): return lax.all_to_all(blocks, axes, 0, 0, tiled=True)  67.1 us
    ppermute x6, starting transfers between devices, turns(): lax.ppermute(block, DEPTH, [(at, (at + shift) % count) for at in range(co...  17.9 us
    ppermute x6, waiting for transfers between devices, turns(): lax.ppermute(block, DEPTH, [(at, (at + shift) % count) for at in range(co...  17.6 us
    all_to_all x2, waiting for transfers between devices, swap(): return lax.all_to_all(blocks, axes, 0, 0, tiled=True)  11.1 us
    all_to_all x2, starting transfers between devices, swap(): return lax.all_to_all(blocks, axes, 0, 0, tiled=True)  10.8 us
    convert_element_type x2, other arithmetic, probe_signs(): return (1 - 2 * (hashed & 1)).astype(jnp.bfloat16)  7.03 us
    all_gather x1, blocking collectives, body(): lax.all_gather(share, TENSOR).astype(jnp.float32)  5.83 us
    dot_general x9, matrix products, dot_rows(): lax.dot_general(left, right, contract_rows, preferred_element_type=jnp.fl...  4.64 us
  transfers between devices with their start and end apart: 9, of which 4 were waited for; matrix products, arithmetic and copies ran while one was open for 7% of the time, Pallas kernels for 1%

profile of v8, /device:TPU:32, one launch (start us, length us, event | category | flops | bytes accessed | tf_op | source)
XLA Modules:
  0.0 161.4 jit_solution(10233336409674441754)
XLA Ops:
  0.6 2.4 %shard_map.145 = bf16[16,112,384]{2,1,0:T(8,128)(2,1)} custom-call(bf16[112,3584]{1,0:T(8,128)(2,1)} %weight_ref.1, f32[1,112]{1,0:T(1,128)} %bitcast.144, bf16[112,128]{1,0:T(8,128)(2,1)} %inputs_ref.1), custom_call_target="tpu_custom_call" | custom-call | bytes 2007040 | tf_op jit(solution)/shard_map/pallas_call | solution.py:161
  3.1 7.2 %all-to-all-start = ((bf16[16,112,384]{2,1,0:T(8,128)(2,1)}), bf16[16,112,384]{2,1,0:T(8,128)(2,1)S(1)}, u32[]{:S(2)}, u32[]{:S(2)}) async-start(bf16[16,112,384]{2,1,0:T(8,128)(2,1)} %shard_map.145), calls=%async_computation | async-start | bytes 2752512 | tf_op jit(solution)/shard_map/all_to_all | solution.py:111
  10.5 0.6 fusion.100
  11.1 4.2 %subtract_convert_fusion = (bf16[1792,224]{1,0:T(8,128)(2,1)}, bf16[1792,224]{1,0:T(8,128)(2,1)}) fusion(s32[]{:T(128)} %bitcast.2, s32[224]{0:T(256)S(1)} %iota_add_fusion.1, s32[1792]{0:T(1024)S(1)} %mul.248, s32[]{:T(128)} %bitcast.1), kind=kLoop, calls=%fused_computation.29 | loop fusion | flops 13246464 | bytes 1613704 | tf_op jit(solution)/shard_map/convert_element_type | solution.py:36
  15.4 2.4 %shard_map.146 = bf16[16,112,256]{2,1,0:T(8,128)(2,1)} custom-call(bf16[112,3584]{1,0:T(8,128)(2,1)} %weight_ref.2), custom_call_target="tpu_custom_call" | custom-call | bytes 2007040 | tf_op jit(solution)/shard_map/pallas_call | solution.py:192
  18.0 2.8 %subtract_convert_fusion.2 = (bf16[112,3584]{1,0:T(8,128)(2,1)S(1)}, bf16[112,3584]{1,0:T(8,128)(2,1)S(1)}) fusion(s32[]{:T(128)} %bitcast.2, s32[3584]{0:T(1024)S(1)} %iota_add_fusion, s32[112]{0:T(128)S(1)} %add_multiply_fusion.2, s32[]{:T(128)} %bitcast.1), kind=kLoop, calls=%fused_computation.44 | loop fusion | flops 13246464 | bytes 1620424 | tf_op jit(solution)/shard_map/convert_element_type | solution.py:36
  20.9 11.1 %all-to-all-done = bf16[16,112,384]{2,1,0:T(8,128)(2,1)S(1)} async-done(((bf16[16,112,384]{2,1,0:T(8,128)(2,1)}), bf16[16,112,384]{2,1,0:T(8,128)(2,1)S(1)}, u32[]{:S(2)}, u32[]{:S(2)}) %all-to-all-start) | async-done | bytes 1376288 | tf_op jit(solution)/shard_map/all_to_all | solution.py:111
  34.0 0.7 convolution_convert_fusion.1
  34.7 0.7 convolution_convert_fusion.2
  35.6 3.6 %all-to-all-start.1 = ((bf16[16,112,256]{2,1,0:T(8,128)(2,1)}), bf16[16,112,256]{2,1,0:T(8,128)(2,1)S(1)}, u32[]{:S(2)}, u32[]{:S(2)}) async-start(bf16[16,112,256]{2,1,0:T(8,128)(2,1)} %shard_map.146), calls=%async_computation.1 | async-start | bytes 1835008 | tf_op jit(solution)/shard_map/all_to_all | solution.py:111
  39.2 5.5 %collective-permute-start.2 = (bf16[464,128]{1,0:T(8,128)(2,1)S(1)}, bf16[464,128]{1,0:T(8,128)(2,1)S(1)}, u32[]{:S(2)}, u32[]{:S(2)}) collective-permute-start(bf16[464,128]{1,0:T(8,128)(2,1)S(1)} %fusion.58), channel_id=1, source_target_pairs={{0,12},{4,0},{8,4},{12,8},{1,13},{5,1},{9,5},{13,9},{2,14},{6,2},{... | collective-permute-start | bytes 356360 | tf_op jit(solution)/shard_map/ppermute | solution.py:122
  44.7 3.8 %collective-permute-start = (bf16[464,128]{1,0:T(8,128)(2,1)S(1)}, bf16[464,128]{1,0:T(8,128)(2,1)S(1)}, u32[]{:S(2)}, u32[]{:S(2)}) collective-permute-start(bf16[464,128]{1,0:T(8,128)(2,1)S(1)} %fusion.58), channel_id=1, source_target_pairs={{0,8},{4,12},{8,0},{12,4},{1,9},{5,13},{9,1},{13,5},{2,10},{6,14},... | collective-permute-start | bytes 356360 | tf_op jit(solution)/shard_map/ppermute | solution.py:122
  48.5 10.1 %collective-permute-done.1 = bf16[464,128]{1,0:T(8,128)(2,1)S(1)} collective-permute-done((bf16[464,128]{1,0:T(8,128)(2,1)S(1)}, bf16[464,128]{1,0:T(8,128)(2,1)S(1)}, u32[]{:S(2)}, u32[]{:S(2)}) %collective-permute-start.1) | collective-permute-done | bytes 118816 | tf_op jit(solution)/shard_map/ppermute | solution.py:122
  60.1 27.7 %all_to_all.25 = bf16[16,448,128]{2,1,0:T(8,128)(2,1)S(1)} all-to-all(bf16[16,448,128]{2,1,0:T(8,128)(2,1)S(1)} %broadcast_in_dim.9), channel_id=1, replica_groups=mesh['y'=4,'x'=4,'h'=4,'l'=2,'c'=2] {'y','x'}, dimensions={0} | all-to-all | bytes 3670016 | tf_op jit(solution)/shard_map/all_to_all | solution.py:111
  88.0 1.0 copy-done.2
  90.2 5.8 %all_gather.4 = bf16[4,2,112,128]{3,2,1,0:T(8,128)(2,1)S(1)} all-gather(bf16[1,2,112,128]{3,2,1,0:T(8,128)(2,1)S(1)} %pad_maximum_fusion.3), channel_id=1, replica_groups=mesh['y'=4,'x'=4,'h'=4,'l'=2,'c'=2] {'l','c'}, dimensions={0}, use_global_device_ids=true | all-gather | bytes 286720 | tf_op jit(solution)/shard_map/all_gather | solution.py:312
  96.1 14.2 %all_to_all.26 = bf16[16,112,128]{2,1,0:T(8,128)(2,1)S(1)} all-to-all(bf16[16,112,128]{2,1,0:T(8,128)(2,1)S(1)} %broadcast_in_dim.10), channel_id=1, replica_groups=mesh['y'=4,'x'=4,'h'=4,'l'=2,'c'=2] {'y','x'}, dimensions={0} | all-to-all | bytes 917504 | tf_op jit(solution)/shard_map/all_to_all | solution.py:111
  110.5 1.7 %collective-permute-done.3 = bf16[1792,128]{1,0:T(8,128)(2,1)S(1)} collective-permute-done((bf16[1792,128]{1,0:T(8,128)(2,1)S(1)}, bf16[1792,128]{1,0:T(8,128)(2,1)S(1)}, u32[]{:S(2)}, u32[]{:S(2)}) %collective-permute-start.3) | collective-permute-done | bytes 458784 | tf_op jit(solution)/shard_map/ppermute | solution.py:317
  113.5 5.4 %collective-permute-start.6 = (bf16[448,128]{1,0:T(8,128)(2,1)S(1)}, bf16[448,128]{1,0:T(8,128)(2,1)S(1)}, u32[]{:S(2)}, u32[]{:S(2)}) collective-permute-start(bf16[448,128]{1,0:T(8,128)(2,1)S(1)} %pad_maximum_fusion.1), channel_id=1, source_target_pairs={{0,12},{4,0},{8,4},{12,8},{1,13},{5,1},{9,5},{13,9},{2,14},{6,2},{... | collective-permute-start | bytes 344072 | tf_op jit(solution)/shard_map/ppermute | solution.py:122
  118.9 3.2 %collective-permute-start.4 = (bf16[448,128]{1,0:T(8,128)(2,1)S(1)}, bf16[448,128]{1,0:T(8,128)(2,1)S(1)}, u32[]{:S(2)}, u32[]{:S(2)}) collective-permute-start(bf16[448,128]{1,0:T(8,128)(2,1)S(1)} %pad_maximum_fusion.1), channel_id=1, source_target_pairs={{0,8},{4,12},{8,0},{12,4},{1,9},{5,13},{9,1},{13,5},{2,10},{6,14},... | collective-permute-start | bytes 344072 | tf_op jit(solution)/shard_map/ppermute | solution.py:122
  123.6 2.2 %clamp_convert_fusion = (bf16[112,3584]{1,0:T(8,128)(2,1)}, bf16[112,3584]{1,0:T(8,128)(2,1)}, bf16[112,3584]{1,0:T(8,128)(2,1)}) fusion(f32[112,3584]{1,0:T(8,128)S(1)} %fusion.1, bf16[112,128]{1,0:T(8,128)(2,1)S(1)} %get-tuple-element.62, bf16[3584,128]{1,0:T(8,128)(2,1)S(1)} %bitcast.134, bf16[112,3584]{1,0:T(8,128)(2,1)S(1)} %copy-done.9), kind=kOutput, calls=%fused_computation.43 | convolution fusion | flops 107175936 | bytes 5763072 | tf_op jit(solution)/shard_map/dot_general | solution.py:207
  125.8 7.5 %collective-permute-done.5 = bf16[448,128]{1,0:T(8,128)(2,1)S(1)} collective-permute-done((bf16[448,128]{1,0:T(8,128)(2,1)S(1)}, bf16[448,128]{1,0:T(8,128)(2,1)S(1)}, u32[]{:S(2)}, u32[]{:S(2)}) %collective-permute-start.5) | collective-permute-done | bytes 114720 | tf_op jit(solution)/shard_map/ppermute | solution.py:122
  133.9 25.2 %all_to_all.27.grads_ref = bf16[16,448,128]{2,1,0:T(8,128)(2,1)S(1)} all-to-all(bf16[16,448,128]{2,1,0:T(8,128)(2,1)S(1)} %broadcast_in_dim.11), channel_id=1, replica_groups=mesh['y'=4,'x'=4,'h'=4,'l'=2,'c'=2] {'y','x'}, dimensions={0} | all-to-all | bytes 3670016 | tf_op jit(solution)/shard_map/all_to_all | solution.py:111
  159.0 2.3 %shard_map.147 = (bf16[112,3584]{1,0:T(8,128)(2,1)}, bf16[112,3584]{1,0:T(8,128)(2,1)}, bf16[112,3584]{1,0:T(8,128)(2,1)}) custom-call(bf16[112,128]{1,0:T(8,128)(2,1)S(1)} %multiply_convert_fusion.3.normed_ref, bf16[16,448,128]{2,1,0:T(8,128)(2,1)S(1)} %all_to_all.27.grads_ref, bf16[112,3584]{1,0:T(8,128)(2,1)S(1)} %get-tuple-element.69.probe_ref, ...), custom_call_target="tpu_custom_call" | custom-call | flops 205520896 | bytes 6422528 | tf_op jit(solution)/shard_map/pallas_call | solution.py:91
  (93 shorter events, 8.8 us)
Async XLA Ops:
  3.1 7.4 %copy-start.8 = (s32[2]{0:T(128)S(1)}, s32[2]{0:T(128)}, u32[]{:S(2)}) copy-start(s32[2]{0:T(128)} %param.19) | copy-start | bytes 28
  3.1 28.9 %all-to-all-start = ((bf16[16,112,384]{2,1,0:T(8,128)(2,1)}), bf16[16,112,384]{2,1,0:T(8,128)(2,1)S(1)}, u32[]{:S(2)}, u32[]{:S(2)}) async-start(bf16[16,112,384]{2,1,0:T(8,128)(2,1)} %shard_map.145), calls=%async_computation | async-start | bytes 2752512 | tf_op jit(solution)/shard_map/all_to_all | solution.py:111
  10.2 5.0 %copy-start.10 = (s32[128]{0:T(128)S(1)}, s32[128]{0:T(128)}, u32[]{:S(2)}) copy-start(s32[128]{0:T(128)} %param.12) | copy-start | bytes 1540
  10.3 5.1 %copy-start.6 = (bf16[112,128]{1,0:T(8,128)(2,1)S(1)}, bf16[112,128]{1,0:T(8,128)(2,1)}, u32[]{:S(2)}) copy-start(bf16[112,128]{1,0:T(8,128)(2,1)} %inputs_ref.1) | copy-start | bytes 86020
  32.0 1.5 copy-start.3
  35.6 23.0 %all-to-all-start.1 = ((bf16[16,112,256]{2,1,0:T(8,128)(2,1)}), bf16[16,112,256]{2,1,0:T(8,128)(2,1)S(1)}, u32[]{:S(2)}, u32[]{:S(2)}) async-start(bf16[16,112,256]{2,1,0:T(8,128)(2,1)} %shard_map.146), calls=%async_computation.1 | async-start | bytes 1835008 | tf_op jit(solution)/shard_map/all_to_all | solution.py:111
  39.2 9.3 %collective-permute-start.2 = (bf16[464,128]{1,0:T(8,128)(2,1)S(1)}, bf16[464,128]{1,0:T(8,128)(2,1)S(1)}, u32[]{:S(2)}, u32[]{:S(2)}) collective-permute-start(bf16[464,128]{1,0:T(8,128)(2,1)S(1)} %fusion.58), channel_id=1, source_target_pairs={{0,12},{4,0},{8,4},{12,8},{1,13},{5,1},{9,5},{13,9},{2,14},{6,2},{... | collective-permute-start | bytes 356360 | tf_op jit(solution)/shard_map/ppermute | solution.py:122
  44.7 13.9 %collective-permute-start.1 = (bf16[464,128]{1,0:T(8,128)(2,1)S(1)}, bf16[464,128]{1,0:T(8,128)(2,1)S(1)}, u32[]{:S(2)}, u32[]{:S(2)}) collective-permute-start(bf16[464,128]{1,0:T(8,128)(2,1)S(1)} %fusion.58), channel_id=1, source_target_pairs={{0,4},{4,8},{8,12},{12,0},{1,5},{5,9},{9,13},{13,1},{2,6},{6,10},{... | collective-permute-start | bytes 356360 | tf_op jit(solution)/shard_map/ppermute | solution.py:122
  44.7 13.9 %collective-permute-start = (bf16[464,128]{1,0:T(8,128)(2,1)S(1)}, bf16[464,128]{1,0:T(8,128)(2,1)S(1)}, u32[]{:S(2)}, u32[]{:S(2)}) collective-permute-start(bf16[464,128]{1,0:T(8,128)(2,1)S(1)} %fusion.58), channel_id=1, source_target_pairs={{0,8},{4,12},{8,0},{12,4},{1,9},{5,13},{9,1},{13,5},{2,10},{6,14},... | collective-permute-start | bytes 356360 | tf_op jit(solution)/shard_map/ppermute | solution.py:122
  87.9 1.1 copy-start.2
  90.1 20.2 %copy-start.7 = (f32[112]{0:T(128)S(1)}, f32[112]{0:T(128)}, u32[]{:S(2)}) copy-start(f32[112]{0:T(128)} %param.11) | copy-start | bytes 1348
  90.2 22.0 %copy-start.4 = (bf16[1792,224]{1,0:T(8,128)(2,1)S(1)}, bf16[1792,224]{1,0:T(8,128)(2,1)}, u32[]{:S(2)}) copy-start(bf16[1792,224]{1,0:T(8,128)(2,1)} %get-tuple-element.60) | copy-start | bytes 2408452
  110.4 1.8 %collective-permute-start.3 = (bf16[1792,128]{1,0:T(8,128)(2,1)S(1)}, bf16[1792,128]{1,0:T(8,128)(2,1)S(1)}, u32[]{:S(2)}, u32[]{:S(2)}) collective-permute-start(bf16[1792,128]{1,0:T(8,128)(2,1)S(1)} %bitcast.137), channel_id=1, source_target_pairs={{0,1},{1,0},{2,3},{3,2},{4,5},{5,4},{6,7},{7,6},{8,9},{9,8},{10,11... | collective-permute-start | bytes 1376264 | tf_op jit(solution)/shard_map/ppermute | solution.py:317
  113.5 9.0 %copy-start.5 = (bf16[112,3584]{1,0:T(8,128)(2,1)S(1)}, bf16[112,3584]{1,0:T(8,128)(2,1)}, u32[]{:S(2)}) copy-start(bf16[112,3584]{1,0:T(8,128)(2,1)} %param.18) | copy-start | bytes 2408452
  113.5 12.3 %collective-permute-start.6 = (bf16[448,128]{1,0:T(8,128)(2,1)S(1)}, bf16[448,128]{1,0:T(8,128)(2,1)S(1)}, u32[]{:S(2)}, u32[]{:S(2)}) collective-permute-start(bf16[448,128]{1,0:T(8,128)(2,1)S(1)} %pad_maximum_fusion.1), channel_id=1, source_target_pairs={{0,12},{4,0},{8,4},{12,8},{1,13},{5,1},{9,5},{13,9},{2,14},{6,2},{... | collective-permute-start | bytes 344072 | tf_op jit(solution)/shard_map/ppermute | solution.py:122
  118.9 14.4 %collective-permute-start.5 = (bf16[448,128]{1,0:T(8,128)(2,1)S(1)}, bf16[448,128]{1,0:T(8,128)(2,1)S(1)}, u32[]{:S(2)}, u32[]{:S(2)}) collective-permute-start(bf16[448,128]{1,0:T(8,128)(2,1)S(1)} %pad_maximum_fusion.1), channel_id=1, source_target_pairs={{0,4},{4,8},{8,12},{12,0},{1,5},{5,9},{9,13},{13,1},{2,6},{6,10},{... | collective-permute-start | bytes 344072 | tf_op jit(solution)/shard_map/ppermute | solution.py:122
  118.9 14.4 %collective-permute-start.4 = (bf16[448,128]{1,0:T(8,128)(2,1)S(1)}, bf16[448,128]{1,0:T(8,128)(2,1)S(1)}, u32[]{:S(2)}, u32[]{:S(2)}) collective-permute-start(bf16[448,128]{1,0:T(8,128)(2,1)S(1)} %pad_maximum_fusion.1), channel_id=1, source_target_pairs={{0,8},{4,12},{8,0},{12,4},{1,9},{5,13},{9,1},{13,5},{2,10},{6,14},... | collective-permute-start | bytes 344072 | tf_op jit(solution)/shard_map/ppermute | solution.py:122
  122.5 1.1 copy-start.9
  133.8 25.2 %copy-start = (bf16[112,3584]{1,0:T(8,128)(2,1)S(1)}, bf16[112,3584]{1,0:T(8,128)(2,1)}, u32[]{:S(2)}) copy-start(bf16[112,3584]{1,0:T(8,128)(2,1)} %mom_ref.1) | copy-start | bytes 2408452
  133.9 25.2 %copy-start.1 = (bf16[112,3584]{1,0:T(8,128)(2,1)S(1)}, bf16[112,3584]{1,0:T(8,128)(2,1)}, u32[]{:S(2)}) copy-start(bf16[112,3584]{1,0:T(8,128)(2,1)} %hess_ref.1) | copy-start | bytes 2408452

commit v9 on v8

--- a/solution.py
+++ b/solution.py
@@ -316,11 +316,11 @@
     held = spread(jnp.where(first_core, cotangent, cotangent_dot), PLANE).reshape(plane_rows, length)
     other = lax.ppermute(held, CORE, [(0, 1), (1, 0)])
     plane_cot = jnp.where(first_core, held, other)
-    plane_cot_dot = jnp.where(first_core, other, held)
+    from_held, from_other = dot_rows(plane_out, held), dot_rows(plane_out, other)
     own = jnp.concatenate(
         [
-            dot_rows(plane_out, plane_cot),
-            dot_rows(plane_out, plane_cot_dot) + dot_rows(plane_probe_out, plane_cot),
+            jnp.where(first_core, from_held, from_other),
+            jnp.where(first_core, from_other, from_held) + dot_rows(plane_probe_out, plane_cot),
         ],
         axis=0,
     ).astype(jnp.bfloat16)

time: 165 us -> 165 us (level)
  no operation moved by 1% of the time
where the time goes in v9:
time: 165 us; the launch traced here: 162 us
  blocking collectives  72.8 us (44%)
  waiting for transfers between devices  30.5 us (18%)
  starting transfers between devices  28.6 us (17%)
  matrix products  9.09 us (6%)
  other arithmetic  8.55 us (5%)
  Pallas kernels  7.18 us (4%)
  local copies, waits for them, and re-layouts  3.74 us (2%)
    all_to_all x3, blocking collectives, swap(): return lax.all_to_all(blocks, axes, 0, 0, tiled=True)  67.1 us
    ppermute x6, starting transfers between devices, turns(): lax.ppermute(block, DEPTH, [(at, (at + shift) % count) for at in range(co...  17.8 us
    ppermute x6, waiting for transfers between devices, turns(): lax.ppermute(block, DEPTH, [(at, (at + shift) % count) for at in range(co...  17.6 us
    all_to_all x2, waiting for transfers between devices, swap(): return lax.all_to_all(blocks, axes, 0, 0, tiled=True)  11.1 us
    all_to_all x2, starting transfers between devices, swap(): return lax.all_to_all(blocks, axes, 0, 0, tiled=True)  10.8 us
    convert_element_type x2, other arithmetic, probe_signs(): return (1 - 2 * (hashed & 1)).astype(jnp.bfloat16)  7.04 us
    all_gather x1, blocking collectives, body(): lax.all_gather(share, TENSOR).astype(jnp.float32)  5.7 us
    dot_general x9, matrix products, dot_rows(): lax.dot_general(left, right, contract_rows, preferred_element_type=jnp.fl...  4.64 us
  transfers between devices with their start and end apart: 9, of which 4 were waited for; matrix products, arithmetic and copies ran while one was open for 7% of the time, Pallas kernels for 1%

profile of v9, /device:TPU:32, one launch (start us, length us, event | category | flops | bytes accessed | tf_op | source)
XLA Modules:
  0.0 161.5 jit_solution(1550474849896204288)
XLA Ops:
  0.6 2.4 %shard_map.145 = bf16[16,112,384]{2,1,0:T(8,128)(2,1)} custom-call(bf16[112,3584]{1,0:T(8,128)(2,1)} %weight_ref.1, f32[1,112]{1,0:T(1,128)} %bitcast.145, bf16[112,128]{1,0:T(8,128)(2,1)} %inputs_ref.1), custom_call_target="tpu_custom_call" | custom-call | bytes 2007040 | tf_op jit(solution)/shard_map/pallas_call | solution.py:161
  3.1 7.2 %all-to-all-start = ((bf16[16,112,384]{2,1,0:T(8,128)(2,1)}), bf16[16,112,384]{2,1,0:T(8,128)(2,1)S(1)}, u32[]{:S(2)}, u32[]{:S(2)}) async-start(bf16[16,112,384]{2,1,0:T(8,128)(2,1)} %shard_map.145), calls=%async_computation | async-start | bytes 2752512 | tf_op jit(solution)/shard_map/all_to_all | solution.py:111
  10.5 0.6 fusion.101
  11.1 4.2 %subtract_convert_fusion = (bf16[1792,224]{1,0:T(8,128)(2,1)}, bf16[1792,224]{1,0:T(8,128)(2,1)}) fusion(s32[]{:T(128)} %bitcast.2, s32[224]{0:T(256)S(1)} %iota_add_fusion.1, s32[1792]{0:T(1024)S(1)} %mul.248, s32[]{:T(128)} %bitcast.1), kind=kLoop, calls=%fused_computation.29 | loop fusion | flops 13246464 | bytes 1613704 | tf_op jit(solution)/shard_map/convert_element_type | solution.py:36
  15.4 2.4 %shard_map.146 = bf16[16,112,256]{2,1,0:T(8,128)(2,1)} custom-call(bf16[112,3584]{1,0:T(8,128)(2,1)} %weight_ref.2), custom_call_target="tpu_custom_call" | custom-call | bytes 2007040 | tf_op jit(solution)/shard_map/pallas_call | solution.py:192
  18.0 2.8 %subtract_convert_fusion.2 = (bf16[112,3584]{1,0:T(8,128)(2,1)S(1)}, bf16[112,3584]{1,0:T(8,128)(2,1)S(1)}) fusion(s32[]{:T(128)} %bitcast.2, s32[3584]{0:T(1024)S(1)} %iota_add_fusion, s32[112]{0:T(128)S(1)} %add_multiply_fusion.2, s32[]{:T(128)} %bitcast.1), kind=kLoop, calls=%fused_computation.44 | loop fusion | flops 13246464 | bytes 1620424 | tf_op jit(solution)/shard_map/convert_element_type | solution.py:36
  20.9 11.1 %all-to-all-done = bf16[16,112,384]{2,1,0:T(8,128)(2,1)S(1)} async-done(((bf16[16,112,384]{2,1,0:T(8,128)(2,1)}), bf16[16,112,384]{2,1,0:T(8,128)(2,1)S(1)}, u32[]{:S(2)}, u32[]{:S(2)}) %all-to-all-start) | async-done | bytes 1376288 | tf_op jit(solution)/shard_map/all_to_all | solution.py:111
  34.0 0.7 convolution_convert_fusion
  34.7 0.7 convolution_convert_fusion.1
  35.6 3.6 %all-to-all-start.1 = ((bf16[16,112,256]{2,1,0:T(8,128)(2,1)}), bf16[16,112,256]{2,1,0:T(8,128)(2,1)S(1)}, u32[]{:S(2)}, u32[]{:S(2)}) async-start(bf16[16,112,256]{2,1,0:T(8,128)(2,1)} %shard_map.146), calls=%async_computation.1 | async-start | bytes 1835008 | tf_op jit(solution)/shard_map/all_to_all | solution.py:111
  39.2 5.5 %collective-permute-start.2 = (bf16[464,128]{1,0:T(8,128)(2,1)S(1)}, bf16[464,128]{1,0:T(8,128)(2,1)S(1)}, u32[]{:S(2)}, u32[]{:S(2)}) collective-permute-start(bf16[464,128]{1,0:T(8,128)(2,1)S(1)} %fusion.59), channel_id=1, source_target_pairs={{0,12},{4,0},{8,4},{12,8},{1,13},{5,1},{9,5},{13,9},{2,14},{6,2},{... | collective-permute-start | bytes 356360 | tf_op jit(solution)/shard_map/ppermute | solution.py:122
  44.7 3.8 %collective-permute-start = (bf16[464,128]{1,0:T(8,128)(2,1)S(1)}, bf16[464,128]{1,0:T(8,128)(2,1)S(1)}, u32[]{:S(2)}, u32[]{:S(2)}) collective-permute-start(bf16[464,128]{1,0:T(8,128)(2,1)S(1)} %fusion.59), channel_id=1, source_target_pairs={{0,8},{4,12},{8,0},{12,4},{1,9},{5,13},{9,1},{13,5},{2,10},{6,14},... | collective-permute-start | bytes 356360 | tf_op jit(solution)/shard_map/ppermute | solution.py:122
  48.5 10.1 %collective-permute-done.1 = bf16[464,128]{1,0:T(8,128)(2,1)S(1)} collective-permute-done((bf16[464,128]{1,0:T(8,128)(2,1)S(1)}, bf16[464,128]{1,0:T(8,128)(2,1)S(1)}, u32[]{:S(2)}, u32[]{:S(2)}) %collective-permute-start.1) | collective-permute-done | bytes 118816 | tf_op jit(solution)/shard_map/ppermute | solution.py:122
  60.1 27.7 %all_to_all.25 = bf16[16,448,128]{2,1,0:T(8,128)(2,1)S(1)} all-to-all(bf16[16,448,128]{2,1,0:T(8,128)(2,1)S(1)} %broadcast_in_dim.9), channel_id=1, replica_groups=mesh['y'=4,'x'=4,'h'=4,'l'=2,'c'=2] {'y','x'}, dimensions={0} | all-to-all | bytes 3670016 | tf_op jit(solution)/shard_map/all_to_all | solution.py:111
  88.0 1.0 copy-done.2
  90.2 5.7 %all_gather.4 = bf16[4,2,112,128]{3,2,1,0:T(8,128)(2,1)S(1)} all-gather(bf16[1,2,112,128]{3,2,1,0:T(8,128)(2,1)S(1)} %pad_maximum_fusion.3), channel_id=1, replica_groups=mesh['y'=4,'x'=4,'h'=4,'l'=2,'c'=2] {'l','c'}, dimensions={0}, use_global_device_ids=true | all-gather | bytes 286720 | tf_op jit(solution)/shard_map/all_gather | solution.py:312
  96.0 14.2 %all_to_all.26 = bf16[16,112,128]{2,1,0:T(8,128)(2,1)S(1)} all-to-all(bf16[16,112,128]{2,1,0:T(8,128)(2,1)S(1)} %broadcast_in_dim.10), channel_id=1, replica_groups=mesh['y'=4,'x'=4,'h'=4,'l'=2,'c'=2] {'y','x'}, dimensions={0} | all-to-all | bytes 917504 | tf_op jit(solution)/shard_map/all_to_all | solution.py:111
  110.3 1.7 %collective-permute-done.3 = bf16[1792,128]{1,0:T(8,128)(2,1)S(1)} collective-permute-done((bf16[1792,128]{1,0:T(8,128)(2,1)S(1)}, bf16[1792,128]{1,0:T(8,128)(2,1)S(1)}, u32[]{:S(2)}, u32[]{:S(2)}) %collective-permute-start.3) | collective-permute-done | bytes 458784 | tf_op jit(solution)/shard_map/ppermute | solution.py:317
  113.7 5.4 %collective-permute-start.6 = (bf16[448,128]{1,0:T(8,128)(2,1)S(1)}, bf16[448,128]{1,0:T(8,128)(2,1)S(1)}, u32[]{:S(2)}, u32[]{:S(2)}) collective-permute-start(bf16[448,128]{1,0:T(8,128)(2,1)S(1)} %pad_maximum_fusion.1), channel_id=1, source_target_pairs={{0,12},{4,0},{8,4},{12,8},{1,13},{5,1},{9,5},{13,9},{2,14},{6,2},{... | collective-permute-start | bytes 344072 | tf_op jit(solution)/shard_map/ppermute | solution.py:122
  119.1 3.1 %collective-permute-start.4 = (bf16[448,128]{1,0:T(8,128)(2,1)S(1)}, bf16[448,128]{1,0:T(8,128)(2,1)S(1)}, u32[]{:S(2)}, u32[]{:S(2)}) collective-permute-start(bf16[448,128]{1,0:T(8,128)(2,1)S(1)} %pad_maximum_fusion.1), channel_id=1, source_target_pairs={{0,8},{4,12},{8,0},{12,4},{1,9},{5,13},{9,1},{13,5},{2,10},{6,14},... | collective-permute-start | bytes 344072 | tf_op jit(solution)/shard_map/ppermute | solution.py:122
  123.8 2.2 %clamp_convert_fusion = (bf16[112,3584]{1,0:T(8,128)(2,1)}, bf16[112,3584]{1,0:T(8,128)(2,1)}, bf16[112,3584]{1,0:T(8,128)(2,1)}) fusion(f32[112,3584]{1,0:T(8,128)S(1)} %fusion.1, bf16[112,128]{1,0:T(8,128)(2,1)S(1)} %get-tuple-element.62, bf16[3584,128]{1,0:T(8,128)(2,1)S(1)} %bitcast.136, bf16[112,3584]{1,0:T(8,128)(2,1)S(1)} %copy-done.9), kind=kOutput, calls=%fused_computation.43 | convolution fusion | flops 107175936 | bytes 5763072 | tf_op jit(solution)/shard_map/dot_general | solution.py:207
  126.0 7.5 %collective-permute-done.5 = bf16[448,128]{1,0:T(8,128)(2,1)S(1)} collective-permute-done((bf16[448,128]{1,0:T(8,128)(2,1)S(1)}, bf16[448,128]{1,0:T(8,128)(2,1)S(1)}, u32[]{:S(2)}, u32[]{:S(2)}) %collective-permute-start.5) | collective-permute-done | bytes 114720 | tf_op jit(solution)/shard_map/ppermute | solution.py:122
  134.0 25.1 %all_to_all.27.grads_ref = bf16[16,448,128]{2,1,0:T(8,128)(2,1)S(1)} all-to-all(bf16[16,448,128]{2,1,0:T(8,128)(2,1)S(1)} %broadcast_in_dim.11), channel_id=1, replica_groups=mesh['y'=4,'x'=4,'h'=4,'l'=2,'c'=2] {'y','x'}, dimensions={0} | all-to-all | bytes 3670016 | tf_op jit(solution)/shard_map/all_to_all | solution.py:111
  159.2 2.4 %shard_map.147 = (bf16[112,3584]{1,0:T(8,128)(2,1)}, bf16[112,3584]{1,0:T(8,128)(2,1)}, bf16[112,3584]{1,0:T(8,128)(2,1)}) custom-call(bf16[112,128]{1,0:T(8,128)(2,1)S(1)} %multiply_convert_fusion.3.normed_ref, bf16[16,448,128]{2,1,0:T(8,128)(2,1)S(1)} %all_to_all.27.grads_ref, bf16[112,3584]{1,0:T(8,128)(2,1)S(1)} %get-tuple-element.69.probe_ref, ...), custom_call_target="tpu_custom_call" | custom-call | flops 205520896 | bytes 6422528 | tf_op jit(solution)/shard_map/pallas_call | solution.py:91
  (93 shorter events, 9.2 us)
Async XLA Ops:
  3.1 7.4 %copy-start.8 = (s32[2]{0:T(128)S(1)}, s32[2]{0:T(128)}, u32[]{:S(2)}) copy-start(s32[2]{0:T(128)} %param.19) | copy-start | bytes 28
  3.1 28.9 %all-to-all-start = ((bf16[16,112,384]{2,1,0:T(8,128)(2,1)}), bf16[16,112,384]{2,1,0:T(8,128)(2,1)S(1)}, u32[]{:S(2)}, u32[]{:S(2)}) async-start(bf16[16,112,384]{2,1,0:T(8,128)(2,1)} %shard_map.145), calls=%async_computation | async-start | bytes 2752512 | tf_op jit(solution)/shard_map/all_to_all | solution.py:111
  10.2 5.0 %copy-start.10 = (s32[128]{0:T(128)S(1)}, s32[128]{0:T(128)}, u32[]{:S(2)}) copy-start(s32[128]{0:T(128)} %param.12) | copy-start | bytes 1540
  10.3 5.1 %copy-start.6 = (bf16[112,128]{1,0:T(8,128)(2,1)S(1)}, bf16[112,128]{1,0:T(8,128)(2,1)}, u32[]{:S(2)}) copy-start(bf16[112,128]{1,0:T(8,128)(2,1)} %inputs_ref.1) | copy-start | bytes 86020
  32.0 1.5 copy-start.3
  35.6 23.0 %all-to-all-start.1 = ((bf16[16,112,256]{2,1,0:T(8,128)(2,1)}), bf16[16,112,256]{2,1,0:T(8,128)(2,1)S(1)}, u32[]{:S(2)}, u32[]{:S(2)}) async-start(bf16[16,112,256]{2,1,0:T(8,128)(2,1)} %shard_map.146), calls=%async_computation.1 | async-start | bytes 1835008 | tf_op jit(solution)/shard_map/all_to_all | solution.py:111
  39.2 9.3 %collective-permute-start.2 = (bf16[464,128]{1,0:T(8,128)(2,1)S(1)}, bf16[464,128]{1,0:T(8,128)(2,1)S(1)}, u32[]{:S(2)}, u32[]{:S(2)}) collective-permute-start(bf16[464,128]{1,0:T(8,128)(2,1)S(1)} %fusion.59), channel_id=1, source_target_pairs={{0,12},{4,0},{8,4},{12,8},{1,13},{5,1},{9,5},{13,9},{2,14},{6,2},{... | collective-permute-start | bytes 356360 | tf_op jit(solution)/shard_map/ppermute | solution.py:122
  44.7 13.9 %collective-permute-start.1 = (bf16[464,128]{1,0:T(8,128)(2,1)S(1)}, bf16[464,128]{1,0:T(8,128)(2,1)S(1)}, u32[]{:S(2)}, u32[]{:S(2)}) collective-permute-start(bf16[464,128]{1,0:T(8,128)(2,1)S(1)} %fusion.59), channel_id=1, source_target_pairs={{0,4},{4,8},{8,12},{12,0},{1,5},{5,9},{9,13},{13,1},{2,6},{6,10},{... | collective-permute-start | bytes 356360 | tf_op jit(solution)/shard_map/ppermute | solution.py:122
  44.7 13.9 %collective-permute-start = (bf16[464,128]{1,0:T(8,128)(2,1)S(1)}, bf16[464,128]{1,0:T(8,128)(2,1)S(1)}, u32[]{:S(2)}, u32[]{:S(2)}) collective-permute-start(bf16[464,128]{1,0:T(8,128)(2,1)S(1)} %fusion.59), channel_id=1, source_target_pairs={{0,8},{4,12},{8,0},{12,4},{1,9},{5,13},{9,1},{13,5},{2,10},{6,14},... | collective-permute-start | bytes 356360 | tf_op jit(solution)/shard_map/ppermute | solution.py:122
  87.9 1.1 copy-start.2
  90.2 20.1 %copy-start.7 = (f32[112]{0:T(128)S(1)}, f32[112]{0:T(128)}, u32[]{:S(2)}) copy-start(f32[112]{0:T(128)} %param.11) | copy-start | bytes 1348
  110.2 1.8 %collective-permute-start.3 = (bf16[1792,128]{1,0:T(8,128)(2,1)S(1)}, bf16[1792,128]{1,0:T(8,128)(2,1)S(1)}, u32[]{:S(2)}, u32[]{:S(2)}) collective-permute-start(bf16[1792,128]{1,0:T(8,128)(2,1)S(1)} %bitcast.139), channel_id=1, source_target_pairs={{0,1},{1,0},{2,3},{3,2},{4,5},{5,4},{6,7},{7,6},{8,9},{9,8},{10,11... | collective-permute-start | bytes 1376264 | tf_op jit(solution)/shard_map/ppermute | solution.py:317
  112.1 1.2 copy-start.4
  113.7 9.0 %copy-start.5 = (bf16[112,3584]{1,0:T(8,128)(2,1)S(1)}, bf16[112,3584]{1,0:T(8,128)(2,1)}, u32[]{:S(2)}) copy-start(bf16[112,3584]{1,0:T(8,128)(2,1)} %param.18) | copy-start | bytes 2408452
  113.7 12.3 %collective-permute-start.6 = (bf16[448,128]{1,0:T(8,128)(2,1)S(1)}, bf16[448,128]{1,0:T(8,128)(2,1)S(1)}, u32[]{:S(2)}, u32[]{:S(2)}) collective-permute-start(bf16[448,128]{1,0:T(8,128)(2,1)S(1)} %pad_maximum_fusion.1), channel_id=1, source_target_pairs={{0,12},{4,0},{8,4},{12,8},{1,13},{5,1},{9,5},{13,9},{2,14},{6,2},{... | collective-permute-start | bytes 344072 | tf_op jit(solution)/shard_map/ppermute | solution.py:122
  119.1 14.4 %collective-permute-start.5 = (bf16[448,128]{1,0:T(8,128)(2,1)S(1)}, bf16[448,128]{1,0:T(8,128)(2,1)S(1)}, u32[]{:S(2)}, u32[]{:S(2)}) collective-permute-start(bf16[448,128]{1,0:T(8,128)(2,1)S(1)} %pad_maximum_fusion.1), channel_id=1, source_target_pairs={{0,4},{4,8},{8,12},{12,0},{1,5},{5,9},{9,13},{13,1},{2,6},{6,10},{... | collective-permute-start | bytes 344072 | tf_op jit(solution)/shard_map/ppermute | solution.py:122
  119.1 14.4 %collective-permute-start.4 = (bf16[448,128]{1,0:T(8,128)(2,1)S(1)}, bf16[448,128]{1,0:T(8,128)(2,1)S(1)}, u32[]{:S(2)}, u32[]{:S(2)}) collective-permute-start(bf16[448,128]{1,0:T(8,128)(2,1)S(1)} %pad_maximum_fusion.1), channel_id=1, source_target_pairs={{0,8},{4,12},{8,0},{12,4},{1,9},{5,13},{9,1},{13,5},{2,10},{6,14},... | collective-permute-start | bytes 344072 | tf_op jit(solution)/shard_map/ppermute | solution.py:122
  122.6 1.1 copy-start.9
  134.0 25.2 %copy-start = (bf16[112,3584]{1,0:T(8,128)(2,1)S(1)}, bf16[112,3584]{1,0:T(8,128)(2,1)}, u32[]{:S(2)}) copy-start(bf16[112,3584]{1,0:T(8,128)(2,1)} %mom_ref.1) | copy-start | bytes 2408452
  134.0 25.1 %copy-start.1 = (bf16[112,3584]{1,0:T(8,128)(2,1)S(1)}, bf16[112,3584]{1,0:T(8,128)(2,1)}, u32[]{:S(2)}) copy-start(bf16[112,3584]{1,0:T(8,128)(2,1)} %hess_ref.1) | copy-start | bytes 2408452
